TPU v7x, 256 devices: a whole 4x4x8 slice. The times are simulated.
256 devices in a mesh: dp: 4 (over z_lo, core), ctx: 64 (over x, y, z_hi).
Axes of the slice: x: 4, y: 4, z: 8 (z_hi: 4, z_lo: 2; z = z_hi * 2 + z_lo), core: 2. Of those that a mesh axis runs over, the one named last changes fastest.
Arguments:
- queries: bfloat16 [4, 8192, 1024], P('dp', 'ctx'), may hold values from -12 to 12
- keys: bfloat16 [4, 8192, 1024], P('dp', 'ctx'), may hold values from -4 to 4
- values: bfloat16 [4, 8192, 1024], P('dp', 'ctx'), may hold values from -18 to 18
- out_grad: bfloat16 [4, 8192, 1024], P('dp', 'ctx'), may hold values from -6 to 6
- w_out: bfloat16 [1024, 1024], replicated, may hold values from -0.1875 to 0.1875
Outputs:
- layer_out: bfloat16 [4, 8192, 1024], P('dp', 'ctx')
- query_grad: bfloat16 [4, 8192, 1024], P('dp', 'ctx')
- key_grad: bfloat16 [4, 8192, 1024], P('dp', 'ctx')
- value_grad: bfloat16 [4, 8192, 1024], P('dp', 'ctx')
- weight_grad: float32 [1024, 1024], P('ctx')
All inputs are finite; a program needn't handle non-finite values.
Results may differ from a plain program's by a relative error of at most 0.018.
Values may be sent and summed in bfloat16 or wider, within the bound.
No kernel may reach another device: no remote copies, remote signals or barrier semaphores. Data moves between devices by JAX's collectives and lax.ppermute only.
A program may use at most 64 MiB of HBM per device.

v0:
```python
import math

import jax
import jax.numpy as jnp
from jax import lax
from jax.sharding import PartitionSpec as P

DH = 64
STRIDE = 1024


def passed_along(shard, axis, by):
    length = lax.axis_size(axis)
    pairs = [(i, i + by) for i in range(length) if 0 <= i + by < length]
    return lax.ppermute(shard, axis, pairs)


def attend(q_part, k_part, v_part, g_part, allowed, score_scale):
    f32 = jnp.float32
    scores = jnp.einsum("ntd,nsd->nts", q_part, k_part, preferred_element_type=f32) * score_scale
    masked = jnp.where(allowed, scores, -jnp.inf)
    row_max = jnp.max(masked, axis=-1, keepdims=True)
    weights = jnp.exp(masked - row_max)
    probs_full = weights / jnp.sum(weights, axis=-1, keepdims=True)
    probs_low = probs_full.astype(jnp.bfloat16)
    output = jnp.einsum("nts,nsd->ntd", probs_low, v_part, preferred_element_type=f32).astype(
        jnp.bfloat16
    )
    delta_sum = jnp.sum(g_part.astype(f32) * output.astype(f32), axis=-1, keepdims=True)
    grad_dot = jnp.einsum("ntd,nsd->nts", g_part, v_part, preferred_element_type=f32)
    score_grad = (probs_full * (grad_dot - delta_sum)).astype(jnp.bfloat16)
    q_grad = (
        jnp.einsum("nts,nsd->ntd", score_grad, k_part, preferred_element_type=f32) * score_scale
    ).astype(jnp.bfloat16)
    k_grad = (
        jnp.einsum("nts,ntd->nsd", score_grad, q_part, preferred_element_type=f32) * score_scale
    )
    v_grad = jnp.einsum("nts,ntd->nsd", probs_low, g_part, preferred_element_type=f32)
    return (output, q_grad, k_grad, v_grad)


def on_device(queries, keys, values, out_grad, w_out):
    clip_count, tok_local, model_width = queries.shape
    half_width = model_width // 2
    head_count = half_width // DH
    score_scale = 1.0 / math.sqrt(DH)
    stride_devs = STRIDE // tok_local
    position = lax.axis_index("ctx")
    n_dev = lax.axis_size("ctx")
    grad_flat = out_grad.reshape(clip_count * tok_local, model_width)
    attention_grad = lax.dot_general(
        grad_flat, w_out, (((1,), (1,)), ((), ())), preferred_element_type=jnp.float32
    ).astype(jnp.bfloat16)
    attention_grad = attention_grad.reshape(clip_count, tok_local, model_width)
    stacked = jnp.stack(
        (
            queries[..., half_width:],
            keys[..., half_width:],
            values[..., half_width:],
            attention_grad[..., half_width:],
        )
    )
    stacked = stacked.reshape(4, clip_count, n_dev, tok_local // n_dev, half_width)
    block = lax.all_to_all(stacked, "ctx", split_axis=2, concat_axis=2, tiled=True)
    member_count, clips_here, dev_count, item_count, width_here = block.shape
    blocks = dev_count // stride_devs
    col_count = stride_devs * item_count
    shaped = block.reshape(member_count, clips_here, blocks, col_count, head_count, DH)
    shaped = jnp.transpose(shaped, (0, 1, 3, 4, 2, 5)).reshape(
        member_count, clips_here * col_count * head_count, blocks, DH
    )
    lower = lax.broadcasted_iota(jnp.int32, (blocks, blocks), 0) >= lax.broadcasted_iota(
        jnp.int32, (blocks, blocks), 1
    )
    results = attend(shaped[0], shaped[1], shaped[2], shaped[3], lower, score_scale)
    joined = jnp.stack(
        (results[0], results[1], results[2].astype(jnp.bfloat16), results[3].astype(jnp.bfloat16))
    )
    joined = joined.reshape(member_count, clips_here, col_count, head_count, blocks, DH)
    joined = jnp.transpose(joined, (0, 1, 4, 2, 3, 5)).reshape(
        member_count, clips_here, dev_count, item_count, width_here
    )
    column_out = lax.all_to_all(joined, "ctx", split_axis=2, concat_axis=2, tiled=True)
    column_out = column_out.reshape(4, clip_count, tok_local, half_width)
    kv_pair = jnp.stack((keys[..., :half_width], values[..., :half_width]))
    earlier = []
    for hop_index in range(stride_devs):
        earlier.append(passed_along(kv_pair, "ctx", hop_index + 1))
    context = jnp.concatenate(earlier[::-1] + [kv_pair], axis=2)
    span = (stride_devs + 1) * tok_local
    row_iota = lax.broadcasted_iota(jnp.int32, (tok_local, span), 0)
    col_iota = lax.broadcasted_iota(jnp.int32, (tok_local, span), 1)
    allowed = (
        (col_iota > row_iota)
        & (col_iota <= row_iota + stride_devs * tok_local)
        & (col_iota >= (stride_devs - position) * tok_local)
    )
    row_q = queries[..., :half_width]
    row_g = attention_grad[..., :half_width]

    def one_head(head_index):
        offset = head_index * DH

        def pick(array):
            return lax.dynamic_slice_in_dim(array, offset, DH, axis=array.ndim - 1)

        return attend(
            pick(row_q), pick(context[0]), pick(context[1]), pick(row_g), allowed, score_scale
        )

    results = lax.map(one_head, jnp.arange(head_count, dtype=jnp.int32))
    out_row = jnp.transpose(results[0], (1, 2, 0, 3)).reshape(clip_count, tok_local, half_width)
    dq_row = jnp.transpose(results[1], (1, 2, 0, 3)).reshape(clip_count, tok_local, half_width)
    kv_grad = jnp.stack((results[2], results[3])).reshape(
        2, head_count, clip_count, stride_devs + 1, tok_local, DH
    )
    summed = kv_grad[:, :, :, stride_devs]
    for hop_index in range(stride_devs):
        summed = summed + passed_along(
            kv_grad[:, :, :, stride_devs - hop_index - 1].astype(jnp.bfloat16),
            "ctx",
            -(hop_index + 1),
        ).astype(jnp.float32)
    dk_row = (
        jnp.transpose(summed[0], (1, 2, 0, 3))
        .reshape(clip_count, tok_local, half_width)
        .astype(jnp.bfloat16)
    )
    dv_row = (
        jnp.transpose(summed[1], (1, 2, 0, 3))
        .reshape(clip_count, tok_local, half_width)
        .astype(jnp.bfloat16)
    )
    attention = jnp.concatenate([out_row, column_out[0]], axis=-1)
    query_grad = jnp.concatenate([dq_row, column_out[1]], axis=-1)
    key_grad = jnp.concatenate([dk_row, column_out[2]], axis=-1)
    value_grad = jnp.concatenate([dv_row, column_out[3]], axis=-1)
    attn_flat = attention.reshape(clip_count * tok_local, model_width)
    layer_out = jnp.dot(attn_flat, w_out, preferred_element_type=jnp.float32).astype(jnp.bfloat16)
    layer_out = layer_out.reshape(clip_count, tok_local, model_width)
    grad_scale = 1.0 / math.sqrt(clip_count * lax.axis_size("dp") * tok_local * n_dev)
    row_share = model_width // n_dev
    all_rows = lax.dot_general(
        attn_flat, grad_flat, (((0,), (0,)), ((), ())), preferred_element_type=jnp.float32
    )
    all_rows = lax.psum(all_rows, ("dp", "ctx"))
    own_rows = lax.dynamic_slice_in_dim(all_rows, position * row_share, row_share, 0)
    weight_grad = own_rows * grad_scale
    return (layer_out, query_grad, key_grad, value_grad, weight_grad)


def solution(mesh):
    placed = (
        P("dp", "ctx", None),
        P("dp", "ctx", None),
        P("dp", "ctx", None),
        P("dp", "ctx", None),
        P(),
    )
    return jax.shard_map(
        on_device,
        mesh=mesh,
        in_specs=placed,
        out_specs=(
            P("dp", "ctx", None),
            P("dp", "ctx", None),
            P("dp", "ctx", None),
            P("dp", "ctx", None),
            P("ctx", None),
        ),
        check_vma=False,
    )
```

profile of v0, /device:TPU:1, one launch (start us, length us, event | category | flops | bytes accessed | tf_op | source)
XLA Modules:
  0.0 524.9 jit_solution(6365571866356572649)
XLA Ops:
  9.2 6.3 %collective-permute-start = (bf16[2,1,128,512]{3,2,1,0:T(8,128)(2,1)}, bf16[2,1,128,512]{3,2,1,0:T(8,128)(2,1)}, u32[]{:S(2)}, u32[]{:S(2)}) collective-permute-start(bf16[2,1,128,512]{3,2,1,0:T(8,128)(2,1)} %pad_maximum_fusion.1), channel_id=1, source_target_pairs={{0,8},{1,9},{2,10},{3,11},{4,12},{5,13},{6,14},{7,15},{8,16},{9,17... | collective-permute-start | bytes 786440 | tf_op jit(solution)/shard_map/ppermute | solution.py:15
  15.5 8.7 %collective-permute-start.1 = (bf16[2,1,128,512]{3,2,1,0:T(8,128)(2,1)}, bf16[2,1,128,512]{3,2,1,0:T(8,128)(2,1)}, u32[]{:S(2)}, u32[]{:S(2)}) collective-permute-start(bf16[2,1,128,512]{3,2,1,0:T(8,128)(2,1)} %pad_maximum_fusion.1), channel_id=1, source_target_pairs={{0,7},{1,8},{2,9},{3,10},{4,11},{5,12},{6,13},{7,14},{8,15},{9,16}... | collective-permute-start | bytes 786440 | tf_op jit(solution)/shard_map/ppermute | solution.py:15
  24.3 3.8 collective-permute-start.2
  28.1 5.9 %collective-permute-start.3 = (bf16[2,1,128,512]{3,2,1,0:T(8,128)(2,1)}, bf16[2,1,128,512]{3,2,1,0:T(8,128)(2,1)}, u32[]{:S(2)}, u32[]{:S(2)}) collective-permute-start(bf16[2,1,128,512]{3,2,1,0:T(8,128)(2,1)} %pad_maximum_fusion.1), channel_id=1, source_target_pairs={{0,5},{1,6},{2,7},{3,8},{4,9},{5,10},{6,11},{7,12},{8,13},{9,14},{... | collective-permute-start | bytes 786440 | tf_op jit(solution)/shard_map/ppermute | solution.py:15
  34.0 2.9 collective-permute-start.4
  36.9 1.8 fusion.45
  40.6 6.9 %all-to-all-start = ((bf16[4,1,64,2,512]{4,3,1,0,2:T(2,128)(2,1)}), bf16[4,1,64,2,512]{4,3,1,0,2:T(2,128)(2,1)S(1)}, u32[]{:S(2)}, u32[]{:S(2)}) async-start(bf16[4,1,64,2,512]{4,3,1,0,2:T(2,128)(2,1)} %pad_maximum_fusion), calls=%async_computation | async-start | bytes 1048576 | tf_op jit(solution)/shard_map/all_to_all | solution.py:64
  49.4 5.0 collective-permute-start.5
  54.4 1.7 constant_dynamic-update-slice_fusion.8
  56.1 4.9 collective-permute-start.6
  62.7 4.0 collective-permute-start.7
  71.7 6.1 %collective-permute-done.5 = bf16[2,1,128,512]{3,2,1,0:T(8,128)(2,1)S(1)} collective-permute-done((bf16[2,1,128,512]{3,2,1,0:T(8,128)(2,1)}, bf16[2,1,128,512]{3,2,1,0:T(8,128)(2,1)S(1)}, u32[]{:S(2)}, u32[]{:S(2)}) %collective-permute-start.5) | collective-permute-done | bytes 262176 | tf_op jit(solution)/shard_map/ppermute | solution.py:15
  82.3 2.2 reshape.287
  90.9 1.7 multiply_reduce_fusion
  98.5 2.2 copy.354
  100.7 16.9 %all-to-all-start.1 = ((bf16[4,1,64,2,512]{4,3,0,1,2:T(2,128)(2,1)}), bf16[4,1,64,2,512]{4,3,0,1,2:T(2,128)(2,1)S(1)}, u32[]{:S(2)}, u32[]{:S(2)}) async-start(bf16[4,1,64,2,512]{4,3,0,1,2:T(2,128)(2,1)} %copy.354), calls=%async_computation.1 | async-start | bytes 1048576 | tf_op jit(solution)/shard_map/all_to_all | solution.py:83
  117.9 78.7 %while.17 = (s32[]{:T(128)}, bf16[8,1,128,64]{2,3,1,0:T(8,128)(2,1)S(1)}, bf16[8,1,128,64]{2,3,1,0:T(8,128)(2,1)}, f32[8,1,1152,64]{2,3,1,0:T(8,128)}, f32[8,1,1...) while((s32[]{:T(128)}, ...), condition=%wide.region_4.5_spmd.clone, body=%wide.region_0.4_spmd.clone.sunk | while | flops 116326016 | bytes 10514143 | solution.py:111
  119.2 1.8 fusion.112
  121.7 1.8 fusion.119
  129.0 1.8 fusion.112
  131.5 1.8 fusion.119
  138.9 1.8 fusion.112
  141.4 1.7 fusion.119
  148.7 1.8 fusion.112
  151.2 1.7 fusion.119
  158.5 1.8 fusion.112
  161.0 1.7 fusion.119
  168.4 1.8 fusion.112
  170.8 1.8 fusion.119
  178.2 1.8 fusion.112
  180.7 1.8 fusion.119
  188.0 1.8 fusion.112
  190.5 1.8 fusion.119
  196.6 4.2 stack.61
  200.9 4.3 stack.62
  205.2 2.6 constant_dynamic-update-slice_fusion.10
  209.0 3.1 convert.15
  214.1 2.7 fusion.49
  216.8 11.0 %fusion.63 = (bf16[2,8,1,1,128,64]{4,3,5,1,2,0:T(2,128)(2,1)S(1)}, bf16[2,8,1,1,128,64]{4,3,5,1,2,0:T(2,128)(2,1)S(1)}, bf16[2,8,1,1,128,64]{4,3,5,1,2,0:T(2,128...) fusion(bf16[2,8,1,9,128,64]{4,3,5,1,2,0:T(8,128)(2,1)} %convert.15), kind=kLoop, calls=%fused_computation.114 | loop fusion | bytes 4194304 | tf_op jit(solution)/shard_map/slice | solution.py:120
  236.7 2.7 collective-permute-done.10
  242.1 5.3 %collective-permute-done.12 = bf16[2,8,1,128,64]{3,4,1,0,2:T(8,128)(2,1)S(1)} collective-permute-done((bf16[2,8,1,128,64]{3,4,1,0,2:T(8,128)(2,1)S(1)}, bf16[2,8,1,128,64]{3,4,1,0,2:T(8,128)(2,1)S(1)}, u32[]{:S(2)}, u32[]{:S(2)}) %collective-permute-start.12) | collective-permute-done | bytes 262176 | tf_op jit(solution)/shard_map/ppermute | solution.py:15
  249.4 2.5 slice.142
  251.9 3.5 collective-permute-done.13
  255.4 11.6 %collective-permute-done.14 = bf16[2,8,1,128,64]{3,4,1,0,2:T(8,128)(2,1)} collective-permute-done((bf16[2,8,1,128,64]{3,4,1,0,2:T(8,128)(2,1)}, bf16[2,8,1,128,64]{3,4,1,0,2:T(8,128)(2,1)}, u32[]{:S(2)}, u32[]{:S(2)}) %collective-permute-start.14) | collective-permute-done | bytes 262176 | tf_op jit(solution)/shard_map/ppermute | solution.py:15
  266.9 7.9 %collective-permute-done.8 = bf16[2,8,1,128,64]{3,4,1,0,2:T(8,128)(2,1)} collective-permute-done((bf16[2,8,1,128,64]{3,4,1,0,2:T(8,128)(2,1)}, bf16[2,8,1,128,64]{3,4,1,0,2:T(8,128)(2,1)}, u32[]{:S(2)}, u32[]{:S(2)}) %collective-permute-start.8) | collective-permute-done | bytes 262176 | tf_op jit(solution)/shard_map/ppermute | solution.py:15
  274.8 6.0 %collective-permute-done.9 = bf16[2,8,1,128,64]{3,4,1,0,2:T(8,128)(2,1)} collective-permute-done((bf16[2,8,1,128,64]{3,4,1,0,2:T(8,128)(2,1)S(1)}, bf16[2,8,1,128,64]{3,4,1,0,2:T(8,128)(2,1)}, u32[]{:S(2)}, u32[]{:S(2)}) %collective-permute-start.9) | collective-permute-done | bytes 262176 | tf_op jit(solution)/shard_map/ppermute | solution.py:15
  280.9 1.9 add_convert_fusion
  287.2 229.4 %all-reduce.2.cloned.1.call-done = f32[1024,1024]{1,0:T(8,128)} async-done(((f32[1024,1024]{1,0:T(8,128)}), f32[1024,1024]{1,0:T(8,128)}) %all-reduce.2.cloned.1.call-update) | async-done | bytes 4194320 | tf_op jit(solution)/shard_map/psum | solution.py:146
  (195 shorter events, 96.6 us)
Async XLA Ops:
  7.2 29.8 %copy-start = (bf16[1024,1024]{1,0:T(8,128)(2,1)S(1)}, bf16[1024,1024]{1,0:T(8,128)(2,1)}, u32[]{:S(2)}) copy-start(bf16[1024,1024]{1,0:T(8,128)(2,1)} %param.11) | copy-start | bytes 6291460
  7.2 31.5 %copy-start.6 = (bf16[1,128,1024]{2,1,0:T(8,128)(2,1)S(1)}, bf16[1,128,1024]{2,1,0:T(8,128)(2,1)}, u32[]{:S(2)}) copy-start(bf16[1,128,1024]{2,1,0:T(8,128)(2,1)} %param.7) | copy-start | bytes 786436
  9.2 40.2 %collective-permute-start = (bf16[2,1,128,512]{3,2,1,0:T(8,128)(2,1)}, bf16[2,1,128,512]{3,2,1,0:T(8,128)(2,1)}, u32[]{:S(2)}, u32[]{:S(2)}) collective-permute-start(bf16[2,1,128,512]{3,2,1,0:T(8,128)(2,1)} %pad_maximum_fusion.1), channel_id=1, source_target_pairs={{0,8},{1,9},{2,10},{3,11},{4,12},{5,13},{6,14},{7,15},{8,16},{9,17... | collective-permute-start | bytes 786440 | tf_op jit(solution)/shard_map/ppermute | solution.py:15
  15.5 40.6 %collective-permute-start.1 = (bf16[2,1,128,512]{3,2,1,0:T(8,128)(2,1)}, bf16[2,1,128,512]{3,2,1,0:T(8,128)(2,1)}, u32[]{:S(2)}, u32[]{:S(2)}) collective-permute-start(bf16[2,1,128,512]{3,2,1,0:T(8,128)(2,1)} %pad_maximum_fusion.1), channel_id=1, source_target_pairs={{0,7},{1,8},{2,9},{3,10},{4,11},{5,12},{6,13},{7,14},{8,15},{9,16}... | collective-permute-start | bytes 786440 | tf_op jit(solution)/shard_map/ppermute | solution.py:15
  24.3 38.4 %collective-permute-start.2 = (bf16[2,1,128,512]{3,2,1,0:T(8,128)(2,1)}, bf16[2,1,128,512]{3,2,1,0:T(8,128)(2,1)}, u32[]{:S(2)}, u32[]{:S(2)}) collective-permute-start(bf16[2,1,128,512]{3,2,1,0:T(8,128)(2,1)} %pad_maximum_fusion.1), channel_id=1, source_target_pairs={{0,6},{1,7},{2,8},{3,9},{4,10},{5,11},{6,12},{7,13},{8,14},{9,15},... | collective-permute-start | bytes 786440 | tf_op jit(solution)/shard_map/ppermute | solution.py:15
  28.1 40.3 %collective-permute-start.3 = (bf16[2,1,128,512]{3,2,1,0:T(8,128)(2,1)}, bf16[2,1,128,512]{3,2,1,0:T(8,128)(2,1)}, u32[]{:S(2)}, u32[]{:S(2)}) collective-permute-start(bf16[2,1,128,512]{3,2,1,0:T(8,128)(2,1)} %pad_maximum_fusion.1), channel_id=1, source_target_pairs={{0,5},{1,6},{2,7},{3,8},{4,9},{5,10},{6,11},{7,12},{8,13},{9,14},{... | collective-permute-start | bytes 786440 | tf_op jit(solution)/shard_map/ppermute | solution.py:15
  34.0 36.0 %collective-permute-start.4 = (bf16[2,1,128,512]{3,2,1,0:T(8,128)(2,1)}, bf16[2,1,128,512]{3,2,1,0:T(8,128)(2,1)}, u32[]{:S(2)}, u32[]{:S(2)}) collective-permute-start(bf16[2,1,128,512]{3,2,1,0:T(8,128)(2,1)} %pad_maximum_fusion.1), channel_id=1, source_target_pairs={{0,4},{1,5},{2,6},{3,7},{4,8},{5,9},{6,10},{7,11},{8,12},{9,13},{1... | collective-permute-start | bytes 786440 | tf_op jit(solution)/shard_map/ppermute | solution.py:15
  40.6 40.5 %all-to-all-start = ((bf16[4,1,64,2,512]{4,3,1,0,2:T(2,128)(2,1)}), bf16[4,1,64,2,512]{4,3,1,0,2:T(2,128)(2,1)S(1)}, u32[]{:S(2)}, u32[]{:S(2)}) async-start(bf16[4,1,64,2,512]{4,3,1,0,2:T(2,128)(2,1)} %pad_maximum_fusion), calls=%async_computation | async-start | bytes 1048576 | tf_op jit(solution)/shard_map/all_to_all | solution.py:64
  49.4 28.4 %collective-permute-start.5 = (bf16[2,1,128,512]{3,2,1,0:T(8,128)(2,1)}, bf16[2,1,128,512]{3,2,1,0:T(8,128)(2,1)S(1)}, u32[]{:S(2)}, u32[]{:S(2)}) collective-permute-start(bf16[2,1,128,512]{3,2,1,0:T(8,128)(2,1)} %pad_maximum_fusion.1), channel_id=1, source_target_pairs={{0,3},{1,4},{2,5},{3,6},{4,7},{5,8},{6,9},{7,10},{8,11},{9,12},{10... | collective-permute-start | bytes 786440 | tf_op jit(solution)/shard_map/ppermute | solution.py:15
  56.1 22.4 %collective-permute-start.6 = (bf16[2,1,128,512]{3,2,1,0:T(8,128)(2,1)}, bf16[2,1,128,512]{3,2,1,0:T(8,128)(2,1)S(1)}, u32[]{:S(2)}, u32[]{:S(2)}) collective-permute-start(bf16[2,1,128,512]{3,2,1,0:T(8,128)(2,1)} %pad_maximum_fusion.1), channel_id=1, source_target_pairs={{0,2},{1,3},{2,4},{3,5},{4,6},{5,7},{6,8},{7,9},{8,10},{9,11},{10,... | collective-permute-start | bytes 786440 | tf_op jit(solution)/shard_map/ppermute | solution.py:15
  62.7 17.0 %collective-permute-start.7 = (bf16[2,1,128,512]{3,2,1,0:T(8,128)(2,1)}, bf16[2,1,128,512]{3,2,1,0:T(8,128)(2,1)S(1)}, u32[]{:S(2)}, u32[]{:S(2)}) collective-permute-start(bf16[2,1,128,512]{3,2,1,0:T(8,128)(2,1)} %pad_maximum_fusion.1), channel_id=1, source_target_pairs={{0,1},{1,2},{2,3},{3,4},{4,5},{5,6},{6,7},{7,8},{8,9},{9,10},{10,1... | collective-permute-start | bytes 786440 | tf_op jit(solution)/shard_map/ppermute | solution.py:15
  85.4 3.2 copy-start.5
  87.7 0.6 copy-start.12
  87.7 0.8 copy-start.13
  95.7 1.0 copy-start.4
  97.1 20.8 %copy-start.10 = (bf16[8,1,128,64]{2,3,1,0:T(8,128)(2,1)S(1)}, bf16[8,1,128,64]{2,3,1,0:T(8,128)(2,1)}, u32[]{:S(2)}) copy-start(bf16[8,1,128,64]{2,3,1,0:T(8,128)(2,1)} %custom-call.2) | copy-start | bytes 393220
  97.2 20.8 %copy-start.14 = (pred[1152]{0:T(1024)(128)(4,1)S(1)}, pred[1152]{0:T(1024)(128)(4,1)}, u32[]{:S(2)}) copy-start(pred[1152]{0:T(1024)(128)(4,1)} %iota_compare_fusion.2) | copy-start | bytes 3460
  97.2 20.8 %copy-start.15 = (s32[128]{0:T(128)S(1)}, s32[128]{0:T(128)}, u32[]{:S(2)}) copy-start(s32[128]{0:T(128)} %iota_add_fusion) | copy-start | bytes 1540
  100.7 112.9 %all-to-all-start.1 = ((bf16[4,1,64,2,512]{4,3,0,1,2:T(2,128)(2,1)}), bf16[4,1,64,2,512]{4,3,0,1,2:T(2,128)(2,1)S(1)}, u32[]{:S(2)}, u32[]{:S(2)}) async-start(bf16[4,1,64,2,512]{4,3,0,1,2:T(2,128)(2,1)} %copy.354), calls=%async_computation.1 | async-start | bytes 1048576 | tf_op jit(solution)/shard_map/all_to_all | solution.py:83
  117.7 398.9 %all-reduce.2.cloned.1.call-start = ((), (), s32[]{:S(2)}) async-start(), calls=%async_computation.2 | async-start | bytes 8388608 | tf_op jit(solution)/shard_map/psum | solution.py:146
  205.2 3.4 copy-start.2
  209.0 4.5 copy-start.1
  209.0 5.1 copy-start.3
  227.8 11.6 %collective-permute-start.10 = (bf16[2,8,1,128,64]{3,4,1,0,2:T(8,128)(2,1)S(1)}, bf16[2,8,1,128,64]{3,4,1,0,2:T(8,128)(2,1)S(1)}, u32[]{:S(2)}, u32[]{:S(2)}) collective-permute-start(bf16[2,8,1,128,64]{3,4,1,0,2:T(8,128)(2,1)S(1)} %bitcast.224), channel_id=1, source_target_pairs={{3,0},{4,1},{5,2},{6,3},{7,4},{8,5},{9,6},{10,7},{11,8},{12,9},{13... | collective-permute-start | bytes 786440 | tf_op jit(solution)/shard_map/ppermute | solution.py:15
  229.2 11.6 %collective-permute-start.11 = (bf16[2,8,1,128,64]{3,4,1,0,2:T(8,128)(2,1)S(1)}, bf16[2,8,1,128,64]{3,4,1,0,2:T(8,128)(2,1)S(1)}, u32[]{:S(2)}, u32[]{:S(2)}) collective-permute-start(bf16[2,8,1,128,64]{3,4,1,0,2:T(8,128)(2,1)S(1)} %bitcast.223), channel_id=1, source_target_pairs={{4,0},{5,1},{6,2},{7,3},{8,4},{9,5},{10,6},{11,7},{12,8},{13,9},{1... | collective-permute-start | bytes 786440 | tf_op jit(solution)/shard_map/ppermute | solution.py:15
  230.5 16.9 %collective-permute-start.12 = (bf16[2,8,1,128,64]{3,4,1,0,2:T(8,128)(2,1)S(1)}, bf16[2,8,1,128,64]{3,4,1,0,2:T(8,128)(2,1)S(1)}, u32[]{:S(2)}, u32[]{:S(2)}) collective-permute-start(bf16[2,8,1,128,64]{3,4,1,0,2:T(8,128)(2,1)S(1)} %bitcast.222), channel_id=1, source_target_pairs={{5,0},{6,1},{7,2},{8,3},{9,4},{10,5},{11,6},{12,7},{13,8},{14,9},{... | collective-permute-start | bytes 786440 | tf_op jit(solution)/shard_map/ppermute | solution.py:15
  231.8 23.5 %collective-permute-start.13 = (bf16[2,8,1,128,64]{3,4,1,0,2:T(8,128)(2,1)S(1)}, bf16[2,8,1,128,64]{3,4,1,0,2:T(8,128)(2,1)}, u32[]{:S(2)}, u32[]{:S(2)}) collective-permute-start(bf16[2,8,1,128,64]{3,4,1,0,2:T(8,128)(2,1)S(1)} %bitcast.220), channel_id=1, source_target_pairs={{6,0},{7,1},{8,2},{9,3},{10,4},{11,5},{12,6},{13,7},{14,8},{15,9},... | collective-permute-start | bytes 786440 | tf_op jit(solution)/shard_map/ppermute | solution.py:15
  233.9 33.0 %collective-permute-start.14 = (bf16[2,8,1,128,64]{3,4,1,0,2:T(8,128)(2,1)}, bf16[2,8,1,128,64]{3,4,1,0,2:T(8,128)(2,1)}, u32[]{:S(2)}, u32[]{:S(2)}) collective-permute-start(bf16[2,8,1,128,64]{3,4,1,0,2:T(8,128)(2,1)} %bitcast.163), channel_id=1, source_target_pairs={{7,0},{8,1},{9,2},{10,3},{11,4},{12,5},{13,6},{14,7},{15,8},{16,9}... | collective-permute-start | bytes 786440 | tf_op jit(solution)/shard_map/ppermute | solution.py:15
  239.5 7.9 %copy-start.7 = (bf16[2,8,1,128,64]{3,4,1,0,2:T(8,128)(2,1)}, bf16[2,8,1,128,64]{3,4,1,0,2:T(8,128)(2,1)S(1)}, u32[]{:S(2)}) copy-start(bf16[2,8,1,128,64]{3,4,1,0,2:T(8,128)(2,1)S(1)} %collective-permute-done.10) | copy-start | bytes 786436
  239.5 27.5 %collective-permute-start.15 = (bf16[2,8,1,128,64]{3,4,1,0,2:T(8,128)(2,1)}, bf16[2,8,1,128,64]{3,4,1,0,2:T(8,128)(2,1)}, u32[]{:S(2)}, u32[]{:S(2)}) collective-permute-start(bf16[2,8,1,128,64]{3,4,1,0,2:T(8,128)(2,1)} %bitcast.162), channel_id=1, source_target_pairs={{8,0},{9,1},{10,2},{11,3},{12,4},{13,5},{14,6},{15,7},{16,8},{17,9... | collective-permute-start | bytes 786440 | tf_op jit(solution)/shard_map/ppermute | solution.py:15
  240.8 6.6 %copy-start.8 = (bf16[2,8,1,128,64]{3,4,1,0,2:T(8,128)(2,1)}, bf16[2,8,1,128,64]{3,4,1,0,2:T(8,128)(2,1)S(1)}, u32[]{:S(2)}) copy-start(bf16[2,8,1,128,64]{3,4,1,0,2:T(8,128)(2,1)S(1)} %collective-permute-done.11) | copy-start | bytes 786436
  240.8 34.1 %collective-permute-start.8 = (bf16[2,8,1,128,64]{3,4,1,0,2:T(8,128)(2,1)}, bf16[2,8,1,128,64]{3,4,1,0,2:T(8,128)(2,1)}, u32[]{:S(2)}, u32[]{:S(2)}) collective-permute-start(bf16[2,8,1,128,64]{3,4,1,0,2:T(8,128)(2,1)} %bitcast.169), channel_id=1, source_target_pairs={{1,0},{2,1},{3,2},{4,3},{5,4},{6,5},{7,6},{8,7},{9,8},{10,9},{11,1... | collective-permute-start | bytes 786440 | tf_op jit(solution)/shard_map/ppermute | solution.py:15
  247.4 0.7 copy-start.9
  248.1 32.8 %collective-permute-start.9 = (bf16[2,8,1,128,64]{3,4,1,0,2:T(8,128)(2,1)S(1)}, bf16[2,8,1,128,64]{3,4,1,0,2:T(8,128)(2,1)}, u32[]{:S(2)}, u32[]{:S(2)}) collective-permute-start(bf16[2,8,1,128,64]{3,4,1,0,2:T(8,128)(2,1)S(1)} %bitcast.221), channel_id=1, source_target_pairs={{2,0},{3,1},{4,2},{5,3},{6,4},{7,5},{8,6},{9,7},{10,8},{11,9},{12,... | collective-permute-start | bytes 786440 | tf_op jit(solution)/shard_map/ppermute | solution.py:15
  282.8 2.4 copy-start.11
Sparse Core Ops, SparseCore 0:
  216.9 299.6 all-reduce.1
where the time goes:
time: 529 us; the launch traced here: 525 us
  waiting for transfers between devices  273 us (52%)
  local copies, waits for them, and re-layouts  79.3 us (15%)
  starting transfers between devices  75.9 us (14%)
  matrix products  56 us (11%)
  other arithmetic  20.6 us (4%)
  between operations  14.7 us (3%)
  loops' own time  5.42 us (1%)
    psum x1, waiting for transfers between devices, on_device(): all_rows = lax.psum(all_rows, ('dp', 'ctx'))  229 us
    ppermute x16, starting transfers between devices, passed_along(): return lax.ppermute(shard, axis, pairs)  51.9 us
    ppermute x16, waiting for transfers between devices, passed_along(): return lax.ppermute(shard, axis, pairs)  43.5 us
    unnamed x53, local copies, waits for them, and re-layouts  22.5 us
    all_to_all x1, starting transfers between devices, on_device(): lax.all_to_all(joined, 'ctx', split_axis=2, concat_axis=2, tiled=True)  16.9 us
    dot_general x9, matrix products, attend(): jnp.einsum('nts,ntd->nsd', probs_low, g_part, preferred_element_type=f32)  14.3 us
    slice x8, local copies, waits for them, and re-layouts, one_head(): context[0]  14.2 us
    slice x1, local copies, waits for them, and re-layouts, on_device(): kv_grad[:, :, :, stride_devs - hop_index - 1].astype(jnp.bfloat16)  11 us
  transfers between devices with their start and end apart: 19, of which 9 were waited for; matrix products, arithmetic and copies ran while one was open for 24% of the time, Pallas kernels for 0%

commit v1 on v0

v1 whole, which is shorter than its diff:
```python
import functools
import math

import jax
import jax.numpy as jnp
from jax import lax
from jax.experimental import pallas as pl
from jax.experimental.pallas import tpu as pltpu
from jax.sharding import Mesh
from jax.sharding import PartitionSpec as P

DH = 64
STRIDE = 1024
LANES = 128
BF16 = jnp.bfloat16
F32 = jnp.float32
SCALE = 1.0 / math.sqrt(DH)
SCALE_LOG2 = SCALE / math.log(2.0)
NT = (((1,), (1,)), ((), ()))
NN = (((1,), (0,)), ((), ()))
VMEM = pl.BlockSpec(memory_space=pltpu.VMEM)
SMEM = pl.BlockSpec(memory_space=pltpu.SMEM)


def dot(a, b, dims=NN):
    return lax.dot_general(a, b, dims, preferred_element_type=F32)


def call(kernel, out_shape, args, scratch=(), flops=0, vmem=32 << 20, smem=0):
    moved = sum(a.size * a.dtype.itemsize for a in args)
    outs = out_shape if isinstance(out_shape, tuple) else (out_shape,)
    moved += sum(math.prod(o.shape) * o.dtype.itemsize for o in outs)
    return pl.pallas_call(
        kernel,
        out_shape=out_shape,
        in_specs=[SMEM] * smem + [VMEM] * (len(args) - smem),
        out_specs=jax.tree.map(lambda _: VMEM, out_shape),
        scratch_shapes=list(scratch),
        compiler_params=pltpu.CompilerParams(vmem_limit_bytes=vmem),
        cost_estimate=pl.CostEstimate(flops=flops, bytes_accessed=moved, transcendentals=0),
    )(*args)


def shape(*dims, dtype=BF16):
    return jax.ShapeDtypeStruct(dims, dtype)


def low_half(rows):
    return lax.broadcasted_iota(jnp.int32, (rows, LANES), 1) < DH


def swap(tile):
    return pltpu.roll(tile, DH, 1)


def paired(a, b, low):
    a, b = a.astype(F32), b.astype(F32)
    first = jnp.where(low, a, swap(b))
    second = jnp.where(low, swap(a), b)
    return first.astype(BF16), second.astype(BF16)


def pack_kernel(q_ref, k_ref, v_ref, og_ref, w_ref, row_ref, col_ref):
    tokens, width = q_ref.shape
    heads = width // DH // 2
    part = tokens // col_ref.shape[0]
    low = low_half(tokens)
    grad = dot(og_ref[...], w_ref[...], NT).astype(BF16)
    for tile in range(heads):
        cut = slice(tile * LANES, (tile + 1) * LANES)
        kv = paired(k_ref[:, cut], v_ref[:, cut], low)
        qg = paired(q_ref[:, cut], grad[:, cut], low)
        for half in range(2):
            head = 2 * tile + half
            if head < heads:
                row_ref[head, :tokens] = kv[half]
                row_ref[head, tokens:] = qg[half]
            else:
                lanes = slice((head - heads) * LANES, (head - heads + 1) * LANES)
                for member in range(col_ref.shape[0]):
                    rows = slice(member * part, (member + 1) * part)
                    col_ref[member, :part, lanes] = kv[half][rows]
                    col_ref[member, part:, lanes] = qg[half][rows]


def split_diag(qg, low):
    zero = jnp.zeros_like(qg)
    return jnp.concatenate([jnp.where(low, qg, zero), jnp.where(low, zero, qg)], axis=0)


def col_kernel(in_ref, out_ref):
    blocks, rows, width = in_ref.shape
    part = rows // 2
    tokens = blocks * part
    low = low_half(tokens)
    key = lax.broadcasted_iota(jnp.int32, (tokens, tokens), 0)
    query = lax.broadcasted_iota(jnp.int32, (tokens, tokens), 1)
    allowed = (key <= query) & (((query - key) & (part - 1)) == 0)
    for head in range(width // LANES):
        cut = slice(head * LANES, (head + 1) * LANES)
        kv = in_ref[:, :part, cut].reshape(tokens, LANES)
        qg = in_ref[:, part:, cut].reshape(tokens, LANES)
        diag = split_diag(qg, low)
        both = dot(kv, diag, NT)
        score = jnp.where(allowed, both[:, :tokens] * SCALE_LOG2, -jnp.inf)
        weight = jnp.exp2(score - jnp.max(score, axis=0, keepdims=True))
        prob = weight / jnp.sum(weight, axis=0, keepdims=True)
        grad = both[:, tokens:]
        delta = jnp.sum(prob * grad, axis=0, keepdims=True)
        score_grad = prob * (grad - delta) * SCALE
        pair = jnp.concatenate([score_grad.astype(BF16), prob.astype(BF16)], axis=1)
        kv_grad = dot(pair, diag).astype(BF16)
        kv_t = kv.astype(F32).T.astype(BF16)
        flat = dot(kv_t, pair)
        back = jnp.concatenate([flat[:DH, :tokens], flat[DH:, tokens:]], axis=0)
        back = back.T.astype(BF16)
        out_ref[:, :part, cut] = back.reshape(blocks, part, LANES)
        out_ref[:, part:, cut] = kv_grad.reshape(blocks, part, LANES)


def row_kernel(first_ref, in_ref, prev_ref, out_ref, kv, kv_t, acc, score, grad, pair):
    tiles = in_ref.shape[0]
    size = in_ref.shape[1] // 2
    span = tiles * size
    chunks = tiles + 1
    low = low_half(size)
    bias = jnp.where(first_ref[0] == 0, -jnp.inf, 0.0).astype(F32)
    for tile in range(tiles):
        own = in_ref[tile, :size]
        before = prev_ref[tile]
        kv[span + tile * size : span + (tile + 1) * size] = own
        kv[tile * size : (tile + 1) * size] = before
        kv_t[:, span + tile * size : span + (tile + 1) * size] = own.astype(F32).T.astype(BF16)
        kv_t[:, tile * size : (tile + 1) * size] = before.astype(F32).T.astype(BF16)
    acc[...] = jnp.zeros_like(acc)
    key = lax.broadcasted_iota(jnp.int32, (size, size), 0)
    query = lax.broadcasted_iota(jnp.int32, (size, size), 1)
    for tile in range(tiles):
        base = tile * size
        diag = split_diag(in_ref[tile, size:], low)
        top = None
        for chunk in range(chunks):
            at = slice(base + chunk * size, base + (chunk + 1) * size)
            rows = slice(chunk * size, (chunk + 1) * size)
            both = dot(kv[at], diag, NT)
            now = both[:, :size] * SCALE_LOG2
            if chunk == 0:
                now = jnp.where(key > query, now, -jnp.inf)
            if chunk == chunks - 1:
                now = jnp.where(key <= query, now, -jnp.inf)
            if tile + chunk < tiles:
                now = now + bias
            score[rows] = now
            grad[rows] = both[:, size:]
            best = jnp.max(now, axis=0, keepdims=True)
            top = best if top is None else jnp.maximum(top, best)
        total = jnp.zeros((1, size), F32)
        inner = jnp.zeros((1, size), F32)
        for chunk in range(chunks):
            rows = slice(chunk * size, (chunk + 1) * size)
            weight = jnp.exp2(score[rows] - top)
            score[rows] = weight
            total = total + jnp.sum(weight, axis=0, keepdims=True)
            inner = inner + jnp.sum(weight * grad[rows], axis=0, keepdims=True)
        scaled = 1.0 / total
        delta = inner * scaled
        for chunk in range(chunks):
            rows = slice(chunk * size, (chunk + 1) * size)
            prob = score[rows] * scaled
            pair[rows, :size] = (prob * (grad[rows] - delta) * SCALE).astype(BF16)
            pair[rows, size:] = prob.astype(BF16)
        window = slice(base, base + chunks * size)
        acc[window] += dot(pair[...], diag)
        flat = dot(kv_t[:, window], pair[...])
        back = jnp.concatenate([flat[:DH, :size], flat[DH:, size:]], axis=0)
        out_ref[tile, :size] = back.T.astype(BF16)
    for tile in range(tiles):
        out_ref[tile, size : 2 * size] = acc[span + tile * size : span + (tile + 1) * size].astype(
            BF16
        )
        out_ref[tile, 2 * size :] = acc[tile * size : (tile + 1) * size].astype(BF16)


def unpaired(first, second, low):
    first, second = first.astype(F32), second.astype(F32)
    return jnp.where(low, first, swap(second)), jnp.where(low, swap(first), second)


def attention_kernel(row_ref, col_ref, att_ref, att_t_ref, dq_ref, prev_ref, turned):
    heads = row_ref.shape[0]
    tokens = row_ref.shape[1] // 3
    part = col_ref.shape[1] // 2
    groups, share, _ = att_t_ref.shape
    low = low_half(tokens)

    def one(head):
        if head < heads:
            return row_ref[head, :tokens]
        cut = slice((head - heads) * LANES, (head - heads + 1) * LANES)
        return col_ref[:, :part, cut].reshape(tokens, LANES)

    for tile in range(heads):
        cut = slice(tile * LANES, (tile + 1) * LANES)
        dq, att = unpaired(one(2 * tile), one(2 * tile + 1), low)
        dq_ref[:, cut] = dq.astype(BF16)
        att_ref[:, cut] = att.astype(BF16)
        turned[cut] = att.T
    for group in range(groups):
        att_t_ref[group] = turned[pl.ds(group, share, stride=groups)].astype(BF16)
    for head in range(heads):
        prev_ref[head] = row_ref[head, 2 * tokens :]


def layer_kernel(att_ref, w_ref, out_ref):
    out_ref[...] = dot(att_ref[...], w_ref[...]).astype(BF16)


def kv_grad_kernel(row_ref, col_ref, later_ref, dk_ref, dv_ref):
    heads = row_ref.shape[0]
    tokens = row_ref.shape[1] // 3
    part = col_ref.shape[1] // 2
    low = low_half(tokens)

    def one(head):
        if head < heads:
            own = row_ref[head, tokens : 2 * tokens].astype(F32)
            return own + later_ref[head].astype(F32)
        cut = slice((head - heads) * LANES, (head - heads + 1) * LANES)
        return col_ref[:, part:, cut].reshape(tokens, LANES)

    for tile in range(heads):
        cut = slice(tile * LANES, (tile + 1) * LANES)
        dk, dv = unpaired(one(2 * tile), one(2 * tile + 1), low)
        dk_ref[:, cut] = dk.astype(BF16)
        dv_ref[:, cut] = dv.astype(BF16)


def weight_kernel(me_ref, att_ref, own_ref, *rest):
    out_ref = rest[-1]
    me = me_ref[0]
    total = dot(att_ref[me], own_ref[...])
    for hop, grad_ref in enumerate(rest[:-1]):
        total = total + dot(att_ref[me ^ (hop + 1)], grad_ref[...])
    out_ref[...] = total.astype(BF16)


def swapped(array, axes):
    return lax.all_to_all(array, axes, split_axis=0, concat_axis=0, tiled=True)


def on_device(queries, keys, values, out_grad, w_out):
    _, tokens, width = queries.shape
    row_axes, plane_axes, line_axes = ("yl", "z"), ("b", "yl"), ("d", "z")
    clips, blocks = lax.axis_size("d"), lax.axis_size("b")
    lines = lax.axis_size("z")
    members = lax.axis_size("yl") * lines
    planes = blocks * lax.axis_size("yl")
    positions = blocks * members
    heads = width // DH // 2
    part = tokens // blocks
    q, k, v, og = (a.reshape(tokens, width) for a in (queries, keys, values, out_grad))
    block_index = lax.axis_index("b").astype(jnp.int32).reshape(1)
    clip_index = lax.axis_index("d").astype(jnp.int32).reshape(1)

    project = 2 * tokens * width * width
    row_in, col_in = call(
        pack_kernel,
        (shape(heads, 2 * tokens, LANES), shape(blocks, 2 * part, heads * LANES)),
        (q, k, v, og, w_out),
        flops=project,
    )
    row_got = swapped(row_in, row_axes)
    onward = [(i, i + 1) for i in range(blocks - 1)]
    prev = lax.ppermute(row_got[:, :tokens], "b", onward)
    col_got = swapped(col_in, "b")
    other_grads = [
        lax.ppermute(og, "d", [(i, i ^ hop) for i in range(clips)]) for hop in range(1, clips)
    ]
    col_res = call(
        col_kernel,
        shape(blocks, 2 * part, heads * LANES),
        (col_got,),
        flops=heads * 12 * tokens * tokens * LANES,
    )
    col_back = swapped(col_res, "b")
    span = members * tokens
    window = span + tokens
    row_res = call(
        row_kernel,
        shape(members, 3 * tokens, LANES),
        (block_index, row_got, prev),
        scratch=(
            pltpu.VMEM((2 * span, LANES), BF16),
            pltpu.VMEM((LANES, 2 * span), BF16),
            pltpu.VMEM((2 * span, LANES), F32),
            pltpu.VMEM((window, tokens), F32),
            pltpu.VMEM((window, tokens), F32),
            pltpu.VMEM((window, 2 * tokens), BF16),
        ),
        flops=members * 12 * window * tokens * LANES,
        smem=1,
    )
    row_back = swapped(row_res, row_axes)
    share = width // clips
    att, att_t, query_grad, before = call(
        attention_kernel,
        (
            shape(tokens, width),
            shape(clips, share, tokens),
            shape(tokens, width),
            shape(heads, tokens, LANES),
        ),
        (row_back, col_back),
        scratch=(pltpu.VMEM((width, tokens), F32),),
    )
    att_got = swapped(att_t, "d")
    later = lax.ppermute(before, "b", [(j, i) for i, j in onward])
    layer_out = call(layer_kernel, shape(tokens, width), (att, w_out), flops=project)
    key_grad, value_grad = call(
        kv_grad_kernel,
        (shape(tokens, width), shape(tokens, width)),
        (row_back, col_back, later),
    )
    partial = call(
        weight_kernel,
        shape(share, width),
        (clip_index, att_got, og, *other_grads),
        flops=project,
        smem=1,
    )
    piece = share // planes
    kept = piece // lines
    partial = swapped(partial.reshape(planes, piece, width), plane_axes)
    summed = jnp.sum(partial.astype(F32), axis=0).astype(BF16)
    sent = jnp.broadcast_to(summed.reshape(1, lines, kept, width), (clips, lines, kept, width))
    got = swapped(sent.reshape(clips * lines, kept, width), line_axes)
    total = jnp.sum(got.reshape(clips, lines, kept, width).astype(F32), axis=1)
    total = jnp.transpose(total, (1, 0, 2)).reshape(kept * clips, width)
    weight_grad = total * (1.0 / math.sqrt(clips * tokens * positions))
    whole = (1, tokens, width)
    return (
        layer_out.reshape(whole),
        query_grad.reshape(whole),
        key_grad.reshape(whole),
        value_grad.reshape(whole),
        weight_grad,
    )


def solution(mesh):
    clips, positions = mesh.devices.shape
    members = 8
    lines = 4
    split = (clips, positions // members, members // lines, lines)
    inner = Mesh(mesh.devices.reshape(split), ("d", "b", "yl", "z"))
    ctx = ("b", "yl", "z")
    placed = P("d", ctx, None)
    return jax.shard_map(
        on_device,
        mesh=inner,
        in_specs=(placed, placed, placed, placed, P()),
        out_specs=(placed, placed, placed, placed, P(ctx, None)),
        check_vma=False,
    )
```

time: 529 us -> 159 us (0.30)
  waiting for transfers between devices: 273 us -> 47.6 us
  local copies, waits for them, and re-layouts: 79.3 us -> 10.9 us
  matrix products: 56 us -> 0 us
  blocking collectives: 0 us -> 37 us
  starting transfers between devices: 75.9 us -> 42.9 us
  other arithmetic: 20.6 us -> 1.2 us
  Pallas kernels: 0 us -> 17.6 us
  between operations: 14.7 us -> 0.75 us
  loops' own time: 5.42 us -> 0 us
    psum x1 -> x0, waiting for transfers between devices: 229 us -> none  [on_device(): all_rows = lax.psum(all_rows, ('dp', 'ctx'))]
    dot_general x57 -> x0, matrix products: 56 us -> none  [the longest x9 14.3 us: attend(): jnp.einsum('nts,ntd->nsd', probs_low, g_part, preferred_element_type=f32)]
    ppermute x16 -> x5, starting transfers between devices: 51.9 us -> 8.86 us  [the longest x1 4.89 us: on_device(): prev = lax.ppermute(row_got[:, :tokens], 'b', onward)]
    all_to_all x0 -> x2, blocking collectives: none -> 37 us  [swapped(): return lax.all_to_all(array, axes, split_axis=0, concat_axis=0, tiled=True)]
    slice x19 -> x1, local copies, waits for them, and re-layouts: 30.7 us -> 0.02 us  [on_device(): prev = lax.ppermute(row_got[:, :tokens], 'b', onward)]
    all_to_all x2 -> x5, waiting for transfers between devices: 0.01 us -> 26.5 us  [swapped(): return lax.all_to_all(array, axes, split_axis=0, concat_axis=0, tiled=True)]
    ppermute x16 -> x5, waiting for transfers between devices: 43.5 us -> 21.2 us  [the longest x3 14 us: on_device(): lax.ppermute(og, 'd', [(i, i ^ hop) for i in range(clips)])]
    pallas_call x0 -> x7, Pallas kernels: none -> 17.6 us  [call(): pl.pallas_call(kernel, out_shape=out_shape, in_specs=[SMEM] * smem + [VME...]
  transfers between devices with their start and end apart: 19 -> 10, of which waited for: 9 -> 6; matrix products, arithmetic and copies ran while one was open for 24% -> 1% of each run, Pallas kernels for 0% -> 8%
where the time goes in v1:
time: 159 us; the launch traced here: 158 us
  waiting for transfers between devices  47.6 us (30%)
  starting transfers between devices  42.9 us (27%)
  blocking collectives  37 us (23%)
  Pallas kernels  17.6 us (11%)
  local copies, waits for them, and re-layouts  10.9 us (7%)
    all_to_all x2, blocking collectives, swapped(): return lax.all_to_all(array, axes, split_axis=0, concat_axis=0, tiled=True)  37 us
    all_to_all x5, starting transfers between devices, swapped(): return lax.all_to_all(array, axes, split_axis=0, concat_axis=0, tiled=True)  34.1 us
    all_to_all x5, waiting for transfers between devices, swapped(): return lax.all_to_all(array, axes, split_axis=0, concat_axis=0, tiled=True)  26.5 us
    pallas_call x7, Pallas kernels, call(): pl.pallas_call(kernel, out_shape=out_shape, in_specs=[SMEM] * smem + [VME...  17.6 us
    ppermute x3, waiting for transfers between devices, on_device(): lax.ppermute(og, 'd', [(i, i ^ hop) for i in range(clips)])  14 us
    unnamed x22, local copies, waits for them, and re-layouts  9.46 us
    ppermute x1, waiting for transfers between devices, on_device(): prev = lax.ppermute(row_got[:, :tokens], 'b', onward)  7.16 us
    ppermute x1, starting transfers between devices, on_device(): prev = lax.ppermute(row_got[:, :tokens], 'b', onward)  4.89 us
  transfers between devices with their start and end apart: 10, of which 6 were waited for; matrix products, arithmetic and copies ran while one was open for 1% of the time, Pallas kernels for 8%

profile of v1, /device:TPU:1, one launch (start us, length us, event | category | flops | bytes accessed | tf_op | source)
XLA Modules:
  0.0 158.0 jit_solution(11020473518679692141)
XLA Ops:
  0.6 0.0 copy-start
  0.6 1.6 %copy-done = bf16[1024,1024]{1,0:T(8,128)(2,1)S(1)} copy-done((bf16[1024,1024]{1,0:T(8,128)(2,1)S(1)}, bf16[1024,1024]{1,0:T(8,128)(2,1)}, u32[]{:S(2)}) %copy-start) | copy-done | bytes 2097176
  2.2 0.0 copy-start.3
  2.2 0.9 copy-done.3
  3.2 0.9 copy-done.5
  4.1 0.9 copy-done.6
  5.1 0.9 copy-done.7
  6.0 1.7 %shard_map.92 = (bf16[8,256,128]{2,1,0:T(8,128)(2,1)}, bf16[8,32,1024]{2,1,0:T(8,128)(2,1)S(1)}) custom-call(bf16[128,1024]{1,0:T(8,128)(2,1)S(1)} %bitcast.23, bf16[128,1024]{1,0:T(8,128)(2,1)S(1)} %bitcast.24, bf16[128,1024]{1,0:T(8,128)(2,1)S(1)} %bitcast.25, bf16[128,1024]{1,0:T(8,128)(2,1)S(1)} %bitcast.21, bf16[1024,1024]{1,0:T(8,128)(2,1)S(1)} %copy-done), custom_call_target="tpu_custom_call" | custom-call | flops 268435456 | bytes 4194304 | tf_op jit(solution)/shard_map/pallas_call | solution.py:33
  7.7 16.9 %all_to_all.35.in_ref = bf16[8,32,1024]{2,1,0:T(8,128)(2,1)S(1)} all-to-all(bf16[8,32,1024]{2,1,0:T(8,128)(2,1)S(1)} %get-tuple-element.14), channel_id=1, replica_groups=mesh['d'=4,'b'=8,'yl'=2,'z'=4] {'b'}, dimensions={0} | all-to-all | bytes 1048576 | tf_op jit(solution)/shard_map/all_to_all | solution.py:248
  24.6 8.3 %all-to-all-start = ((bf16[8,256,128]{2,1,0:T(8,128)(2,1)}), bf16[8,256,128]{2,1,0:T(8,128)(2,1)S(1)}, u32[]{:S(2)}, u32[]{:S(2)}) async-start(bf16[8,256,128]{2,1,0:T(8,128)(2,1)} %get-tuple-element.13), calls=%async_computation | async-start | bytes 1048576 | tf_op jit(solution)/shard_map/all_to_all | solution.py:248
  32.9 3.0 %shard_map.94 = bf16[8,32,1024]{2,1,0:T(8,128)(2,1)} custom-call(bf16[8,32,1024]{2,1,0:T(8,128)(2,1)S(1)} %all_to_all.35.in_ref), custom_call_target="tpu_custom_call" | custom-call | flops 201326592 | bytes 1048576 | tf_op jit(solution)/shard_map/pallas_call | solution.py:33
  35.8 10.6 %all-to-all-done.in_ref = bf16[8,256,128]{2,1,0:T(8,128)(2,1)S(1)} async-done(((bf16[8,256,128]{2,1,0:T(8,128)(2,1)}), bf16[8,256,128]{2,1,0:T(8,128)(2,1)S(1)}, u32[]{:S(2)}, u32[]{:S(2)}) %all-to-all-start) | async-done | bytes 524320 | tf_op jit(solution)/shard_map/all_to_all | solution.py:248
  46.4 4.2 %all-to-all-start.3 = ((bf16[8,32,1024]{2,1,0:T(8,128)(2,1)}), bf16[8,32,1024]{2,1,0:T(8,128)(2,1)S(1)}, u32[]{:S(2)}, u32[]{:S(2)}) async-start(bf16[8,32,1024]{2,1,0:T(8,128)(2,1)} %shard_map.94), calls=%async_computation.3 | async-start | bytes 1048576 | tf_op jit(solution)/shard_map/all_to_all | solution.py:248
  50.6 4.9 %collective-permute-start = (bf16[8,128,128]{2,1,0:T(8,128)(2,1)S(1)}, bf16[8,128,128]{2,1,0:T(8,128)(2,1)S(1)}, u32[]{:S(2)}, u32[]{:S(2)}) collective-permute-start(bf16[8,128,128]{2,1,0:T(8,128)(2,1)S(1)} %slice.4), channel_id=1, source_target_pairs={{0,8},{8,16},{16,24},{24,32},{32,40},{40,48},{48,56},{1,9},{9,17},... | collective-permute-start | bytes 786440 | tf_op jit(solution)/shard_map/ppermute | solution.py:274
  55.5 7.2 %collective-permute-done.prev_ref = bf16[8,128,128]{2,1,0:T(8,128)(2,1)S(1)} collective-permute-done((bf16[8,128,128]{2,1,0:T(8,128)(2,1)S(1)}, bf16[8,128,128]{2,1,0:T(8,128)(2,1)S(1)}, u32[]{:S(2)}, u32[]{:S(2)}) %collective-permute-start) | collective-permute-done | bytes 262176 | tf_op jit(solution)/shard_map/ppermute | solution.py:274
  62.6 6.7 %shard_map.93 = bf16[8,384,128]{2,1,0:T(8,128)(2,1)S(1)} custom-call(s32[1]{0:T(128)} %bitcast.first_ref, bf16[8,256,128]{2,1,0:T(8,128)(2,1)S(1)} %all-to-all-done.in_ref, bf16[8,128,128]{2,1,0:T(8,128)(2,1)S(1)} %collective-permute-done.prev_ref), custom_call_target="tpu_custom_call" | custom-call | flops 1811939328 | bytes 1572868 | tf_op jit(solution)/shard_map/pallas_call | solution.py:33
  69.3 0.0 all-to-all-done.3.col_ref
  69.4 20.2 %all_to_all.36.row_ref = bf16[8,384,128]{2,1,0:T(8,128)(2,1)S(1)} all-to-all(bf16[8,384,128]{2,1,0:T(8,128)(2,1)S(1)} %shard_map.93), channel_id=1, replica_groups=mesh['d'=4,'b'=8,'yl'=2,'z'=4] {'yl','z'}, dimensions={0} | all-to-all | bytes 1572864 | tf_op jit(solution)/shard_map/all_to_all | solution.py:248
  89.5 1.2 shard_map.95
  90.8 0.7 copy-done.8
  91.5 0.7 copy-done.10
  92.2 10.5 %all-to-all-start.4 = ((bf16[4,256,128]{2,1,0:T(8,128)(2,1)}), bf16[4,256,128]{2,1,0:T(8,128)(2,1)}, u32[]{:S(2)}, u32[]{:S(2)}) async-start(bf16[4,256,128]{2,1,0:T(8,128)(2,1)} %get-tuple-element.20), calls=%async_computation.4 | async-start | bytes 524288 | tf_op jit(solution)/shard_map/all_to_all | solution.py:248
  102.7 0.0 collective-permute-start.2
  102.7 2.6 %collective-permute-start.3 = (bf16[128,1024]{1,0:T(8,128)(2,1)}, bf16[128,1024]{1,0:T(8,128)(2,1)}, u32[]{:S(2)}, u32[]{:S(2)}) collective-permute-start(bf16[128,1024]{1,0:T(8,128)(2,1)} %bitcast.19), channel_id=1, source_target_pairs={{0,128},{64,192},{128,0},{192,64},{1,129},{65,193},{129,1},{193,65... | collective-permute-start | bytes 786440 | tf_op jit(solution)/shard_map/ppermute | solution.py:277
  105.3 0.1 collective-permute-start.4
  105.3 0.0 collective-permute-done.2.rest_0_
  105.3 7.4 %collective-permute-done.3.rest_1_ = bf16[128,1024]{1,0:T(8,128)(2,1)} collective-permute-done((bf16[128,1024]{1,0:T(8,128)(2,1)}, bf16[128,1024]{1,0:T(8,128)(2,1)}, u32[]{:S(2)}, u32[]{:S(2)}) %collective-permute-start.3) | collective-permute-done | bytes 262176 | tf_op jit(solution)/shard_map/ppermute | solution.py:277
  112.7 6.6 %collective-permute-done.4.rest_2_ = bf16[128,1024]{1,0:T(8,128)(2,1)} collective-permute-done((bf16[128,1024]{1,0:T(8,128)(2,1)}, bf16[128,1024]{1,0:T(8,128)(2,1)}, u32[]{:S(2)}, u32[]{:S(2)}) %collective-permute-start.4) | collective-permute-done | bytes 262176 | tf_op jit(solution)/shard_map/ppermute | solution.py:277
  119.3 0.0 all-to-all-done.4.att_ref
  119.4 0.9 copy-done.4
  120.3 1.9 %shard_map.98 = bf16[256,1024]{1,0:T(8,128)(2,1)S(1)} custom-call(s32[1]{0:T(128)} %bitcast.9.me_ref, bf16[4,256,128]{2,1,0:T(8,128)(2,1)} %all-to-all-done.4.att_ref, bf16[128,1024]{1,0:T(8,128)(2,1)S(1)} %bitcast.22, bf16[128,1024]{1,0:T(8,128)(2,1)} %collective-permute-done.2.rest_0_, bf16[128,1024]{1,0:T(8,128)(2,1)} %collective-permute-done.3.rest_1_, ...), custom_call_target="tpu_custom_call" | custom-call | flops 268435456 | bytes 1835012 | tf_op jit(solution)/shard_map/pallas_call | solution.py:33
  122.2 0.0 copy-start.2
  122.2 0.8 copy-done.2
  123.0 7.0 %all-to-all-start.5 = ((bf16[16,16,1024]{2,1,0:T(8,128)(2,1)}), bf16[16,16,1024]{2,1,0:T(8,128)(2,1)}, u32[]{:S(2)}, u32[]{:S(2)}) async-start(bf16[16,16,1024]{2,1,0:T(8,128)(2,1)} %bitcast.17), calls=%async_computation.5 | async-start | bytes 1048576 | tf_op jit(solution)/shard_map/all_to_all | solution.py:248
  130.0 1.3 collective-permute-start.1
  131.3 10.7 %all-to-all-done.5 = bf16[16,16,1024]{2,1,0:T(8,128)(2,1)} async-done(((bf16[16,16,1024]{2,1,0:T(8,128)(2,1)}), bf16[16,16,1024]{2,1,0:T(8,128)(2,1)}, u32[]{:S(2)}, u32[]{:S(2)}) %all-to-all-start.5) | async-done | bytes 524320 | tf_op jit(solution)/shard_map/all_to_all | solution.py:248
  142.0 1.1 reduce_sum.21
  143.2 0.7 broadcast_in_dim.8
  143.8 4.1 %all-to-all-start.6 = ((bf16[16,4,1024]{2,1,0:T(4,128)(2,1)}), bf16[16,4,1024]{2,1,0:T(4,128)(2,1)S(1)}, u32[]{:S(2)}, u32[]{:S(2)}) async-start(bf16[16,4,1024]{2,1,0:T(4,128)(2,1)} %bitcast.11), calls=%async_computation.6 | async-start | bytes 262144 | tf_op jit(solution)/shard_map/all_to_all | solution.py:248
  147.9 0.0 copy-done.1
  147.9 0.0 copy-start.9
  147.9 0.9 copy-done.9
  148.9 1.1 shard_map.96
  150.0 0.0 collective-permute-done.1.later_ref
  150.0 2.0 %shard_map.97 = (bf16[128,1024]{1,0:T(8,128)(2,1)}, bf16[128,1024]{1,0:T(8,128)(2,1)}) custom-call(bf16[8,384,128]{2,1,0:T(8,128)(2,1)S(1)} %all_to_all.36.row_ref, bf16[8,32,1024]{2,1,0:T(8,128)(2,1)S(1)} %all-to-all-done.3.col_ref, bf16[8,128,128]{2,1,0:T(8,128)(2,1)} %collective-permute-done.1.later_ref), custom_call_target="tpu_custom_call" | custom-call | bytes 2097152 | tf_op jit(solution)/shard_map/pallas_call | solution.py:33
  152.0 5.2 %all-to-all-done.6 = bf16[16,4,1024]{2,1,0:T(4,128)(2,1)S(1)} async-done(((bf16[16,4,1024]{2,1,0:T(4,128)(2,1)}), bf16[16,4,1024]{2,1,0:T(4,128)(2,1)S(1)}, u32[]{:S(2)}, u32[]{:S(2)}) %all-to-all-start.6) | async-done | bytes 131104 | tf_op jit(solution)/shard_map/all_to_all | solution.py:248
  157.2 0.1 convert_reduce_fusion
  157.3 0.7 mul.15
  (11 shorter events, 0.1 us)
Async XLA Ops:
  0.6 1.6 %copy-start = (bf16[1024,1024]{1,0:T(8,128)(2,1)S(1)}, bf16[1024,1024]{1,0:T(8,128)(2,1)}, u32[]{:S(2)}) copy-start(bf16[1024,1024]{1,0:T(8,128)(2,1)} %w_ref.3) | copy-start | bytes 6291460
  2.2 0.9 copy-start.3
  3.2 0.9 copy-start.5
  4.1 0.9 copy-start.6
  5.1 0.9 copy-start.7
  24.6 21.8 %all-to-all-start = ((bf16[8,256,128]{2,1,0:T(8,128)(2,1)}), bf16[8,256,128]{2,1,0:T(8,128)(2,1)S(1)}, u32[]{:S(2)}, u32[]{:S(2)}) async-start(bf16[8,256,128]{2,1,0:T(8,128)(2,1)} %get-tuple-element.13), calls=%async_computation | async-start | bytes 1048576 | tf_op jit(solution)/shard_map/all_to_all | solution.py:248
  46.4 22.9 %all-to-all-start.3 = ((bf16[8,32,1024]{2,1,0:T(8,128)(2,1)}), bf16[8,32,1024]{2,1,0:T(8,128)(2,1)S(1)}, u32[]{:S(2)}, u32[]{:S(2)}) async-start(bf16[8,32,1024]{2,1,0:T(8,128)(2,1)} %shard_map.94), calls=%async_computation.3 | async-start | bytes 1048576 | tf_op jit(solution)/shard_map/all_to_all | solution.py:248
  50.6 12.1 %collective-permute-start = (bf16[8,128,128]{2,1,0:T(8,128)(2,1)S(1)}, bf16[8,128,128]{2,1,0:T(8,128)(2,1)S(1)}, u32[]{:S(2)}, u32[]{:S(2)}) collective-permute-start(bf16[8,128,128]{2,1,0:T(8,128)(2,1)S(1)} %slice.4), channel_id=1, source_target_pairs={{0,8},{8,16},{16,24},{24,32},{32,40},{40,48},{48,56},{1,9},{9,17},... | collective-permute-start | bytes 786440 | tf_op jit(solution)/shard_map/ppermute | solution.py:274
  90.8 0.7 copy-start.8
  91.5 0.7 copy-start.10
  92.2 27.2 %all-to-all-start.4 = ((bf16[4,256,128]{2,1,0:T(8,128)(2,1)}), bf16[4,256,128]{2,1,0:T(8,128)(2,1)}, u32[]{:S(2)}, u32[]{:S(2)}) async-start(bf16[4,256,128]{2,1,0:T(8,128)(2,1)} %get-tuple-element.20), calls=%async_computation.4 | async-start | bytes 524288 | tf_op jit(solution)/shard_map/all_to_all | solution.py:248
  102.7 45.3 %copy-start.1 = (bf16[1024,1024]{1,0:T(8,128)(2,1)S(1)}, bf16[1024,1024]{1,0:T(8,128)(2,1)}, u32[]{:S(2)}) copy-start(bf16[1024,1024]{1,0:T(8,128)(2,1)} %w_ref.3) | copy-start | bytes 6291460
  102.7 2.7 %collective-permute-start.2 = (bf16[128,1024]{1,0:T(8,128)(2,1)}, bf16[128,1024]{1,0:T(8,128)(2,1)}, u32[]{:S(2)}, u32[]{:S(2)}) collective-permute-start(bf16[128,1024]{1,0:T(8,128)(2,1)} %bitcast.18), channel_id=1, source_target_pairs={{0,64},{64,0},{128,192},{192,128},{1,65},{65,1},{129,193},{193,129... | collective-permute-start | bytes 786440 | tf_op jit(solution)/shard_map/ppermute | solution.py:277
  102.7 10.1 %collective-permute-start.3 = (bf16[128,1024]{1,0:T(8,128)(2,1)}, bf16[128,1024]{1,0:T(8,128)(2,1)}, u32[]{:S(2)}, u32[]{:S(2)}) collective-permute-start(bf16[128,1024]{1,0:T(8,128)(2,1)} %bitcast.19), channel_id=1, source_target_pairs={{0,128},{64,192},{128,0},{192,64},{1,129},{65,193},{129,1},{193,65... | collective-permute-start | bytes 786440 | tf_op jit(solution)/shard_map/ppermute | solution.py:277
  105.3 14.1 %collective-permute-start.4 = (bf16[128,1024]{1,0:T(8,128)(2,1)}, bf16[128,1024]{1,0:T(8,128)(2,1)}, u32[]{:S(2)}, u32[]{:S(2)}) collective-permute-start(bf16[128,1024]{1,0:T(8,128)(2,1)} %bitcast.20), channel_id=1, source_target_pairs={{0,192},{64,128},{128,64},{192,0},{1,193},{65,129},{129,65},{193,1... | collective-permute-start | bytes 786440 | tf_op jit(solution)/shard_map/ppermute | solution.py:277
  119.4 1.0 copy-start.4
  122.2 0.8 copy-start.2
  123.0 19.0 %all-to-all-start.5 = ((bf16[16,16,1024]{2,1,0:T(8,128)(2,1)}), bf16[16,16,1024]{2,1,0:T(8,128)(2,1)}, u32[]{:S(2)}, u32[]{:S(2)}) async-start(bf16[16,16,1024]{2,1,0:T(8,128)(2,1)} %bitcast.17), calls=%async_computation.5 | async-start | bytes 1048576 | tf_op jit(solution)/shard_map/all_to_all | solution.py:248
  130.0 20.0 %collective-permute-start.1 = (bf16[8,128,128]{2,1,0:T(8,128)(2,1)}, bf16[8,128,128]{2,1,0:T(8,128)(2,1)}, u32[]{:S(2)}, u32[]{:S(2)}) collective-permute-start(bf16[8,128,128]{2,1,0:T(8,128)(2,1)} %copy-done.10), channel_id=1, source_target_pairs={{8,0},{16,8},{24,16},{32,24},{40,32},{48,40},{56,48},{9,1},{17,9},... | collective-permute-start | bytes 786440 | tf_op jit(solution)/shard_map/ppermute | solution.py:317
  143.8 13.3 %all-to-all-start.6 = ((bf16[16,4,1024]{2,1,0:T(4,128)(2,1)}), bf16[16,4,1024]{2,1,0:T(4,128)(2,1)S(1)}, u32[]{:S(2)}, u32[]{:S(2)}) async-start(bf16[16,4,1024]{2,1,0:T(4,128)(2,1)} %bitcast.11), calls=%async_computation.6 | async-start | bytes 262144 | tf_op jit(solution)/shard_map/all_to_all | solution.py:248
  147.9 1.0 copy-start.9

commit v2 on v1

--- a/solution.py
+++ b/solution.py
@@ -14,26 +14,28 @@
 LANES = 128
 BF16 = jnp.bfloat16
 F32 = jnp.float32
+ROOM = 60 << 20
 SCALE = 1.0 / math.sqrt(DH)
 SCALE_LOG2 = SCALE / math.log(2.0)
 NT = (((1,), (1,)), ((), ()))
 NN = (((1,), (0,)), ((), ()))
 VMEM = pl.BlockSpec(memory_space=pltpu.VMEM)
 SMEM = pl.BlockSpec(memory_space=pltpu.SMEM)
+HBM = pl.BlockSpec(memory_space=pltpu.HBM)
 
 
 def dot(a, b, dims=NN):
     return lax.dot_general(a, b, dims, preferred_element_type=F32)
 
 
-def call(kernel, out_shape, args, scratch=(), flops=0, vmem=32 << 20, smem=0):
+def call(kernel, out_shape, args, scratch=(), flops=0, vmem=32 << 20, specs=None):
     moved = sum(a.size * a.dtype.itemsize for a in args)
     outs = out_shape if isinstance(out_shape, tuple) else (out_shape,)
     moved += sum(math.prod(o.shape) * o.dtype.itemsize for o in outs)
     return pl.pallas_call(
         kernel,
         out_shape=out_shape,
-        in_specs=[SMEM] * smem + [VMEM] * (len(args) - smem),
+        in_specs=specs or [VMEM] * len(args),
         out_specs=jax.tree.map(lambda _: VMEM, out_shape),
         scratch_shapes=list(scratch),
         compiler_params=pltpu.CompilerParams(vmem_limit_bytes=vmem),
@@ -60,11 +62,21 @@
     return first.astype(BF16), second.astype(BF16)
 
 
-def pack_kernel(q_ref, k_ref, v_ref, og_ref, w_ref, row_ref, col_ref):
+def pack_kernel(flip_ref, q_hbm, k_hbm, v_hbm, og_hbm, w_hbm, row_ref, col_ref, *scratch):
+    *held, sems = scratch
+    copies = [
+        pltpu.make_async_copy(source, target, sems.at[i])
+        for i, (source, target) in enumerate(zip((og_hbm, w_hbm, k_hbm, v_hbm, q_hbm), held))
+    ]
+    for copy in copies:
+        copy.start()
+    og_ref, w_ref, k_ref, v_ref, q_ref = held
     tokens, width = q_ref.shape
     heads = width // DH // 2
     part = tokens // col_ref.shape[0]
     low = low_half(tokens)
+    for copy in copies:
+        copy.wait()
     grad = dot(og_ref[...], w_ref[...], NT).astype(BF16)
     for tile in range(heads):
         cut = slice(tile * LANES, (tile + 1) * LANES)
@@ -73,8 +85,9 @@
         for half in range(2):
             head = 2 * tile + half
             if head < heads:
-                row_ref[head, :tokens] = kv[half]
-                row_ref[head, tokens:] = qg[half]
+                slot = head ^ flip_ref[0]
+                row_ref[slot, :tokens] = kv[half]
+                row_ref[slot, tokens:] = qg[half]
             else:
                 lanes = slice((head - heads) * LANES, (head - heads + 1) * LANES)
                 for member in range(col_ref.shape[0]):
@@ -186,47 +199,53 @@
     return jnp.where(low, first, swap(second)), jnp.where(low, swap(first), second)
 
 
-def attention_kernel(row_ref, col_ref, att_ref, att_t_ref, dq_ref, prev_ref, turned):
+def packed_head(flip_ref, row_ref, col_ref, head, which):
     heads = row_ref.shape[0]
     tokens = row_ref.shape[1] // 3
     part = col_ref.shape[1] // 2
-    groups, share, _ = att_t_ref.shape
+    if head < heads:
+        return row_ref[head ^ flip_ref[0], which * tokens : (which + 1) * tokens]
+    cut = slice((head - heads) * LANES, (head - heads + 1) * LANES)
+    return col_ref[:, which * part : (which + 1) * part, cut].reshape(tokens, LANES)
+
+
+def turn_kernel(flip_ref, me_ref, row_ref, col_ref, *rest):
+    outs, turned = rest[:-1], rest[-1]
+    heads = row_ref.shape[0]
+    groups = len(outs)
+    share, tokens = outs[0].shape
     low = low_half(tokens)
-
-    def one(head):
-        if head < heads:
-            return row_ref[head, :tokens]
-        cut = slice((head - heads) * LANES, (head - heads + 1) * LANES)
-        return col_ref[:, :part, cut].reshape(tokens, LANES)
-
+    for tile in range(heads):
+        first = packed_head(flip_ref, row_ref, col_ref, 2 * tile, 0).astype(F32)
+        second = packed_head(flip_ref, row_ref, col_ref, 2 * tile + 1, 0).astype(F32)
+        att = jnp.where(low, swap(first), second)
+        turned[tile * LANES : (tile + 1) * LANES] = att.T
+    for hop, out_ref in enumerate(outs):
+        out_ref[...] = turned[pl.ds(me_ref[0] ^ hop, share, stride=groups)].astype(BF16)
+
+
+def layer_kernel(flip_ref, row_ref, col_ref, w_ref, out_ref, dq_ref, att):
+    heads = row_ref.shape[0]
+    low = low_half(att.shape[0])
     for tile in range(heads):
         cut = slice(tile * LANES, (tile + 1) * LANES)
-        dq, att = unpaired(one(2 * tile), one(2 * tile + 1), low)
+        first = packed_head(flip_ref, row_ref, col_ref, 2 * tile, 0)
+        second = packed_head(flip_ref, row_ref, col_ref, 2 * tile + 1, 0)
+        dq, out = unpaired(first, second, low)
         dq_ref[:, cut] = dq.astype(BF16)
-        att_ref[:, cut] = att.astype(BF16)
-        turned[cut] = att.T
-    for group in range(groups):
-        att_t_ref[group] = turned[pl.ds(group, share, stride=groups)].astype(BF16)
-    for head in range(heads):
-        prev_ref[head] = row_ref[head, 2 * tokens :]
-
-
-def layer_kernel(att_ref, w_ref, out_ref):
-    out_ref[...] = dot(att_ref[...], w_ref[...]).astype(BF16)
-
-
-def kv_grad_kernel(row_ref, col_ref, later_ref, dk_ref, dv_ref):
+        att[:, cut] = out.astype(BF16)
+    out_ref[...] = dot(att[...], w_ref[...]).astype(BF16)
+
+
+def kv_grad_kernel(lines, flip_ref, row_ref, col_ref, later_ref, dk_ref, dv_ref):
     heads = row_ref.shape[0]
-    tokens = row_ref.shape[1] // 3
-    part = col_ref.shape[1] // 2
-    low = low_half(tokens)
+    low = low_half(dk_ref.shape[0])
 
     def one(head):
+        mine = packed_head(flip_ref, row_ref, col_ref, head, 1)
         if head < heads:
-            own = row_ref[head, tokens : 2 * tokens].astype(F32)
-            return own + later_ref[head].astype(F32)
-        cut = slice((head - heads) * LANES, (head - heads + 1) * LANES)
-        return col_ref[:, part:, cut].reshape(tokens, LANES)
+            return mine.astype(F32) + later_ref[head ^ flip_ref[0] ^ lines].astype(F32)
+        return mine
 
     for tile in range(heads):
         cut = slice(tile * LANES, (tile + 1) * LANES)
@@ -235,13 +254,56 @@
         dv_ref[:, cut] = dv.astype(BF16)
 
 
-def weight_kernel(me_ref, att_ref, own_ref, *rest):
-    out_ref = rest[-1]
-    me = me_ref[0]
-    total = dot(att_ref[me], own_ref[...])
-    for hop, grad_ref in enumerate(rest[:-1]):
-        total = total + dot(att_ref[me ^ (hop + 1)], grad_ref[...])
-    out_ref[...] = total.astype(BF16)
+def weight_kernel(*refs):
+    count = (len(refs) - 2) // 2
+    sources, out_ref, held, sems = refs[:count], refs[count], refs[count + 1 : -1], refs[-1]
+    copies = [
+        pltpu.make_async_copy(source, target, sems.at[i])
+        for i, (source, target) in enumerate(zip(sources, held))
+    ]
+    for copy in copies:
+        copy.start()
+    for copy in copies:
+        copy.wait()
+    half = count // 2
+    total = None
+    for att, grad in zip(held[:half], held[half:]):
+        term = dot(att[...], grad[...])
+        total = term if total is None else total + term
+    out_ref[...] = total.astype(BF16).reshape(out_ref.shape)
+
+
+def plane_sum_kernel(in_ref, out_ref):
+    planes, piece, width = in_ref.shape
+    pieces, rows, lanes = out_ref.shape
+    kept = rows * lanes // width
+    lines = piece // kept
+    total = in_ref[0].astype(F32)
+    for plane in range(1, planes):
+        total = total + in_ref[plane].astype(F32)
+    for line in range(lines):
+        mine = total[line * kept : (line + 1) * kept]
+        cuts = [mine[:, i * lanes : (i + 1) * lanes] for i in range(width // lanes)]
+        packed = jnp.concatenate(cuts, axis=0).astype(BF16)
+        for clip in range(pieces // lines):
+            out_ref[clip * lines + line] = packed
+
+
+def line_sum_kernel(clips, factor, in_ref, out_ref):
+    pieces, rows, lanes = in_ref.shape
+    lines = pieces // clips
+    kept = out_ref.shape[0] // clips
+    for clip in range(clips):
+        total = in_ref[clip * lines].astype(F32)
+        for line in range(1, lines):
+            total = total + in_ref[clip * lines + line].astype(F32)
+        total = total * factor
+        for part in range(rows // kept):
+            cut = slice(part * lanes, (part + 1) * lanes)
+            for row in range(kept):
+                at = part * kept + row
+                to = row * clips + clip
+                out_ref[to : to + 1, cut] = total[at : at + 1]
 
 
 def swapped(array, axes):
@@ -253,29 +315,46 @@
     row_axes, plane_axes, line_axes = ("yl", "z"), ("b", "yl"), ("d", "z")
     clips, blocks = lax.axis_size("d"), lax.axis_size("b")
     lines = lax.axis_size("z")
-    members = lax.axis_size("yl") * lines
-    planes = blocks * lax.axis_size("yl")
+    yl = lax.axis_size("yl")
+    members = yl * lines
+    planes = blocks * yl
     positions = blocks * members
     heads = width // DH // 2
     part = tokens // blocks
     q, k, v, og = (a.reshape(tokens, width) for a in (queries, keys, values, out_grad))
     block_index = lax.axis_index("b").astype(jnp.int32).reshape(1)
     clip_index = lax.axis_index("d").astype(jnp.int32).reshape(1)
+    flip = (block_index & 1) * lines
 
     project = 2 * tokens * width * width
     row_in, col_in = call(
         pack_kernel,
         (shape(heads, 2 * tokens, LANES), shape(blocks, 2 * part, heads * LANES)),
-        (q, k, v, og, w_out),
+        (flip, q, k, v, og, w_out),
+        scratch=(
+            pltpu.VMEM((tokens, width), BF16),
+            pltpu.VMEM(w_out.shape, BF16),
+            pltpu.VMEM((tokens, width), BF16),
+            pltpu.VMEM((tokens, width), BF16),
+            pltpu.VMEM((tokens, width), BF16),
+            pltpu.SemaphoreType.DMA((5,)),
+        ),
         flops=project,
+        vmem=ROOM,
+        specs=[SMEM] + [HBM] * 5,
     )
     row_got = swapped(row_in, row_axes)
-    onward = [(i, i + 1) for i in range(blocks - 1)]
-    prev = lax.ppermute(row_got[:, :tokens], "b", onward)
+    row_got, col_in, og_later = lax.optimization_barrier((row_got, col_in, og))
+    onward = [
+        (i * yl + j, (i + 1) * yl + j ^ 1) for i in range(blocks - 1) for j in range(yl)
+    ]
+    prev = lax.ppermute(row_got[:, :tokens], ("b", "yl"), onward)
+    other_grads = [
+        lax.ppermute(og_later, "d", [(i, i ^ hop) for i in range(clips)])
+        for hop in range(1, clips)
+    ]
     col_got = swapped(col_in, "b")
-    other_grads = [
-        lax.ppermute(og, "d", [(i, i ^ hop) for i in range(clips)]) for hop in range(1, clips)
-    ]
+    col_got, prev = lax.optimization_barrier((col_got, prev))
     col_res = call(
         col_kernel,
         shape(blocks, 2 * part, heads * LANES),
@@ -298,45 +377,66 @@
             pltpu.VMEM((window, 2 * tokens), BF16),
         ),
         flops=members * 12 * window * tokens * LANES,
-        smem=1,
-    )
+        specs=[SMEM, VMEM, VMEM],
+    )
+    row_res, *other_grads = lax.optimization_barrier((row_res, *other_grads))
     row_back = swapped(row_res, row_axes)
     share = width // clips
-    att, att_t, query_grad, before = call(
-        attention_kernel,
-        (
-            shape(tokens, width),
-            shape(clips, share, tokens),
-            shape(tokens, width),
-            shape(heads, tokens, LANES),
-        ),
-        (row_back, col_back),
+    piece = share // planes
+    kept = piece // lines
+    turned = call(
+        turn_kernel,
+        (shape(share, tokens),) * clips,
+        (flip, clip_index, row_back, col_back),
         scratch=(pltpu.VMEM((width, tokens), F32),),
-    )
-    att_got = swapped(att_t, "d")
-    later = lax.ppermute(before, "b", [(j, i) for i, j in onward])
-    layer_out = call(layer_kernel, shape(tokens, width), (att, w_out), flops=project)
+        specs=[SMEM, SMEM, VMEM, VMEM],
+    )
+    att_got = [turned[0]] + [
+        lax.ppermute(turned[hop], "d", [(i, i ^ hop) for i in range(clips)])
+        for hop in range(1, clips)
+    ]
+    later = lax.ppermute(
+        row_back[:, 2 * tokens :], "b", [(i + 1, i) for i in range(blocks - 1)]
+    )
+    layer_out, query_grad = call(
+        layer_kernel,
+        (shape(tokens, width), shape(tokens, width)),
+        (flip, row_back, col_back, w_out),
+        scratch=(pltpu.VMEM((tokens, width), BF16),),
+        flops=project,
+        specs=[SMEM, VMEM, VMEM, VMEM],
+    )
     key_grad, value_grad = call(
-        kv_grad_kernel,
+        functools.partial(kv_grad_kernel, lines),
         (shape(tokens, width), shape(tokens, width)),
-        (row_back, col_back, later),
+        (flip, row_back, col_back, later),
+        specs=[SMEM, VMEM, VMEM, VMEM],
     )
     partial = call(
         weight_kernel,
-        shape(share, width),
-        (clip_index, att_got, og, *other_grads),
+        shape(planes, piece, width),
+        (*att_got, og, *other_grads),
+        scratch=(
+            *[pltpu.VMEM((share, tokens), BF16)] * clips,
+            *[pltpu.VMEM((tokens, width), BF16)] * clips,
+            pltpu.SemaphoreType.DMA((2 * clips,)),
+        ),
         flops=project,
-        smem=1,
-    )
-    piece = share // planes
-    kept = piece // lines
-    partial = swapped(partial.reshape(planes, piece, width), plane_axes)
-    summed = jnp.sum(partial.astype(F32), axis=0).astype(BF16)
-    sent = jnp.broadcast_to(summed.reshape(1, lines, kept, width), (clips, lines, kept, width))
-    got = swapped(sent.reshape(clips * lines, kept, width), line_axes)
-    total = jnp.sum(got.reshape(clips, lines, kept, width).astype(F32), axis=1)
-    total = jnp.transpose(total, (1, 0, 2)).reshape(kept * clips, width)
-    weight_grad = total * (1.0 / math.sqrt(clips * tokens * positions))
+        vmem=ROOM,
+        specs=[HBM] * (2 * clips),
+    )
+    lanes = kept * width // piece
+    summed = call(
+        plane_sum_kernel,
+        shape(clips * lines, piece, lanes),
+        (swapped(partial, plane_axes),),
+    )
+    factor = 1.0 / math.sqrt(clips * tokens * positions)
+    weight_grad = call(
+        functools.partial(line_sum_kernel, clips, factor),
+        shape(kept * clips, width, dtype=F32),
+        (swapped(summed, line_axes),),
+    )
     whole = (1, tokens, width)
     return (
         layer_out.reshape(whole),

time: 159 us -> 148 us (0.931)
  blocking collectives: 37 us -> 24.1 us
  local copies, waits for them, and re-layouts: 10.9 us -> 3.38 us
  Pallas kernels: 17.6 us -> 23.4 us
  starting transfers between devices: 42.9 us -> 48.1 us
    all_to_all x2 -> x1, blocking collectives: 37 us -> 24.1 us  [swapped(): return lax.all_to_all(array, axes, split_axis=0, concat_axis=0, tiled=True)]
    ppermute x5 -> x8, starting transfers between devices: 8.86 us -> 18.9 us  [the longest x3 8.12 us: on_device(): lax.ppermute(turned[hop], 'd', [(i, i ^ hop) for i in range(clips)])]
    unnamed x22 -> x16, local copies, waits for them, and re-layouts: 9.46 us -> 2.65 us
    ppermute x5 -> x8, waiting for transfers between devices: 21.2 us -> 14.4 us  [the longest x1 7.19 us: on_device(): prev = lax.ppermute(row_got[:, :tokens], ('b', 'yl'), onward)]
    all_to_all x5, waiting for transfers between devices: 26.5 us -> 32.8 us  [swapped(): return lax.all_to_all(array, axes, split_axis=0, concat_axis=0, tiled=True)]
    pallas_call x7 -> x9, Pallas kernels: 17.6 us -> 23.4 us  [call(): pl.pallas_call(kernel, out_shape=out_shape, in_specs=specs or [VMEM] * le...]
    all_to_all x5, starting transfers between devices: 34.1 us -> 29.1 us  [swapped(): return lax.all_to_all(array, axes, split_axis=0, concat_axis=0, tiled=True)]
  transfers between devices with their start and end apart: 10 -> 13, of which waited for: 6 -> 7; matrix products, arithmetic and copies ran while one was open for 1% -> 1% of each run, Pallas kernels for 8% -> 9%
where the time goes in v2:
time: 148 us; the launch traced here: 147 us
  starting transfers between devices  48.1 us (32%)
  waiting for transfers between devices  47.2 us (32%)
  blocking collectives  24.1 us (16%)
  Pallas kernels  23.4 us (16%)
  local copies, waits for them, and re-layouts  3.38 us (2%)
    all_to_all x5, waiting for transfers between devices, swapped(): return lax.all_to_all(array, axes, split_axis=0, concat_axis=0, tiled=True)  32.8 us
    all_to_all x5, starting transfers between devices, swapped(): return lax.all_to_all(array, axes, split_axis=0, concat_axis=0, tiled=True)  29.1 us
    all_to_all x1, blocking collectives, swapped(): return lax.all_to_all(array, axes, split_axis=0, concat_axis=0, tiled=True)  24.1 us
    pallas_call x9, Pallas kernels, call(): pl.pallas_call(kernel, out_shape=out_shape, in_specs=specs or [VMEM] * le...  23.4 us
    ppermute x3, starting transfers between devices, on_device(): lax.ppermute(turned[hop], 'd', [(i, i ^ hop) for i in range(clips)])  8.12 us
    ppermute x1, waiting for transfers between devices, on_device(): prev = lax.ppermute(row_got[:, :tokens], ('b', 'yl'), onward)  7.19 us
    ppermute x3, starting transfers between devices, on_device(): lax.ppermute(og_later, 'd', [(i, i ^ hop) for i in range(clips)])  5.52 us
    ppermute x1, starting transfers between devices, on_device(): prev = lax.ppermute(row_got[:, :tokens], ('b', 'yl'), onward)  4.01 us
  transfers between devices with their start and end apart: 13, of which 7 were waited for; matrix products, arithmetic and copies ran while one was open for 1% of the time, Pallas kernels for 9%

profile of v2, /device:TPU:1, one launch (start us, length us, event | category | flops | bytes accessed | tf_op | source)
XLA Modules:
  0.0 146.8 jit_solution(529049215868785473)
XLA Ops:
  0.6 3.6 %shard_map.92 = (bf16[8,256,128]{2,1,0:T(8,128)(2,1)}, bf16[8,32,1024]{2,1,0:T(8,128)(2,1)}) custom-call(s32[1]{0:T(128)S(6)} %mul.3.flip_ref, bf16[128,1024]{1,0:T(8,128)(2,1)} %bitcast.15, bf16[128,1024]{1,0:T(8,128)(2,1)} %bitcast.16, bf16[128,1024]{1,0:T(8,128)(2,1)} %bitcast.17, bf16[128,1024]{1,0:T(8,128)(2,1)} %bitcast.10, bf16[1024,1024]{1,0:T(8,128)(2,1)} %w_ref.1), custom_call_target="tpu_custom_call" | custom-call | flops 268435456 | bytes 4194308 | tf_op jit(solution)/shard_map/pallas_call | solution.py:35
  4.3 24.1 %all_to_all.30.in_ref = bf16[8,256,128]{2,1,0:T(8,128)(2,1)S(1)} all-to-all(bf16[8,256,128]{2,1,0:T(8,128)(2,1)} %get-tuple-element.24), channel_id=1, replica_groups=mesh['d'=4,'b'=8,'yl'=2,'z'=4] {'yl','z'}, dimensions={0} | all-to-all | bytes 1048576 | tf_op jit(solution)/shard_map/all_to_all | solution.py:310
  28.4 0.0 copy-start.2
  28.4 6.6 %all-to-all-start.1 = ((bf16[8,32,1024]{2,1,0:T(8,128)(2,1)}), bf16[8,32,1024]{2,1,0:T(8,128)(2,1)S(1)}, u32[]{:S(2)}, u32[]{:S(2)}) async-start(bf16[8,32,1024]{2,1,0:T(8,128)(2,1)} %get-tuple-element.27), calls=%async_computation.1 | async-start | bytes 1048576 | tf_op jit(solution)/shard_map/all_to_all | solution.py:310
  34.9 4.0 %collective-permute-start = (bf16[8,128,128]{2,1,0:T(8,128)(2,1)S(1)}, bf16[8,128,128]{2,1,0:T(8,128)(2,1)S(1)}, u32[]{:S(2)}, u32[]{:S(2)}) collective-permute-start(bf16[8,128,128]{2,1,0:T(8,128)(2,1)S(1)} %slice.6), channel_id=1, source_target_pairs={{0,12},{4,8},{8,20},{12,16},{16,28},{20,24},{24,36},{28,32},{32,44... | collective-permute-start | bytes 786440 | tf_op jit(solution)/shard_map/ppermute | solution.py:351
  39.0 7.2 %collective-permute-done.prev_ref = bf16[8,128,128]{2,1,0:T(8,128)(2,1)S(1)} collective-permute-done((bf16[8,128,128]{2,1,0:T(8,128)(2,1)S(1)}, bf16[8,128,128]{2,1,0:T(8,128)(2,1)S(1)}, u32[]{:S(2)}, u32[]{:S(2)}) %collective-permute-start) | collective-permute-done | bytes 262176 | tf_op jit(solution)/shard_map/ppermute | solution.py:351
  46.2 0.0 all-to-all-done.1.in_ref
  46.2 3.0 %shard_map.94 = bf16[8,32,1024]{2,1,0:T(8,128)(2,1)} custom-call(bf16[8,32,1024]{2,1,0:T(8,128)(2,1)S(1)} %all-to-all-done.1.in_ref), custom_call_target="tpu_custom_call" | custom-call | flops 201326592 | bytes 1048576 | tf_op jit(solution)/shard_map/pallas_call | solution.py:35
  49.1 6.9 %all-to-all-start.3 = ((bf16[8,32,1024]{2,1,0:T(8,128)(2,1)}), bf16[8,32,1024]{2,1,0:T(8,128)(2,1)S(1)}, u32[]{:S(2)}, u32[]{:S(2)}) async-start(bf16[8,32,1024]{2,1,0:T(8,128)(2,1)} %shard_map.94), calls=%async_computation.3 | async-start | bytes 1048576 | tf_op jit(solution)/shard_map/all_to_all | solution.py:310
  56.1 0.0 copy-done.2
  56.1 2.3 %collective-permute-start.1 = (bf16[128,1024]{1,0:T(8,128)(2,1)S(1)}, bf16[128,1024]{1,0:T(8,128)(2,1)S(1)}, u32[]{:S(2)}, u32[]{:S(2)}) collective-permute-start(bf16[128,1024]{1,0:T(8,128)(2,1)S(1)} %bitcast.12), channel_id=1, source_target_pairs={{0,64},{64,0},{128,192},{192,128},{1,65},{65,1},{129,193},{193,129... | collective-permute-start | bytes 786440 | tf_op jit(solution)/shard_map/ppermute | solution.py:353
  58.4 3.1 %collective-permute-start.2 = (bf16[128,1024]{1,0:T(8,128)(2,1)S(1)}, bf16[128,1024]{1,0:T(8,128)(2,1)S(1)}, u32[]{:S(2)}, u32[]{:S(2)}) collective-permute-start(bf16[128,1024]{1,0:T(8,128)(2,1)S(1)} %bitcast.13), channel_id=1, source_target_pairs={{0,128},{64,192},{128,0},{192,64},{1,129},{65,193},{129,1},{193,65... | collective-permute-start | bytes 786440 | tf_op jit(solution)/shard_map/ppermute | solution.py:353
  61.5 0.1 collective-permute-start.3
  61.6 7.6 %shard_map.93 = bf16[8,384,128]{2,1,0:T(8,128)(2,1)} custom-call(s32[1]{0:T(128)} %bitcast.first_ref, bf16[8,256,128]{2,1,0:T(8,128)(2,1)S(1)} %all_to_all.30.in_ref, bf16[8,128,128]{2,1,0:T(8,128)(2,1)S(1)} %collective-permute-done.prev_ref), custom_call_target="tpu_custom_call" | custom-call | flops 1811939328 | bytes 1572868 | tf_op jit(solution)/shard_map/pallas_call | solution.py:35
  69.2 0.0 collective-permute-done.1.refs_5_
  69.2 0.0 copy-start.3
  69.2 0.0 collective-permute-done.2.refs_6_
  69.2 0.7 copy-done.3
  69.9 0.7 copy-done.4
  70.6 3.2 %collective-permute-done.3.refs_7_ = bf16[128,1024]{1,0:T(8,128)(2,1)} collective-permute-done((bf16[128,1024]{1,0:T(8,128)(2,1)S(1)}, bf16[128,1024]{1,0:T(8,128)(2,1)}, u32[]{:S(2)}, u32[]{:S(2)}) %collective-permute-start.3) | collective-permute-done | bytes 262176 | tf_op jit(solution)/shard_map/ppermute | solution.py:353
  73.8 0.0 all-to-all-done.3.col_ref
  73.8 3.5 %all-to-all-start.2 = ((bf16[8,384,128]{2,1,0:T(8,128)(2,1)}), bf16[8,384,128]{2,1,0:T(8,128)(2,1)S(1)}, u32[]{:S(2)}, u32[]{:S(2)}) async-start(bf16[8,384,128]{2,1,0:T(8,128)(2,1)} %shard_map.93), calls=%async_computation.2 | async-start | bytes 1572864 | tf_op jit(solution)/shard_map/all_to_all | solution.py:310
  77.4 18.0 %all-to-all-done.2.row_ref = bf16[8,384,128]{2,1,0:T(8,128)(2,1)S(1)} async-done(((bf16[8,384,128]{2,1,0:T(8,128)(2,1)}), bf16[8,384,128]{2,1,0:T(8,128)(2,1)S(1)}, u32[]{:S(2)}, u32[]{:S(2)}) %all-to-all-start.2) | async-done | bytes 786464 | tf_op jit(solution)/shard_map/all_to_all | solution.py:310
  95.4 0.4 shard_map.97
  95.8 0.0 copy-start.1
  95.8 0.6 copy-done.1
  96.5 1.4 collective-permute-start.5
  97.8 6.7 %collective-permute-start.6 = (bf16[256,128]{1,0:T(8,128)(2,1)S(1)}, bf16[256,128]{1,0:T(8,128)(2,1)S(1)}, u32[]{:S(2)}, u32[]{:S(2)}) collective-permute-start(bf16[256,128]{1,0:T(8,128)(2,1)S(1)} %get-tuple-element.38), channel_id=1, source_target_pairs={{0,128},{64,192},{128,0},{192,64},{1,129},{65,193},{129,1},{193,65... | collective-permute-start | bytes 196616 | tf_op jit(solution)/shard_map/ppermute | solution.py:395
  104.6 0.0 collective-permute-start.7
  104.6 0.0 collective-permute-done.5.refs_1_
  104.6 2.5 %collective-permute-done.6.refs_2_ = bf16[256,128]{1,0:T(8,128)(2,1)S(1)} collective-permute-done((bf16[256,128]{1,0:T(8,128)(2,1)S(1)}, bf16[256,128]{1,0:T(8,128)(2,1)S(1)}, u32[]{:S(2)}, u32[]{:S(2)}) %collective-permute-start.6) | collective-permute-done | bytes 65568 | tf_op jit(solution)/shard_map/ppermute | solution.py:395
  107.1 1.5 %collective-permute-done.7.refs_3_ = bf16[256,128]{1,0:T(8,128)(2,1)S(1)} collective-permute-done((bf16[256,128]{1,0:T(8,128)(2,1)S(1)}, bf16[256,128]{1,0:T(8,128)(2,1)S(1)}, u32[]{:S(2)}, u32[]{:S(2)}) %collective-permute-start.7) | collective-permute-done | bytes 65568 | tf_op jit(solution)/shard_map/ppermute | solution.py:395
  108.6 0.0 copy-done.5
  108.6 0.0 copy-done.6
  108.6 0.6 copy-done.7
  109.2 3.0 %shard_map.98 = bf16[16,16,1024]{2,1,0:T(8,128)(2,1)} custom-call(bf16[256,128]{1,0:T(8,128)(2,1)} %copy-done.1, bf16[256,128]{1,0:T(8,128)(2,1)} %copy-done.5, bf16[256,128]{1,0:T(8,128)(2,1)} %copy-done.6, bf16[256,128]{1,0:T(8,128)(2,1)} %copy-done.7, bf16[128,1024]{1,0:T(8,128)(2,1)} %bitcast.11, bf16[128,1024]{1,0:T(8,128)(2,1)} %copy-done.3, ...), custom_call_target="tpu_custom_call" | custom-call | flops 268435456 | bytes 1835008 | tf_op jit(solution)/shard_map/pallas_call | solution.py:35
  112.2 7.1 %all-to-all-start.4 = ((bf16[16,16,1024]{2,1,0:T(8,128)(2,1)}), bf16[16,16,1024]{2,1,0:T(8,128)(2,1)}, u32[]{:S(2)}, u32[]{:S(2)}) async-start(bf16[16,16,1024]{2,1,0:T(8,128)(2,1)} %shard_map.98), calls=%async_computation.4 | async-start | bytes 1048576 | tf_op jit(solution)/shard_map/all_to_all | solution.py:310
  119.3 0.7 slice.8
  120.0 1.3 collective-permute-start.4
  121.3 8.8 %all-to-all-done.4.in_ref = bf16[16,16,1024]{2,1,0:T(8,128)(2,1)} async-done(((bf16[16,16,1024]{2,1,0:T(8,128)(2,1)}), bf16[16,16,1024]{2,1,0:T(8,128)(2,1)}, u32[]{:S(2)}, u32[]{:S(2)}) %all-to-all-start.4) | async-done | bytes 524320 | tf_op jit(solution)/shard_map/all_to_all | solution.py:310
  130.1 1.8 %shard_map.99 = bf16[16,16,256]{2,1,0:T(8,128)(2,1)} custom-call(bf16[16,16,1024]{2,1,0:T(8,128)(2,1)} %all-to-all-done.4.in_ref), custom_call_target="tpu_custom_call" | custom-call | bytes 655360 | tf_op jit(solution)/shard_map/pallas_call | solution.py:35
  131.8 5.0 %all-to-all-start.5 = ((bf16[16,16,256]{2,1,0:T(8,128)(2,1)}), bf16[16,16,256]{2,1,0:T(8,128)(2,1)S(1)}, u32[]{:S(2)}, u32[]{:S(2)}) async-start(bf16[16,16,256]{2,1,0:T(8,128)(2,1)} %shard_map.99), calls=%async_computation.5 | async-start | bytes 262144 | tf_op jit(solution)/shard_map/all_to_all | solution.py:310
  136.9 0.0 copy-done
  136.9 1.3 shard_map.95
  138.2 0.0 collective-permute-done.4.later_ref
  138.2 2.0 %shard_map.96 = (bf16[128,1024]{1,0:T(8,128)(2,1)}, bf16[128,1024]{1,0:T(8,128)(2,1)}) custom-call(s32[1]{0:T(128)S(6)} %mul.3.flip_ref, bf16[8,384,128]{2,1,0:T(8,128)(2,1)S(1)} %all-to-all-done.2.row_ref, bf16[8,32,1024]{2,1,0:T(8,128)(2,1)S(1)} %all-to-all-done.3.col_ref, bf16[8,128,128]{2,1,0:T(8,128)(2,1)} %collective-permute-done.4.later_ref), custom_call_target="tpu_custom_call" | custom-call | bytes 2097156 | tf_op jit(solution)/shard_map/pallas_call | solution.py:35
  140.1 6.0 %all-to-all-done.5.in_ref = bf16[16,16,256]{2,1,0:T(8,128)(2,1)S(1)} async-done(((bf16[16,16,256]{2,1,0:T(8,128)(2,1)}), bf16[16,16,256]{2,1,0:T(8,128)(2,1)S(1)}, u32[]{:S(2)}, u32[]{:S(2)}) %all-to-all-start.5) | async-done | bytes 131104 | tf_op jit(solution)/shard_map/all_to_all | solution.py:310
  146.1 0.7 shard_map.100
  (6 shorter events, 0.0 us)
Async XLA Ops:
  28.4 27.7 %copy-start.2 = (bf16[1,128,1024]{2,1,0:T(8,128)(2,1)S(1)}, bf16[1,128,1024]{2,1,0:T(8,128)(2,1)}, u32[]{:S(2)}) copy-start(bf16[1,128,1024]{2,1,0:T(8,128)(2,1)} %param.8) | copy-start | bytes 786436
  28.4 17.8 %all-to-all-start.1 = ((bf16[8,32,1024]{2,1,0:T(8,128)(2,1)}), bf16[8,32,1024]{2,1,0:T(8,128)(2,1)S(1)}, u32[]{:S(2)}, u32[]{:S(2)}) async-start(bf16[8,32,1024]{2,1,0:T(8,128)(2,1)} %get-tuple-element.27), calls=%async_computation.1 | async-start | bytes 1048576 | tf_op jit(solution)/shard_map/all_to_all | solution.py:310
  34.9 11.2 %collective-permute-start = (bf16[8,128,128]{2,1,0:T(8,128)(2,1)S(1)}, bf16[8,128,128]{2,1,0:T(8,128)(2,1)S(1)}, u32[]{:S(2)}, u32[]{:S(2)}) collective-permute-start(bf16[8,128,128]{2,1,0:T(8,128)(2,1)S(1)} %slice.6), channel_id=1, source_target_pairs={{0,12},{4,8},{8,20},{12,16},{16,28},{20,24},{24,36},{28,32},{32,44... | collective-permute-start | bytes 786440 | tf_op jit(solution)/shard_map/ppermute | solution.py:351
  49.1 24.7 %all-to-all-start.3 = ((bf16[8,32,1024]{2,1,0:T(8,128)(2,1)}), bf16[8,32,1024]{2,1,0:T(8,128)(2,1)S(1)}, u32[]{:S(2)}, u32[]{:S(2)}) async-start(bf16[8,32,1024]{2,1,0:T(8,128)(2,1)} %shard_map.94), calls=%async_computation.3 | async-start | bytes 1048576 | tf_op jit(solution)/shard_map/all_to_all | solution.py:310
  56.1 13.1 %collective-permute-start.1 = (bf16[128,1024]{1,0:T(8,128)(2,1)S(1)}, bf16[128,1024]{1,0:T(8,128)(2,1)S(1)}, u32[]{:S(2)}, u32[]{:S(2)}) collective-permute-start(bf16[128,1024]{1,0:T(8,128)(2,1)S(1)} %bitcast.12), channel_id=1, source_target_pairs={{0,64},{64,0},{128,192},{192,128},{1,65},{65,1},{129,193},{193,129... | collective-permute-start | bytes 786440 | tf_op jit(solution)/shard_map/ppermute | solution.py:353
  58.4 10.8 %collective-permute-start.2 = (bf16[128,1024]{1,0:T(8,128)(2,1)S(1)}, bf16[128,1024]{1,0:T(8,128)(2,1)S(1)}, u32[]{:S(2)}, u32[]{:S(2)}) collective-permute-start(bf16[128,1024]{1,0:T(8,128)(2,1)S(1)} %bitcast.13), channel_id=1, source_target_pairs={{0,128},{64,192},{128,0},{192,64},{1,129},{65,193},{129,1},{193,65... | collective-permute-start | bytes 786440 | tf_op jit(solution)/shard_map/ppermute | solution.py:353
  61.5 12.3 %collective-permute-start.3 = (bf16[128,1024]{1,0:T(8,128)(2,1)S(1)}, bf16[128,1024]{1,0:T(8,128)(2,1)}, u32[]{:S(2)}, u32[]{:S(2)}) collective-permute-start(bf16[128,1024]{1,0:T(8,128)(2,1)S(1)} %bitcast.14), channel_id=1, source_target_pairs={{0,192},{64,128},{128,64},{192,0},{1,193},{65,129},{129,65},{193,1... | collective-permute-start | bytes 786440 | tf_op jit(solution)/shard_map/ppermute | solution.py:353
  69.2 0.7 copy-start.3
  69.9 0.7 copy-start.4
  73.8 21.6 %all-to-all-start.2 = ((bf16[8,384,128]{2,1,0:T(8,128)(2,1)}), bf16[8,384,128]{2,1,0:T(8,128)(2,1)S(1)}, u32[]{:S(2)}, u32[]{:S(2)}) async-start(bf16[8,384,128]{2,1,0:T(8,128)(2,1)} %shard_map.93), calls=%async_computation.2 | async-start | bytes 1572864 | tf_op jit(solution)/shard_map/all_to_all | solution.py:310
  95.8 0.6 copy-start.1
  96.5 8.1 %collective-permute-start.5 = (bf16[256,128]{1,0:T(8,128)(2,1)S(1)}, bf16[256,128]{1,0:T(8,128)(2,1)S(1)}, u32[]{:S(2)}, u32[]{:S(2)}) collective-permute-start(bf16[256,128]{1,0:T(8,128)(2,1)S(1)} %get-tuple-element.37), channel_id=1, source_target_pairs={{0,64},{64,0},{128,192},{192,128},{1,65},{65,1},{129,193},{193,129... | collective-permute-start | bytes 196616 | tf_op jit(solution)/shard_map/ppermute | solution.py:395
  97.8 9.2 %collective-permute-start.6 = (bf16[256,128]{1,0:T(8,128)(2,1)S(1)}, bf16[256,128]{1,0:T(8,128)(2,1)S(1)}, u32[]{:S(2)}, u32[]{:S(2)}) collective-permute-start(bf16[256,128]{1,0:T(8,128)(2,1)S(1)} %get-tuple-element.38), channel_id=1, source_target_pairs={{0,128},{64,192},{128,0},{192,64},{1,129},{65,193},{129,1},{193,65... | collective-permute-start | bytes 196616 | tf_op jit(solution)/shard_map/ppermute | solution.py:395
  104.6 4.0 %collective-permute-start.7 = (bf16[256,128]{1,0:T(8,128)(2,1)S(1)}, bf16[256,128]{1,0:T(8,128)(2,1)S(1)}, u32[]{:S(2)}, u32[]{:S(2)}) collective-permute-start(bf16[256,128]{1,0:T(8,128)(2,1)S(1)} %get-tuple-element.39), channel_id=1, source_target_pairs={{0,192},{64,128},{128,64},{192,0},{1,193},{65,129},{129,65},{193,1... | collective-permute-start | bytes 196616 | tf_op jit(solution)/shard_map/ppermute | solution.py:395
  104.6 4.0 %copy-start.5 = (bf16[256,128]{1,0:T(8,128)(2,1)}, bf16[256,128]{1,0:T(8,128)(2,1)S(1)}, u32[]{:S(2)}) copy-start(bf16[256,128]{1,0:T(8,128)(2,1)S(1)} %collective-permute-done.5.refs_1_) | copy-start | bytes 196612
  107.1 1.5 %copy-start.6 = (bf16[256,128]{1,0:T(8,128)(2,1)}, bf16[256,128]{1,0:T(8,128)(2,1)S(1)}, u32[]{:S(2)}) copy-start(bf16[256,128]{1,0:T(8,128)(2,1)S(1)} %collective-permute-done.6.refs_2_) | copy-start | bytes 196612
  108.6 0.6 copy-start.7
  109.2 27.7 %copy-start = (bf16[1024,1024]{1,0:T(8,128)(2,1)S(1)}, bf16[1024,1024]{1,0:T(8,128)(2,1)}, u32[]{:S(2)}) copy-start(bf16[1024,1024]{1,0:T(8,128)(2,1)} %w_ref.1) | copy-start | bytes 6291460
  112.2 17.9 %all-to-all-start.4 = ((bf16[16,16,1024]{2,1,0:T(8,128)(2,1)}), bf16[16,16,1024]{2,1,0:T(8,128)(2,1)}, u32[]{:S(2)}, u32[]{:S(2)}) async-start(bf16[16,16,1024]{2,1,0:T(8,128)(2,1)} %shard_map.98), calls=%async_computation.4 | async-start | bytes 1048576 | tf_op jit(solution)/shard_map/all_to_all | solution.py:310
  120.0 18.1 %collective-permute-start.4 = (bf16[8,128,128]{2,1,0:T(8,128)(2,1)}, bf16[8,128,128]{2,1,0:T(8,128)(2,1)}, u32[]{:S(2)}, u32[]{:S(2)}) collective-permute-start(bf16[8,128,128]{2,1,0:T(8,128)(2,1)} %slice.8), channel_id=1, source_target_pairs={{8,0},{16,8},{24,16},{32,24},{40,32},{48,40},{56,48},{9,1},{17,9},... | collective-permute-start | bytes 786440 | tf_op jit(solution)/shard_map/ppermute | solution.py:398
  131.8 14.3 %all-to-all-start.5 = ((bf16[16,16,256]{2,1,0:T(8,128)(2,1)}), bf16[16,16,256]{2,1,0:T(8,128)(2,1)S(1)}, u32[]{:S(2)}, u32[]{:S(2)}) async-start(bf16[16,16,256]{2,1,0:T(8,128)(2,1)} %shard_map.99), calls=%async_computation.5 | async-start | bytes 262144 | tf_op jit(solution)/shard_map/all_to_all | solution.py:310

commit v3 on v2

--- a/solution.py
+++ b/solution.py
@@ -15,6 +15,7 @@
 BF16 = jnp.bfloat16
 F32 = jnp.float32
 ROOM = 60 << 20
+EARLY = 7
 SCALE = 1.0 / math.sqrt(DH)
 SCALE_LOG2 = SCALE / math.log(2.0)
 NT = (((1,), (1,)), ((), ()))
@@ -28,7 +29,7 @@
     return lax.dot_general(a, b, dims, preferred_element_type=F32)
 
 
-def call(kernel, out_shape, args, scratch=(), flops=0, vmem=32 << 20, specs=None):
+def call(kernel, out_shape, args, scratch=(), flops=0, vmem=24 << 20, specs=None):
     moved = sum(a.size * a.dtype.itemsize for a in args)
     outs = out_shape if isinstance(out_shape, tuple) else (out_shape,)
     moved += sum(math.prod(o.shape) * o.dtype.itemsize for o in outs)
@@ -62,38 +63,72 @@
     return first.astype(BF16), second.astype(BF16)
 
 
-def pack_kernel(flip_ref, q_hbm, k_hbm, v_hbm, og_hbm, w_hbm, row_ref, col_ref, *scratch):
-    *held, sems = scratch
+def fetch(pairs, sems):
     copies = [
         pltpu.make_async_copy(source, target, sems.at[i])
-        for i, (source, target) in enumerate(zip((og_hbm, w_hbm, k_hbm, v_hbm, q_hbm), held))
+        for i, (source, target) in enumerate(pairs)
     ]
     for copy in copies:
         copy.start()
-    og_ref, w_ref, k_ref, v_ref, q_ref = held
-    tokens, width = q_ref.shape
-    heads = width // DH // 2
-    part = tokens // col_ref.shape[0]
-    low = low_half(tokens)
     for copy in copies:
         copy.wait()
+
+
+def pack_row_kernel(flip_ref, q_hbm, k_hbm, v_hbm, og_hbm, w_hbm, row_ref, grad_ref, *scratch):
+    og_ref, w_ref, k_ref, v_ref, q_ref, sems = scratch
+    tokens = og_ref.shape[0]
+    half = k_ref.shape[1]
+    fetch(
+        (
+            (og_hbm, og_ref),
+            (w_hbm, w_ref),
+            (k_hbm.at[:, :half], k_ref),
+            (v_hbm.at[:, :half], v_ref),
+            (q_hbm.at[:, :half], q_ref),
+        ),
+        sems,
+    )
+    low = low_half(tokens)
     grad = dot(og_ref[...], w_ref[...], NT).astype(BF16)
-    for tile in range(heads):
+    grad_ref[...] = grad[:, half:]
+    for tile in range(half // LANES):
         cut = slice(tile * LANES, (tile + 1) * LANES)
         kv = paired(k_ref[:, cut], v_ref[:, cut], low)
         qg = paired(q_ref[:, cut], grad[:, cut], low)
-        for half in range(2):
-            head = 2 * tile + half
-            if head < heads:
-                slot = head ^ flip_ref[0]
-                row_ref[slot, :tokens] = kv[half]
-                row_ref[slot, tokens:] = qg[half]
-            else:
-                lanes = slice((head - heads) * LANES, (head - heads + 1) * LANES)
-                for member in range(col_ref.shape[0]):
-                    rows = slice(member * part, (member + 1) * part)
-                    col_ref[member, :part, lanes] = kv[half][rows]
-                    col_ref[member, part:, lanes] = qg[half][rows]
+        for side in range(2):
+            slot = (2 * tile + side) ^ flip_ref[0]
+            row_ref[slot, :tokens] = kv[side]
+            row_ref[slot, tokens:] = qg[side]
+
+
+def pack_col_kernel(me_ref, q_hbm, k_hbm, v_hbm, grad_hbm, *rest):
+    count = len(rest) - 7
+    outs = rest[:count]
+    k_ref, v_ref, q_ref, grad_ref, kv_all, qg_all, sems = rest[count:]
+    tokens, half = k_ref.shape
+    part = tokens // count
+    fetch(
+        (
+            (k_hbm.at[:, half:], k_ref),
+            (v_hbm.at[:, half:], v_ref),
+            (q_hbm.at[:, half:], q_ref),
+            (grad_hbm, grad_ref),
+        ),
+        sems,
+    )
+    low = low_half(tokens)
+    for tile in range(half // LANES):
+        cut = slice(tile * LANES, (tile + 1) * LANES)
+        kv = paired(k_ref[:, cut], v_ref[:, cut], low)
+        qg = paired(q_ref[:, cut], grad_ref[:, cut], low)
+        for side in range(2):
+            lanes = slice((2 * tile + side) * LANES, (2 * tile + side + 1) * LANES)
+            kv_all[:, lanes] = kv[side]
+            qg_all[:, lanes] = qg[side]
+    for hop, out_ref in enumerate(outs):
+        rows = pl.ds(pl.multiple_of((me_ref[0] ^ hop) * part, part), part)
+        out_ref[:part] = kv_all[rows]
+        out_ref[part:] = qg_all[rows]
 
 
 def split_diag(qg, low):
@@ -101,18 +136,22 @@
     return jnp.concatenate([jnp.where(low, qg, zero), jnp.where(low, zero, qg)], axis=0)
 
 
-def col_kernel(in_ref, out_ref):
-    blocks, rows, width = in_ref.shape
+def col_kernel(me_ref, *rest):
+    count = (len(rest) - 2) // 2
+    sources, outs, held, sems = rest[:count], rest[count : 2 * count], rest[-2], rest[-1]
+    fetch([(source, held.at[i]) for i, source in enumerate(sources)], sems)
+    blocks, rows, width = held.shape
     part = rows // 2
     tokens = blocks * part
     low = low_half(tokens)
     key = lax.broadcasted_iota(jnp.int32, (tokens, tokens), 0)
     query = lax.broadcasted_iota(jnp.int32, (tokens, tokens), 1)
-    allowed = (key <= query) & (((query - key) & (part - 1)) == 0)
+    flip = me_ref[0] * part
+    allowed = ((key ^ flip) <= (query ^ flip)) & (((query ^ key) & (part - 1)) == 0)
     for head in range(width // LANES):
         cut = slice(head * LANES, (head + 1) * LANES)
-        kv = in_ref[:, :part, cut].reshape(tokens, LANES)
-        qg = in_ref[:, part:, cut].reshape(tokens, LANES)
+        kv = held[:, :part, cut].reshape(tokens, LANES)
+        qg = held[:, part:, cut].reshape(tokens, LANES)
         diag = split_diag(qg, low)
         both = dot(kv, diag, NT)
         score = jnp.where(allowed, both[:, :tokens] * SCALE_LOG2, -jnp.inf)
@@ -127,35 +166,38 @@
         flat = dot(kv_t, pair)
         back = jnp.concatenate([flat[:DH, :tokens], flat[DH:, tokens:]], axis=0)
         back = back.T.astype(BF16)
-        out_ref[:, :part, cut] = back.reshape(blocks, part, LANES)
-        out_ref[:, part:, cut] = kv_grad.reshape(blocks, part, LANES)
-
-
-def row_kernel(first_ref, in_ref, prev_ref, out_ref, kv, kv_t, acc, score, grad, pair):
-    tiles = in_ref.shape[0]
-    size = in_ref.shape[1] // 2
+        for slot, out_ref in enumerate(outs):
+            at = slice(slot * part, (slot + 1) * part)
+            out_ref[:part, cut] = back[at]
+            out_ref[part:, cut] = kv_grad[at]
+
+
+def row_kernel(first_ref, in_hbm, prev_hbm, out_ref, kv, qg, kv_t, acc, score, grad, pair, sems):
+    tiles, size, _ = qg.shape
     span = tiles * size
     chunks = tiles + 1
     low = low_half(size)
     bias = jnp.where(first_ref[0] == 0, -jnp.inf, 0.0).astype(F32)
-    for tile in range(tiles):
-        own = in_ref[tile, :size]
-        before = prev_ref[tile]
-        kv[span + tile * size : span + (tile + 1) * size] = own
-        kv[tile * size : (tile + 1) * size] = before
-        kv_t[:, span + tile * size : span + (tile + 1) * size] = own.astype(F32).T.astype(BF16)
-        kv_t[:, tile * size : (tile + 1) * size] = before.astype(F32).T.astype(BF16)
+    fetch(
+        (
+            (in_hbm.at[:, :size], kv.at[tiles:]),
+            (in_hbm.at[:, size:], qg),
+            (prev_hbm, kv.at[:tiles]),
+        ),
+        sems,
+    )
+    for block in range(2 * tiles):
+        kv_t[:, block * size : (block + 1) * size] = kv[block].astype(F32).T.astype(BF16)
     acc[...] = jnp.zeros_like(acc)
     key = lax.broadcasted_iota(jnp.int32, (size, size), 0)
     query = lax.broadcasted_iota(jnp.int32, (size, size), 1)
     for tile in range(tiles):
         base = tile * size
-        diag = split_diag(in_ref[tile, size:], low)
+        diag = split_diag(qg[tile], low)
         top = None
         for chunk in range(chunks):
-            at = slice(base + chunk * size, base + (chunk + 1) * size)
             rows = slice(chunk * size, (chunk + 1) * size)
-            both = dot(kv[at], diag, NT)
+            both = dot(kv[tile + chunk], diag, NT)
             now = both[:, :size] * SCALE_LOG2
             if chunk == 0:
                 now = jnp.where(key > query, now, -jnp.inf)
@@ -199,55 +241,72 @@
     return jnp.where(low, first, swap(second)), jnp.where(low, swap(first), second)
 
 
-def packed_head(flip_ref, row_ref, col_ref, head, which):
-    heads = row_ref.shape[0]
-    tokens = row_ref.shape[1] // 3
-    part = col_ref.shape[1] // 2
+def fetch_packed(block_ref, row_hbm, col_hbms, row, col, sems, which):
+    tokens, part = row.shape[1], col.shape[1]
+    pairs = [(row_hbm.at[:, which * tokens : (which + 1) * tokens], row)]
+    for hop, col_hbm in enumerate(col_hbms):
+        source = col_hbm.at[which * part : (which + 1) * part]
+        pairs.append((source, col.at[block_ref[0] ^ hop]))
+    fetch(pairs, sems)
+
+
+def packed_head(flip_ref, row, col, head):
+    heads, tokens, _ = row.shape
     if head < heads:
-        return row_ref[head ^ flip_ref[0], which * tokens : (which + 1) * tokens]
+        return row[head ^ flip_ref[0]]
     cut = slice((head - heads) * LANES, (head - heads + 1) * LANES)
-    return col_ref[:, which * part : (which + 1) * part, cut].reshape(tokens, LANES)
-
-
-def turn_kernel(flip_ref, me_ref, row_ref, col_ref, *rest):
-    outs, turned = rest[:-1], rest[-1]
-    heads = row_ref.shape[0]
-    groups = len(outs)
+    return col[:, :, cut].reshape(tokens, LANES)
+
+
+def turn_kernel(clips, flip_ref, block_ref, me_ref, row_hbm, *rest):
+    col_hbms, outs = rest[: -clips - 4], rest[-clips - 4 : -4]
+    row, col, turned, sems = rest[-4:]
+    fetch_packed(block_ref, row_hbm, col_hbms, row, col, sems, 0)
     share, tokens = outs[0].shape
     low = low_half(tokens)
-    for tile in range(heads):
-        first = packed_head(flip_ref, row_ref, col_ref, 2 * tile, 0).astype(F32)
-        second = packed_head(flip_ref, row_ref, col_ref, 2 * tile + 1, 0).astype(F32)
+    for tile in range(row.shape[0]):
+        first = packed_head(flip_ref, row, col, 2 * tile).astype(F32)
+        second = packed_head(flip_ref, row, col, 2 * tile + 1).astype(F32)
         att = jnp.where(low, swap(first), second)
         turned[tile * LANES : (tile + 1) * LANES] = att.T
     for hop, out_ref in enumerate(outs):
-        out_ref[...] = turned[pl.ds(me_ref[0] ^ hop, share, stride=groups)].astype(BF16)
-
-
-def layer_kernel(flip_ref, row_ref, col_ref, w_ref, out_ref, dq_ref, att):
-    heads = row_ref.shape[0]
+        out_ref[...] = turned[pl.ds(me_ref[0] ^ hop, share, stride=clips)].astype(BF16)
+
+
+def layer_kernel(flip_ref, block_ref, w_hbm, row_hbm, *rest):
+    col_hbms, out_ref, dq_ref = rest[:-7], rest[-7], rest[-6]
+    row, col, att, w_ref, sems = rest[-5:]
+    copy = pltpu.make_async_copy(w_hbm, w_ref, sems.at[len(col_hbms) + 1])
+    copy.start()
+    fetch_packed(block_ref, row_hbm, col_hbms, row, col, sems, 0)
     low = low_half(att.shape[0])
-    for tile in range(heads):
+    for tile in range(row.shape[0]):
         cut = slice(tile * LANES, (tile + 1) * LANES)
-        first = packed_head(flip_ref, row_ref, col_ref, 2 * tile, 0)
-        second = packed_head(flip_ref, row_ref, col_ref, 2 * tile + 1, 0)
+        first = packed_head(flip_ref, row, col, 2 * tile)
+        second = packed_head(flip_ref, row, col, 2 * tile + 1)
         dq, out = unpaired(first, second, low)
         dq_ref[:, cut] = dq.astype(BF16)
         att[:, cut] = out.astype(BF16)
+    copy.wait()
     out_ref[...] = dot(att[...], w_ref[...]).astype(BF16)
 
 
-def kv_grad_kernel(lines, flip_ref, row_ref, col_ref, later_ref, dk_ref, dv_ref):
-    heads = row_ref.shape[0]
+def kv_grad_kernel(lines, flip_ref, block_ref, later_hbm, row_hbm, *rest):
+    col_hbms, dk_ref, dv_ref = rest[:-6], rest[-6], rest[-5]
+    row, col, later, sems = rest[-4:]
+    copy = pltpu.make_async_copy(later_hbm, later, sems.at[len(col_hbms) + 1])
+    copy.start()
+    fetch_packed(block_ref, row_hbm, col_hbms, row, col, sems, 1)
+    copy.wait()
     low = low_half(dk_ref.shape[0])
 
     def one(head):
-        mine = packed_head(flip_ref, row_ref, col_ref, head, 1)
-        if head < heads:
-            return mine.astype(F32) + later_ref[head ^ flip_ref[0] ^ lines].astype(F32)
+        mine = packed_head(flip_ref, row, col, head)
+        if head < row.shape[0]:
+            return mine.astype(F32) + later[head ^ flip_ref[0] ^ lines].astype(F32)
         return mine
 
-    for tile in range(heads):
+    for tile in range(row.shape[0]):
         cut = slice(tile * LANES, (tile + 1) * LANES)
         dk, dv = unpaired(one(2 * tile), one(2 * tile + 1), low)
         dk_ref[:, cut] = dk.astype(BF16)
@@ -255,22 +314,16 @@
 
 
 def weight_kernel(*refs):
-    count = (len(refs) - 2) // 2
-    sources, out_ref, held, sems = refs[:count], refs[count], refs[count + 1 : -1], refs[-1]
-    copies = [
-        pltpu.make_async_copy(source, target, sems.at[i])
-        for i, (source, target) in enumerate(zip(sources, held))
-    ]
-    for copy in copies:
-        copy.start()
-    for copy in copies:
-        copy.wait()
-    half = count // 2
-    total = None
-    for att, grad in zip(held[:half], held[half:]):
-        term = dot(att[...], grad[...])
-        total = term if total is None else total + term
-    out_ref[...] = total.astype(BF16).reshape(out_ref.shape)
+    count = (len(refs) - 4) // 2
+    out_ref, att, grad, sems = refs[2 * count :]
+    tokens = att.shape[1] // count
+    pairs = []
+    for i in range(count):
+        at = pl.ds(i * tokens, tokens)
+        pairs.append((refs[i], att.at[:, at]))
+        pairs.append((refs[count + i], grad.at[at]))
+    fetch(pairs, sems)
+    out_ref[...] = dot(att[...], grad[...]).astype(BF16).reshape(out_ref.shape)
 
 
 def plane_sum_kernel(in_ref, out_ref):
@@ -327,41 +380,63 @@
     flip = (block_index & 1) * lines
 
     project = 2 * tokens * width * width
-    row_in, col_in = call(
-        pack_kernel,
-        (shape(heads, 2 * tokens, LANES), shape(blocks, 2 * part, heads * LANES)),
+    half = width // 2
+    sems = pltpu.SemaphoreType.DMA
+    row_in, grad_col = call(
+        pack_row_kernel,
+        (shape(heads, 2 * tokens, LANES), shape(tokens, half)),
         (flip, q, k, v, og, w_out),
         scratch=(
             pltpu.VMEM((tokens, width), BF16),
             pltpu.VMEM(w_out.shape, BF16),
-            pltpu.VMEM((tokens, width), BF16),
-            pltpu.VMEM((tokens, width), BF16),
-            pltpu.VMEM((tokens, width), BF16),
-            pltpu.SemaphoreType.DMA((5,)),
+            *[pltpu.VMEM((tokens, half), BF16)] * 3,
+            sems((5,)),
         ),
         flops=project,
         vmem=ROOM,
         specs=[SMEM] + [HBM] * 5,
     )
     row_got = swapped(row_in, row_axes)
-    row_got, col_in, og_later = lax.optimization_barrier((row_got, col_in, og))
-    onward = [
-        (i * yl + j, (i + 1) * yl + j ^ 1) for i in range(blocks - 1) for j in range(yl)
-    ]
+    col_piece = shape(2 * part, heads * LANES)
+    col_in = call(
+        pack_col_kernel,
+        (col_piece,) * blocks,
+        (block_index, q, k, v, grad_col),
+        scratch=(
+            *[pltpu.VMEM((tokens, half), BF16)] * 4,
+            *[pltpu.VMEM((tokens, width), BF16)] * 2,
+            sems((4,)),
+        ),
+        specs=[SMEM] + [HBM] * 4,
+    )
+
+    def to_members(pieces, hops):
+        return [
+            lax.ppermute(pieces[hop], "b", [(i, i ^ hop) for i in range(blocks)]) for hop in hops
+        ]
+
+    first, second = range(1, EARLY + 1), range(EARLY + 1, blocks)
+    col_got = to_members(col_in, first)
+    row_got, og_later, *rest = lax.optimization_barrier(
+        (row_got, og, *col_got, *(col_in[hop] for hop in second))
+    )
+    col_got, col_wait = rest[:EARLY], dict(zip(second, rest[EARLY:]))
+    onward = [(i * yl + j, (i + 1) * yl + j ^ 1) for i in range(blocks - 1) for j in range(yl)]
     prev = lax.ppermute(row_got[:, :tokens], ("b", "yl"), onward)
+    col_got = [col_in[0], *col_got, *to_members(col_wait, second)]
+    col_res = call(
+        col_kernel,
+        (col_piece,) * blocks,
+        (block_index, *col_got),
+        scratch=(pltpu.VMEM((blocks, 2 * part, heads * LANES), BF16), sems((blocks,))),
+        flops=heads * 12 * tokens * tokens * LANES,
+        specs=[SMEM] + [HBM] * blocks,
+    )
     other_grads = [
         lax.ppermute(og_later, "d", [(i, i ^ hop) for i in range(clips)])
         for hop in range(1, clips)
     ]
-    col_got = swapped(col_in, "b")
-    col_got, prev = lax.optimization_barrier((col_got, prev))
-    col_res = call(
-        col_kernel,
-        shape(blocks, 2 * part, heads * LANES),
-        (col_got,),
-        flops=heads * 12 * tokens * tokens * LANES,
-    )
-    col_back = swapped(col_res, "b")
+    prev, col_res = lax.optimization_barrier((prev, col_res))
     span = members * tokens
     window = span + tokens
     row_res = call(
@@ -369,27 +444,31 @@
         shape(members, 3 * tokens, LANES),
         (block_index, row_got, prev),
         scratch=(
-            pltpu.VMEM((2 * span, LANES), BF16),
+            pltpu.VMEM((2 * members, tokens, LANES), BF16),
+            pltpu.VMEM((members, tokens, LANES), BF16),
             pltpu.VMEM((LANES, 2 * span), BF16),
             pltpu.VMEM((2 * span, LANES), F32),
             pltpu.VMEM((window, tokens), F32),
             pltpu.VMEM((window, tokens), F32),
             pltpu.VMEM((window, 2 * tokens), BF16),
+            sems((3,)),
         ),
         flops=members * 12 * window * tokens * LANES,
-        specs=[SMEM, VMEM, VMEM],
-    )
-    row_res, *other_grads = lax.optimization_barrier((row_res, *other_grads))
+        specs=[SMEM, HBM, HBM],
+    )
+    row_res, col_res, other_grads = lax.optimization_barrier((row_res, col_res, other_grads))
     row_back = swapped(row_res, row_axes)
+    col_back = [col_res[0], *to_members(col_res, range(1, blocks))]
     share = width // clips
     piece = share // planes
     kept = piece // lines
+    packed = (pltpu.VMEM((heads, tokens, LANES), BF16), pltpu.VMEM((blocks, part, width), BF16))
     turned = call(
-        turn_kernel,
+        functools.partial(turn_kernel, clips),
         (shape(share, tokens),) * clips,
-        (flip, clip_index, row_back, col_back),
-        scratch=(pltpu.VMEM((width, tokens), F32),),
-        specs=[SMEM, SMEM, VMEM, VMEM],
+        (flip, block_index, clip_index, row_back, *col_back),
+        scratch=(*packed, pltpu.VMEM((width, tokens), F32), sems((blocks + 1,))),
+        specs=[SMEM] * 3 + [HBM] * (blocks + 1),
     )
     att_got = [turned[0]] + [
         lax.ppermute(turned[hop], "d", [(i, i ^ hop) for i in range(clips)])
@@ -401,25 +480,36 @@
     layer_out, query_grad = call(
         layer_kernel,
         (shape(tokens, width), shape(tokens, width)),
-        (flip, row_back, col_back, w_out),
-        scratch=(pltpu.VMEM((tokens, width), BF16),),
+        (flip, block_index, w_out, row_back, *col_back),
+        scratch=(
+            *packed,
+            pltpu.VMEM((tokens, width), BF16),
+            pltpu.VMEM(w_out.shape, BF16),
+            sems((blocks + 2,)),
+        ),
         flops=project,
-        specs=[SMEM, VMEM, VMEM, VMEM],
+        specs=[SMEM] * 2 + [HBM] * (blocks + 2),
     )
     key_grad, value_grad = call(
         functools.partial(kv_grad_kernel, lines),
         (shape(tokens, width), shape(tokens, width)),
-        (flip, row_back, col_back, later),
-        specs=[SMEM, VMEM, VMEM, VMEM],
-    )
+        (flip, block_index, later, row_back, *col_back),
+        scratch=(
+            *packed,
+            pltpu.VMEM((heads, tokens, LANES), BF16),
+            sems((blocks + 2,)),
+        ),
+        specs=[SMEM] * 2 + [HBM] * (blocks + 2),
+    )
+    att_got, layer_out = lax.optimization_barrier((att_got, layer_out))
     partial = call(
         weight_kernel,
         shape(planes, piece, width),
         (*att_got, og, *other_grads),
         scratch=(
-            *[pltpu.VMEM((share, tokens), BF16)] * clips,
-            *[pltpu.VMEM((tokens, width), BF16)] * clips,
-            pltpu.SemaphoreType.DMA((2 * clips,)),
+            pltpu.VMEM((share, clips * tokens), BF16),
+            pltpu.VMEM((clips * tokens, width), BF16),
+            sems((2 * clips,)),
         ),
         flops=project,
         vmem=ROOM,

time: 148 us -> 128 us (0.86)
  blocking collectives: 24.1 us -> 0 us
  starting transfers between devices: 48.1 us -> 68.3 us
  waiting for transfers between devices: 47.2 us -> 33.6 us
    ppermute x0 -> x14, starting transfers between devices: none -> 24.5 us  [to_members(): lax.ppermute(pieces[hop], 'b', [(i, i ^ hop) for i in range(blocks)])]
    all_to_all x1 -> x0, blocking collectives: 24.1 us -> none  [swapped(): return lax.all_to_all(array, axes, split_axis=0, concat_axis=0, tiled=True)]
    all_to_all x5 -> x4, waiting for transfers between devices: 32.8 us -> 19.8 us  [swapped(): return lax.all_to_all(array, axes, split_axis=0, concat_axis=0, tiled=True)]
    ppermute x0 -> x14, waiting for transfers between devices: none -> 11.1 us  [to_members(): lax.ppermute(pieces[hop], 'b', [(i, i ^ hop) for i in range(blocks)])]
    ppermute x1, waiting for transfers between devices: 7.19 us -> 0.01 us  [on_device(): prev = lax.ppermute(row_got[:, :tokens], ('b', 'yl'), onward)]
    ppermute x3, waiting for transfers between devices: 3.21 us -> 0.8 us  [on_device(): lax.ppermute(og_later, 'd', [(i, i ^ hop) for i in range(clips)])]
    ppermute x3, waiting for transfers between devices: 3.98 us -> 1.96 us  [on_device(): lax.ppermute(turned[hop], 'd', [(i, i ^ hop) for i in range(clips)])]
    all_to_all x5 -> x4, starting transfers between devices: 29.1 us -> 27.2 us  [swapped(): return lax.all_to_all(array, axes, split_axis=0, concat_axis=0, tiled=True)]
  transfers between devices with their start and end apart: 13 -> 26, of which waited for: 7 -> 11; matrix products, arithmetic and copies ran while one was open for 1% -> 0% of each run, Pallas kernels for 9% -> 12%
where the time goes in v3:
time: 128 us
  starting transfers between devices  68.3 us (53%)
  waiting for transfers between devices  33.6 us (26%)
  Pallas kernels  22.6 us (18%)
  local copies, waits for them, and re-layouts  2.48 us (2%)
    all_to_all x4, starting transfers between devices, swapped(): return lax.all_to_all(array, axes, split_axis=0, concat_axis=0, tiled=True)  27.2 us
    ppermute x14, starting transfers between devices, to_members(): lax.ppermute(pieces[hop], 'b', [(i, i ^ hop) for i in range(blocks)])  24.5 us
    pallas_call x10, Pallas kernels, call(): pl.pallas_call(kernel, out_shape=out_shape, in_specs=specs or [VMEM] * le...  22.6 us
    all_to_all x4, waiting for transfers between devices, swapped(): return lax.all_to_all(array, axes, split_axis=0, concat_axis=0, tiled=True)  19.8 us
    ppermute x14, waiting for transfers between devices, to_members(): lax.ppermute(pieces[hop], 'b', [(i, i ^ hop) for i in range(blocks)])  11.1 us
    ppermute x3, starting transfers between devices, on_device(): lax.ppermute(turned[hop], 'd', [(i, i ^ hop) for i in range(clips)])  6.41 us
    ppermute x3, starting transfers between devices, on_device(): lax.ppermute(og_later, 'd', [(i, i ^ hop) for i in range(clips)])  4.66 us
    ppermute x1, starting transfers between devices, on_device(): prev = lax.ppermute(row_got[:, :tokens], ('b', 'yl'), onward)  4.27 us
  transfers between devices with their start and end apart: 26, of which 11 were waited for; matrix products, arithmetic and copies ran while one was open for 0% of the time, Pallas kernels for 12%

profile of v3, /device:TPU:1, one launch (start us, length us, event | category | flops | bytes accessed | tf_op | source)
XLA Modules:
  0.0 127.9 jit_solution(3476400233199426335)
XLA Ops:
  0.7 3.3 %shard_map.92 = (bf16[8,256,128]{2,1,0:T(8,128)(2,1)}, bf16[128,512]{1,0:T(8,128)(2,1)}) custom-call(s32[1]{0:T(128)S(6)} %mul.3.flip_ref, bf16[128,1024]{1,0:T(8,128)(2,1)} %bitcast.10, bf16[128,1024]{1,0:T(8,128)(2,1)} %bitcast.12, bf16[128,1024]{1,0:T(8,128)(2,1)} %bitcast.14, bf16[128,1024]{1,0:T(8,128)(2,1)} %bitcast.5.og_hbm.refs_4_, ...), custom_call_target="tpu_custom_call" | custom-call | flops 268435456 | bytes 3801092 | tf_op jit(solution)/shard_map/pallas_call | solution.py:36
  4.0 10.0 %all-to-all-start = ((bf16[8,256,128]{2,1,0:T(8,128)(2,1)}), bf16[8,256,128]{2,1,0:T(8,128)(2,1)S(1)}, u32[]{:S(2)}, u32[]{:S(2)}) async-start(bf16[8,256,128]{2,1,0:T(8,128)(2,1)} %get-tuple-element.66), calls=%async_computation | async-start | bytes 1048576 | tf_op jit(solution)/shard_map/all_to_all | solution.py:363
  14.1 0.9 copy-done.5
  15.0 0.5 shard_map.93
  15.5 2.7 %collective-permute-start = (bf16[32,1024]{1,0:T(8,128)(2,1)S(1)}, bf16[32,1024]{1,0:T(8,128)(2,1)S(1)}, u32[]{:S(2)}, u32[]{:S(2)}) collective-permute-start(bf16[32,1024]{1,0:T(8,128)(2,1)S(1)} %get-tuple-element.68), channel_id=1, source_target_pairs={{0,8},{8,0},{16,24},{24,16},{32,40},{40,32},{48,56},{56,48},{1,9},... | collective-permute-start | bytes 196616 | tf_op jit(solution)/shard_map/ppermute | solution.py:415
  18.2 1.2 collective-permute-start.1
  19.4 0.3 collective-permute-start.2
  19.7 2.7 %collective-permute-start.3 = (bf16[32,1024]{1,0:T(8,128)(2,1)S(1)}, bf16[32,1024]{1,0:T(8,128)(2,1)S(1)}, u32[]{:S(2)}, u32[]{:S(2)}) collective-permute-start(bf16[32,1024]{1,0:T(8,128)(2,1)S(1)} %get-tuple-element.71), channel_id=1, source_target_pairs={{0,32},{8,40},{16,48},{24,56},{32,0},{40,8},{48,16},{56,24},{1,33}... | collective-permute-start | bytes 196616 | tf_op jit(solution)/shard_map/ppermute | solution.py:415
  22.5 2.6 %collective-permute-start.4 = (bf16[32,1024]{1,0:T(8,128)(2,1)S(1)}, bf16[32,1024]{1,0:T(8,128)(2,1)S(1)}, u32[]{:S(2)}, u32[]{:S(2)}) collective-permute-start(bf16[32,1024]{1,0:T(8,128)(2,1)S(1)} %get-tuple-element.72), channel_id=1, source_target_pairs={{0,40},{8,32},{16,56},{24,48},{32,8},{40,0},{48,24},{56,16},{1,41}... | collective-permute-start | bytes 196616 | tf_op jit(solution)/shard_map/ppermute | solution.py:415
  25.1 2.5 %collective-permute-start.5 = (bf16[32,1024]{1,0:T(8,128)(2,1)S(1)}, bf16[32,1024]{1,0:T(8,128)(2,1)S(1)}, u32[]{:S(2)}, u32[]{:S(2)}) collective-permute-start(bf16[32,1024]{1,0:T(8,128)(2,1)S(1)} %get-tuple-element.73), channel_id=1, source_target_pairs={{0,48},{8,56},{16,32},{24,40},{32,16},{40,24},{48,0},{56,8},{1,49}... | collective-permute-start | bytes 196616 | tf_op jit(solution)/shard_map/ppermute | solution.py:415
  27.5 0.3 collective-permute-start.6
  27.8 2.4 %collective-permute-done.4.rest_5_ = bf16[32,1024]{1,0:T(8,128)(2,1)S(1)} collective-permute-done((bf16[32,1024]{1,0:T(8,128)(2,1)S(1)}, bf16[32,1024]{1,0:T(8,128)(2,1)S(1)}, u32[]{:S(2)}, u32[]{:S(2)}) %collective-permute-start.4) | collective-permute-done | bytes 65568 | tf_op jit(solution)/shard_map/ppermute | solution.py:415
  30.2 0.2 collective-permute-done.5.rest_6_
  30.4 3.9 %collective-permute-done.6.rest_7_ = bf16[32,1024]{1,0:T(8,128)(2,1)S(1)} collective-permute-done((bf16[32,1024]{1,0:T(8,128)(2,1)S(1)}, bf16[32,1024]{1,0:T(8,128)(2,1)S(1)}, u32[]{:S(2)}, u32[]{:S(2)}) %collective-permute-start.6) | collective-permute-done | bytes 65568 | tf_op jit(solution)/shard_map/ppermute | solution.py:415
  34.3 4.3 %collective-permute-start.7 = (bf16[8,128,128]{2,1,0:T(8,128)(2,1)S(1)}, bf16[8,128,128]{2,1,0:T(8,128)(2,1)S(1)}, u32[]{:S(2)}, u32[]{:S(2)}) collective-permute-start(bf16[8,128,128]{2,1,0:T(8,128)(2,1)S(1)} %slice.6), channel_id=1, source_target_pairs={{0,12},{4,8},{8,20},{12,16},{16,28},{20,24},{24,36},{28,32},{32,44... | collective-permute-start | bytes 786440 | tf_op jit(solution)/shard_map/ppermute | solution.py:425
  38.6 3.9 %collective-permute-start.10 = (bf16[128,1024]{1,0:T(8,128)(2,1)}, bf16[128,1024]{1,0:T(8,128)(2,1)}, u32[]{:S(2)}, u32[]{:S(2)}) collective-permute-start(bf16[128,1024]{1,0:T(8,128)(2,1)} %bitcast.5.og_hbm.refs_4_), channel_id=1, source_target_pairs={{0,192},{64,128},{128,64},{192,0},{1,193},{65,129},{129,65},{193,1... | collective-permute-start | bytes 786440 | tf_op jit(solution)/shard_map/ppermute | solution.py:436
  42.5 0.7 collective-permute-start.9
  43.2 3.6 %shard_map.94 = (bf16[32,1024]{1,0:T(8,128)(2,1)S(1)}, bf16[32,1024]{1,0:T(8,128)(2,1)S(1)}, bf16[32,1024]{1,0:T(8,128)(2,1)S(1)}, bf16[32,1024]{1,0:T(8,128)(2,...) custom-call(s32[1]{0:T(128)} %bitcast.me_ref.first_ref.block_ref, ...), custom_call_target="tpu_custom_call" | custom-call | flops 201326592 | bytes 1048580 | tf_op jit(solution)/shard_map/pallas_call | solution.py:36
  46.8 6.8 %shard_map.95 = bf16[8,384,128]{2,1,0:T(8,128)(2,1)S(1)} custom-call(s32[1]{0:T(128)} %bitcast.me_ref.first_ref.block_ref, bf16[8,256,128]{2,1,0:T(8,128)(2,1)S(1)} %all-to-all-done.in_hbm, bf16[8,128,128]{2,1,0:T(8,128)(2,1)S(1)} %collective-permute-done.7.prev_hbm), custom_call_target="tpu_custom_call" | custom-call | flops 1811939328 | bytes 1572868 | tf_op jit(solution)/shard_map/pallas_call | solution.py:36
  53.6 0.9 copy-done.4
  54.5 0.8 collective-permute-done.9.refs_6_
  55.3 6.5 %all-to-all-start.1 = ((bf16[8,384,128]{2,1,0:T(8,128)(2,1)}), bf16[8,384,128]{2,1,0:T(8,128)(2,1)S(1)}, u32[]{:S(2)}, u32[]{:S(2)}) async-start(bf16[8,384,128]{2,1,0:T(8,128)(2,1)} %copy-done.4), calls=%async_computation.1 | async-start | bytes 1572864 | tf_op jit(solution)/shard_map/all_to_all | solution.py:363
  61.8 0.9 collective-permute-start.11
  62.7 0.3 collective-permute-start.12
  63.0 3.0 %collective-permute-start.13 = (bf16[32,1024]{1,0:T(8,128)(2,1)}, bf16[32,1024]{1,0:T(8,128)(2,1)S(1)}, u32[]{:S(2)}, u32[]{:S(2)}) collective-permute-start(bf16[32,1024]{1,0:T(8,128)(2,1)} %get-tuple-element.106), channel_id=1, source_target_pairs={{0,24},{8,16},{16,8},{24,0},{32,56},{40,48},{48,40},{56,32},{1,25}... | collective-permute-start | bytes 196616 | tf_op jit(solution)/shard_map/ppermute | solution.py:415
  66.0 0.7 collective-permute-start.14
  66.7 2.9 %collective-permute-start.15 = (bf16[32,1024]{1,0:T(8,128)(2,1)}, bf16[32,1024]{1,0:T(8,128)(2,1)S(1)}, u32[]{:S(2)}, u32[]{:S(2)}) collective-permute-start(bf16[32,1024]{1,0:T(8,128)(2,1)} %get-tuple-element.108), channel_id=1, source_target_pairs={{0,40},{8,32},{16,56},{24,48},{32,8},{40,0},{48,24},{56,16},{1,41}... | collective-permute-start | bytes 196616 | tf_op jit(solution)/shard_map/ppermute | solution.py:415
  69.6 1.5 %collective-permute-start.16 = (bf16[32,1024]{1,0:T(8,128)(2,1)S(1)}, bf16[32,1024]{1,0:T(8,128)(2,1)S(1)}, u32[]{:S(2)}, u32[]{:S(2)}) collective-permute-start(bf16[32,1024]{1,0:T(8,128)(2,1)S(1)} %get-tuple-element.109), channel_id=1, source_target_pairs={{0,48},{8,56},{16,32},{24,40},{32,16},{40,24},{48,0},{56,8},{1,49}... | collective-permute-start | bytes 196616 | tf_op jit(solution)/shard_map/ppermute | solution.py:415
  71.1 3.0 %collective-permute-start.17 = (bf16[32,1024]{1,0:T(8,128)(2,1)S(1)}, bf16[32,1024]{1,0:T(8,128)(2,1)S(1)}, u32[]{:S(2)}, u32[]{:S(2)}) collective-permute-start(bf16[32,1024]{1,0:T(8,128)(2,1)S(1)} %get-tuple-element.110), channel_id=1, source_target_pairs={{0,56},{8,48},{16,40},{24,32},{32,24},{40,16},{48,8},{56,0},{1,57}... | collective-permute-start | bytes 196616 | tf_op jit(solution)/shard_map/ppermute | solution.py:415
  74.1 0.9 collective-permute-done.16.rest_6_
  74.9 3.8 %collective-permute-done.17.rest_7_ = bf16[32,1024]{1,0:T(8,128)(2,1)S(1)} collective-permute-done((bf16[32,1024]{1,0:T(8,128)(2,1)S(1)}, bf16[32,1024]{1,0:T(8,128)(2,1)S(1)}, u32[]{:S(2)}, u32[]{:S(2)}) %collective-permute-start.17) | collective-permute-done | bytes 65568 | tf_op jit(solution)/shard_map/ppermute | solution.py:415
  78.7 2.6 %all-to-all-done.1.row_hbm = bf16[8,384,128]{2,1,0:T(8,128)(2,1)S(1)} async-done(((bf16[8,384,128]{2,1,0:T(8,128)(2,1)}), bf16[8,384,128]{2,1,0:T(8,128)(2,1)S(1)}, u32[]{:S(2)}, u32[]{:S(2)}) %all-to-all-start.1) | async-done | bytes 786464 | tf_op jit(solution)/shard_map/all_to_all | solution.py:363
  81.3 0.9 shard_map.96
  82.2 1.9 %collective-permute-start.18 = (bf16[256,128]{1,0:T(8,128)(2,1)S(1)}, bf16[256,128]{1,0:T(8,128)(2,1)S(1)}, u32[]{:S(2)}, u32[]{:S(2)}) collective-permute-start(bf16[256,128]{1,0:T(8,128)(2,1)S(1)} %get-tuple-element.112), channel_id=1, source_target_pairs={{0,64},{64,0},{128,192},{192,128},{1,65},{65,1},{129,193},{193,129... | collective-permute-start | bytes 196616 | tf_op jit(solution)/shard_map/ppermute | solution.py:474
  84.0 4.5 %collective-permute-start.19 = (bf16[256,128]{1,0:T(8,128)(2,1)S(1)}, bf16[256,128]{1,0:T(8,128)(2,1)S(1)}, u32[]{:S(2)}, u32[]{:S(2)}) collective-permute-start(bf16[256,128]{1,0:T(8,128)(2,1)S(1)} %get-tuple-element.113), channel_id=1, source_target_pairs={{0,128},{64,192},{128,0},{192,64},{1,129},{65,193},{129,1},{193,65... | collective-permute-start | bytes 196616 | tf_op jit(solution)/shard_map/ppermute | solution.py:474
  88.6 2.0 %shard_map.97 = (bf16[128,1024]{1,0:T(8,128)(2,1)}, bf16[128,1024]{1,0:T(8,128)(2,1)}) custom-call(s32[1]{0:T(128)S(6)} %mul.3.flip_ref, s32[1]{0:T(128)} %bitcast.me_ref.first_ref.block_ref, bf16[1024,1024]{1,0:T(8,128)(2,1)S(1)} %copy-done, bf16[8,384,128]{2,1,0:T(8,128)(2,1)S(1)} %all-to-all-done.1.row_hbm, ...), custom_call_target="tpu_custom_call" | custom-call | flops 268435456 | bytes 3932168 | tf_op jit(solution)/shard_map/pallas_call | solution.py:36
  90.6 0.2 collective-permute-done.19.refs_2_
  90.8 1.7 %collective-permute-done.20.refs_3_ = bf16[256,128]{1,0:T(8,128)(2,1)S(1)} collective-permute-done((bf16[256,128]{1,0:T(8,128)(2,1)S(1)}, bf16[256,128]{1,0:T(8,128)(2,1)S(1)}, u32[]{:S(2)}, u32[]{:S(2)}) %collective-permute-start.20) | collective-permute-done | bytes 65568 | tf_op jit(solution)/shard_map/ppermute | solution.py:474
  92.6 0.6 copy-done.9
  93.2 2.6 %shard_map.99 = bf16[16,16,1024]{2,1,0:T(8,128)(2,1)} custom-call(bf16[256,128]{1,0:T(8,128)(2,1)} %copy-done.6, bf16[256,128]{1,0:T(8,128)(2,1)} %copy-done.7, bf16[256,128]{1,0:T(8,128)(2,1)} %copy-done.8, bf16[256,128]{1,0:T(8,128)(2,1)} %copy-done.9, bf16[128,1024]{1,0:T(8,128)(2,1)} %bitcast.5.og_hbm.refs_4_, ...), custom_call_target="tpu_custom_call" | custom-call | flops 268435456 | bytes 1835008 | tf_op jit(solution)/shard_map/pallas_call | solution.py:36
  95.8 4.3 %all-to-all-start.2 = ((bf16[16,16,1024]{2,1,0:T(8,128)(2,1)}), bf16[16,16,1024]{2,1,0:T(8,128)(2,1)S(1)}, u32[]{:S(2)}, u32[]{:S(2)}) async-start(bf16[16,16,1024]{2,1,0:T(8,128)(2,1)} %shard_map.99), calls=%async_computation.2 | async-start | bytes 1048576 | tf_op jit(solution)/shard_map/all_to_all | solution.py:363
  100.1 1.3 %collective-permute-start.21 = (bf16[8,128,128]{2,1,0:T(8,128)(2,1)S(1)}, bf16[8,128,128]{2,1,0:T(8,128)(2,1)S(1)}, u32[]{:S(2)}, u32[]{:S(2)}) collective-permute-start(bf16[8,128,128]{2,1,0:T(8,128)(2,1)S(1)} %slice.8), channel_id=1, source_target_pairs={{8,0},{16,8},{24,16},{32,24},{40,32},{48,40},{56,48},{9,1},{17,9},... | collective-permute-start | bytes 786440 | tf_op jit(solution)/shard_map/ppermute | solution.py:477
  101.4 9.5 %all-to-all-done.2.in_ref = bf16[16,16,1024]{2,1,0:T(8,128)(2,1)S(1)} async-done(((bf16[16,16,1024]{2,1,0:T(8,128)(2,1)}), bf16[16,16,1024]{2,1,0:T(8,128)(2,1)S(1)}, u32[]{:S(2)}, u32[]{:S(2)}) %all-to-all-start.2) | async-done | bytes 524320 | tf_op jit(solution)/shard_map/all_to_all | solution.py:363
  110.8 0.7 shard_map.100
  111.6 6.4 %all-to-all-start.3 = ((bf16[16,16,256]{2,1,0:T(8,128)(2,1)}), bf16[16,16,256]{2,1,0:T(8,128)(2,1)S(1)}, u32[]{:S(2)}, u32[]{:S(2)}) async-start(bf16[16,16,256]{2,1,0:T(8,128)(2,1)} %shard_map.100), calls=%async_computation.3 | async-start | bytes 262144 | tf_op jit(solution)/shard_map/all_to_all | solution.py:363
  118.0 1.5 %shard_map.98 = (bf16[128,1024]{1,0:T(8,128)(2,1)}, bf16[128,1024]{1,0:T(8,128)(2,1)}) custom-call(s32[1]{0:T(128)S(6)} %mul.3.flip_ref, s32[1]{0:T(128)} %bitcast.me_ref.first_ref.block_ref, bf16[8,128,128]{2,1,0:T(8,128)(2,1)S(1)} %collective-permute-done.21.later_hbm, bf16[8,384,128]{2,1,0:T(8,128)(2,1)S(1)} %all-to-all-done.1.row_hbm, ...), custom_call_target="tpu_custom_call" | custom-call | bytes 2097160 | tf_op jit(solution)/shard_map/pallas_call | solution.py:36
  119.5 7.7 %all-to-all-done.3.in_ref = bf16[16,16,256]{2,1,0:T(8,128)(2,1)S(1)} async-done(((bf16[16,16,256]{2,1,0:T(8,128)(2,1)}), bf16[16,16,256]{2,1,0:T(8,128)(2,1)S(1)}, u32[]{:S(2)}, u32[]{:S(2)}) %all-to-all-start.3) | async-done | bytes 131104 | tf_op jit(solution)/shard_map/all_to_all | solution.py:363
  127.2 0.7 shard_map.101
  (36 shorter events, 0.2 us)
Async XLA Ops:
  0.6 13.4 %copy-start.1 = (bf16[1,128,1024]{2,1,0:T(8,128)(2,1)S(1)}, bf16[1,128,1024]{2,1,0:T(8,128)(2,1)}, u32[]{:S(2)}) copy-start(bf16[1,128,1024]{2,1,0:T(8,128)(2,1)} %param.5) | copy-start | bytes 786436
  0.6 13.4 %copy-start.2 = (bf16[1,128,1024]{2,1,0:T(8,128)(2,1)S(1)}, bf16[1,128,1024]{2,1,0:T(8,128)(2,1)}, u32[]{:S(2)}) copy-start(bf16[1,128,1024]{2,1,0:T(8,128)(2,1)} %param.6) | copy-start | bytes 786436
  0.7 13.4 %copy-start.3 = (bf16[1,128,1024]{2,1,0:T(8,128)(2,1)S(1)}, bf16[1,128,1024]{2,1,0:T(8,128)(2,1)}, u32[]{:S(2)}) copy-start(bf16[1,128,1024]{2,1,0:T(8,128)(2,1)} %param.7) | copy-start | bytes 786436
  4.0 30.3 %all-to-all-start = ((bf16[8,256,128]{2,1,0:T(8,128)(2,1)}), bf16[8,256,128]{2,1,0:T(8,128)(2,1)S(1)}, u32[]{:S(2)}, u32[]{:S(2)}) async-start(bf16[8,256,128]{2,1,0:T(8,128)(2,1)} %get-tuple-element.66), calls=%async_computation | async-start | bytes 1048576 | tf_op jit(solution)/shard_map/all_to_all | solution.py:363
  14.1 0.9 copy-start.5
  15.5 9.6 %collective-permute-start = (bf16[32,1024]{1,0:T(8,128)(2,1)S(1)}, bf16[32,1024]{1,0:T(8,128)(2,1)S(1)}, u32[]{:S(2)}, u32[]{:S(2)}) collective-permute-start(bf16[32,1024]{1,0:T(8,128)(2,1)S(1)} %get-tuple-element.68), channel_id=1, source_target_pairs={{0,8},{8,0},{16,24},{24,16},{32,40},{40,32},{48,56},{56,48},{1,9},... | collective-permute-start | bytes 196616 | tf_op jit(solution)/shard_map/ppermute | solution.py:415
  18.2 9.3 %collective-permute-start.1 = (bf16[32,1024]{1,0:T(8,128)(2,1)S(1)}, bf16[32,1024]{1,0:T(8,128)(2,1)S(1)}, u32[]{:S(2)}, u32[]{:S(2)}) collective-permute-start(bf16[32,1024]{1,0:T(8,128)(2,1)S(1)} %get-tuple-element.69), channel_id=1, source_target_pairs={{0,16},{8,24},{16,0},{24,8},{32,48},{40,56},{48,32},{56,40},{1,17}... | collective-permute-start | bytes 196616 | tf_op jit(solution)/shard_map/ppermute | solution.py:415
  19.4 8.4 %collective-permute-start.2 = (bf16[32,1024]{1,0:T(8,128)(2,1)S(1)}, bf16[32,1024]{1,0:T(8,128)(2,1)S(1)}, u32[]{:S(2)}, u32[]{:S(2)}) collective-permute-start(bf16[32,1024]{1,0:T(8,128)(2,1)S(1)} %get-tuple-element.70), channel_id=1, source_target_pairs={{0,24},{8,16},{16,8},{24,0},{32,56},{40,48},{48,40},{56,32},{1,25}... | collective-permute-start | bytes 196616 | tf_op jit(solution)/shard_map/ppermute | solution.py:415
  19.7 8.1 %collective-permute-start.3 = (bf16[32,1024]{1,0:T(8,128)(2,1)S(1)}, bf16[32,1024]{1,0:T(8,128)(2,1)S(1)}, u32[]{:S(2)}, u32[]{:S(2)}) collective-permute-start(bf16[32,1024]{1,0:T(8,128)(2,1)S(1)} %get-tuple-element.71), channel_id=1, source_target_pairs={{0,32},{8,40},{16,48},{24,56},{32,0},{40,8},{48,16},{56,24},{1,33}... | collective-permute-start | bytes 196616 | tf_op jit(solution)/shard_map/ppermute | solution.py:415
  22.5 7.7 %collective-permute-start.4 = (bf16[32,1024]{1,0:T(8,128)(2,1)S(1)}, bf16[32,1024]{1,0:T(8,128)(2,1)S(1)}, u32[]{:S(2)}, u32[]{:S(2)}) collective-permute-start(bf16[32,1024]{1,0:T(8,128)(2,1)S(1)} %get-tuple-element.72), channel_id=1, source_target_pairs={{0,40},{8,32},{16,56},{24,48},{32,8},{40,0},{48,24},{56,16},{1,41}... | collective-permute-start | bytes 196616 | tf_op jit(solution)/shard_map/ppermute | solution.py:415
  25.1 5.3 %collective-permute-start.5 = (bf16[32,1024]{1,0:T(8,128)(2,1)S(1)}, bf16[32,1024]{1,0:T(8,128)(2,1)S(1)}, u32[]{:S(2)}, u32[]{:S(2)}) collective-permute-start(bf16[32,1024]{1,0:T(8,128)(2,1)S(1)} %get-tuple-element.73), channel_id=1, source_target_pairs={{0,48},{8,56},{16,32},{24,40},{32,16},{40,24},{48,0},{56,8},{1,49}... | collective-permute-start | bytes 196616 | tf_op jit(solution)/shard_map/ppermute | solution.py:415
  27.5 6.7 %collective-permute-start.6 = (bf16[32,1024]{1,0:T(8,128)(2,1)S(1)}, bf16[32,1024]{1,0:T(8,128)(2,1)S(1)}, u32[]{:S(2)}, u32[]{:S(2)}) collective-permute-start(bf16[32,1024]{1,0:T(8,128)(2,1)S(1)} %get-tuple-element.74), channel_id=1, source_target_pairs={{0,56},{8,48},{16,40},{24,32},{32,24},{40,16},{48,8},{56,0},{1,57}... | collective-permute-start | bytes 196616 | tf_op jit(solution)/shard_map/ppermute | solution.py:415
  34.3 12.5 %collective-permute-start.7 = (bf16[8,128,128]{2,1,0:T(8,128)(2,1)S(1)}, bf16[8,128,128]{2,1,0:T(8,128)(2,1)S(1)}, u32[]{:S(2)}, u32[]{:S(2)}) collective-permute-start(bf16[8,128,128]{2,1,0:T(8,128)(2,1)S(1)} %slice.6), channel_id=1, source_target_pairs={{0,12},{4,8},{8,20},{12,16},{16,28},{20,24},{24,36},{28,32},{32,44... | collective-permute-start | bytes 786440 | tf_op jit(solution)/shard_map/ppermute | solution.py:425
  38.6 15.9 %collective-permute-start.10 = (bf16[128,1024]{1,0:T(8,128)(2,1)}, bf16[128,1024]{1,0:T(8,128)(2,1)}, u32[]{:S(2)}, u32[]{:S(2)}) collective-permute-start(bf16[128,1024]{1,0:T(8,128)(2,1)} %bitcast.5.og_hbm.refs_4_), channel_id=1, source_target_pairs={{0,192},{64,128},{128,64},{192,0},{1,193},{65,129},{129,65},{193,1... | collective-permute-start | bytes 786440 | tf_op jit(solution)/shard_map/ppermute | solution.py:436
  42.5 12.8 %collective-permute-start.9 = (bf16[128,1024]{1,0:T(8,128)(2,1)}, bf16[128,1024]{1,0:T(8,128)(2,1)}, u32[]{:S(2)}, u32[]{:S(2)}) collective-permute-start(bf16[128,1024]{1,0:T(8,128)(2,1)} %bitcast.5.og_hbm.refs_4_), channel_id=1, source_target_pairs={{0,128},{64,192},{128,0},{192,64},{1,129},{65,193},{129,1},{193,65... | collective-permute-start | bytes 786440 | tf_op jit(solution)/shard_map/ppermute | solution.py:436
  43.2 12.1 %collective-permute-start.8 = (bf16[128,1024]{1,0:T(8,128)(2,1)}, bf16[128,1024]{1,0:T(8,128)(2,1)}, u32[]{:S(2)}, u32[]{:S(2)}) collective-permute-start(bf16[128,1024]{1,0:T(8,128)(2,1)} %bitcast.5.og_hbm.refs_4_), channel_id=1, source_target_pairs={{0,64},{64,0},{128,192},{192,128},{1,65},{65,1},{129,193},{193,129... | collective-permute-start | bytes 786440 | tf_op jit(solution)/shard_map/ppermute | solution.py:436
  53.6 0.9 copy-start.4
  54.5 34.0 %copy-start = (bf16[1024,1024]{1,0:T(8,128)(2,1)S(1)}, bf16[1024,1024]{1,0:T(8,128)(2,1)}, u32[]{:S(2)}) copy-start(bf16[1024,1024]{1,0:T(8,128)(2,1)} %w_hbm.3) | copy-start | bytes 6291460
  55.3 25.9 %all-to-all-start.1 = ((bf16[8,384,128]{2,1,0:T(8,128)(2,1)}), bf16[8,384,128]{2,1,0:T(8,128)(2,1)S(1)}, u32[]{:S(2)}, u32[]{:S(2)}) async-start(bf16[8,384,128]{2,1,0:T(8,128)(2,1)} %copy-done.4), calls=%async_computation.1 | async-start | bytes 1572864 | tf_op jit(solution)/shard_map/all_to_all | solution.py:363
  61.8 7.8 %collective-permute-start.11 = (bf16[32,1024]{1,0:T(8,128)(2,1)S(1)}, bf16[32,1024]{1,0:T(8,128)(2,1)S(1)}, u32[]{:S(2)}, u32[]{:S(2)}) collective-permute-start(bf16[32,1024]{1,0:T(8,128)(2,1)S(1)} %get-tuple-element.104), channel_id=1, source_target_pairs={{0,8},{8,0},{16,24},{24,16},{32,40},{40,32},{48,56},{56,48},{1,9},... | collective-permute-start | bytes 196616 | tf_op jit(solution)/shard_map/ppermute | solution.py:415
  62.7 8.3 %collective-permute-start.12 = (bf16[32,1024]{1,0:T(8,128)(2,1)S(1)}, bf16[32,1024]{1,0:T(8,128)(2,1)S(1)}, u32[]{:S(2)}, u32[]{:S(2)}) collective-permute-start(bf16[32,1024]{1,0:T(8,128)(2,1)S(1)} %get-tuple-element.105), channel_id=1, source_target_pairs={{0,16},{8,24},{16,0},{24,8},{32,48},{40,56},{48,32},{56,40},{1,17}... | collective-permute-start | bytes 196616 | tf_op jit(solution)/shard_map/ppermute | solution.py:415
  63.0 11.0 %collective-permute-start.13 = (bf16[32,1024]{1,0:T(8,128)(2,1)}, bf16[32,1024]{1,0:T(8,128)(2,1)S(1)}, u32[]{:S(2)}, u32[]{:S(2)}) collective-permute-start(bf16[32,1024]{1,0:T(8,128)(2,1)} %get-tuple-element.106), channel_id=1, source_target_pairs={{0,24},{8,16},{16,8},{24,0},{32,56},{40,48},{48,40},{56,32},{1,25}... | collective-permute-start | bytes 196616 | tf_op jit(solution)/shard_map/ppermute | solution.py:415
  66.0 8.1 %collective-permute-start.14 = (bf16[32,1024]{1,0:T(8,128)(2,1)}, bf16[32,1024]{1,0:T(8,128)(2,1)S(1)}, u32[]{:S(2)}, u32[]{:S(2)}) collective-permute-start(bf16[32,1024]{1,0:T(8,128)(2,1)} %get-tuple-element.107), channel_id=1, source_target_pairs={{0,32},{8,40},{16,48},{24,56},{32,0},{40,8},{48,16},{56,24},{1,33}... | collective-permute-start | bytes 196616 | tf_op jit(solution)/shard_map/ppermute | solution.py:415
  66.7 7.4 %collective-permute-start.15 = (bf16[32,1024]{1,0:T(8,128)(2,1)}, bf16[32,1024]{1,0:T(8,128)(2,1)S(1)}, u32[]{:S(2)}, u32[]{:S(2)}) collective-permute-start(bf16[32,1024]{1,0:T(8,128)(2,1)} %get-tuple-element.108), channel_id=1, source_target_pairs={{0,40},{8,32},{16,56},{24,48},{32,8},{40,0},{48,24},{56,16},{1,41}... | collective-permute-start | bytes 196616 | tf_op jit(solution)/shard_map/ppermute | solution.py:415
  69.6 5.3 %collective-permute-start.16 = (bf16[32,1024]{1,0:T(8,128)(2,1)S(1)}, bf16[32,1024]{1,0:T(8,128)(2,1)S(1)}, u32[]{:S(2)}, u32[]{:S(2)}) collective-permute-start(bf16[32,1024]{1,0:T(8,128)(2,1)S(1)} %get-tuple-element.109), channel_id=1, source_target_pairs={{0,48},{8,56},{16,32},{24,40},{32,16},{40,24},{48,0},{56,8},{1,49}... | collective-permute-start | bytes 196616 | tf_op jit(solution)/shard_map/ppermute | solution.py:415
  71.1 7.6 %collective-permute-start.17 = (bf16[32,1024]{1,0:T(8,128)(2,1)S(1)}, bf16[32,1024]{1,0:T(8,128)(2,1)S(1)}, u32[]{:S(2)}, u32[]{:S(2)}) collective-permute-start(bf16[32,1024]{1,0:T(8,128)(2,1)S(1)} %get-tuple-element.110), channel_id=1, source_target_pairs={{0,56},{8,48},{16,40},{24,32},{32,24},{40,16},{48,8},{56,0},{1,57}... | collective-permute-start | bytes 196616 | tf_op jit(solution)/shard_map/ppermute | solution.py:415
  82.1 8.4 %copy-start.6 = (bf16[256,128]{1,0:T(8,128)(2,1)}, bf16[256,128]{1,0:T(8,128)(2,1)S(1)}, u32[]{:S(2)}) copy-start(bf16[256,128]{1,0:T(8,128)(2,1)S(1)} %get-tuple-element.120.refs_0_) | copy-start | bytes 196612
  82.2 8.4 %collective-permute-start.18 = (bf16[256,128]{1,0:T(8,128)(2,1)S(1)}, bf16[256,128]{1,0:T(8,128)(2,1)S(1)}, u32[]{:S(2)}, u32[]{:S(2)}) collective-permute-start(bf16[256,128]{1,0:T(8,128)(2,1)S(1)} %get-tuple-element.112), channel_id=1, source_target_pairs={{0,64},{64,0},{128,192},{192,128},{1,65},{65,1},{129,193},{193,129... | collective-permute-start | bytes 196616 | tf_op jit(solution)/shard_map/ppermute | solution.py:474
  84.0 6.8 %collective-permute-start.19 = (bf16[256,128]{1,0:T(8,128)(2,1)S(1)}, bf16[256,128]{1,0:T(8,128)(2,1)S(1)}, u32[]{:S(2)}, u32[]{:S(2)}) collective-permute-start(bf16[256,128]{1,0:T(8,128)(2,1)S(1)} %get-tuple-element.113), channel_id=1, source_target_pairs={{0,128},{64,192},{128,0},{192,64},{1,129},{65,193},{129,1},{193,65... | collective-permute-start | bytes 196616 | tf_op jit(solution)/shard_map/ppermute | solution.py:474
  88.5 4.1 %collective-permute-start.20 = (bf16[256,128]{1,0:T(8,128)(2,1)S(1)}, bf16[256,128]{1,0:T(8,128)(2,1)S(1)}, u32[]{:S(2)}, u32[]{:S(2)}) collective-permute-start(bf16[256,128]{1,0:T(8,128)(2,1)S(1)} %get-tuple-element.114), channel_id=1, source_target_pairs={{0,192},{64,128},{128,64},{192,0},{1,193},{65,129},{129,65},{193,1... | collective-permute-start | bytes 196616 | tf_op jit(solution)/shard_map/ppermute | solution.py:474
  90.6 2.0 %copy-start.7 = (bf16[256,128]{1,0:T(8,128)(2,1)}, bf16[256,128]{1,0:T(8,128)(2,1)S(1)}, u32[]{:S(2)}) copy-start(bf16[256,128]{1,0:T(8,128)(2,1)S(1)} %collective-permute-done.18.refs_1_) | copy-start | bytes 196612
  90.8 1.7 %copy-start.8 = (bf16[256,128]{1,0:T(8,128)(2,1)}, bf16[256,128]{1,0:T(8,128)(2,1)S(1)}, u32[]{:S(2)}) copy-start(bf16[256,128]{1,0:T(8,128)(2,1)S(1)} %collective-permute-done.19.refs_2_) | copy-start | bytes 196612
  92.6 0.6 copy-start.9
  95.8 15.1 %all-to-all-start.2 = ((bf16[16,16,1024]{2,1,0:T(8,128)(2,1)}), bf16[16,16,1024]{2,1,0:T(8,128)(2,1)S(1)}, u32[]{:S(2)}, u32[]{:S(2)}) async-start(bf16[16,16,1024]{2,1,0:T(8,128)(2,1)} %shard_map.99), calls=%async_computation.2 | async-start | bytes 1048576 | tf_op jit(solution)/shard_map/all_to_all | solution.py:363
  100.1 17.9 %collective-permute-start.21 = (bf16[8,128,128]{2,1,0:T(8,128)(2,1)S(1)}, bf16[8,128,128]{2,1,0:T(8,128)(2,1)S(1)}, u32[]{:S(2)}, u32[]{:S(2)}) collective-permute-start(bf16[8,128,128]{2,1,0:T(8,128)(2,1)S(1)} %slice.8), channel_id=1, source_target_pairs={{8,0},{16,8},{24,16},{32,24},{40,32},{48,40},{56,48},{9,1},{17,9},... | collective-permute-start | bytes 786440 | tf_op jit(solution)/shard_map/ppermute | solution.py:477
  111.6 15.7 %all-to-all-start.3 = ((bf16[16,16,256]{2,1,0:T(8,128)(2,1)}), bf16[16,16,256]{2,1,0:T(8,128)(2,1)S(1)}, u32[]{:S(2)}, u32[]{:S(2)}) async-start(bf16[16,16,256]{2,1,0:T(8,128)(2,1)} %shard_map.100), calls=%async_computation.3 | async-start | bytes 262144 | tf_op jit(solution)/shard_map/all_to_all | solution.py:363

commit v4 on v3

--- a/solution.py
+++ b/solution.py
@@ -15,7 +15,6 @@
 BF16 = jnp.bfloat16
 F32 = jnp.float32
 ROOM = 60 << 20
-EARLY = 7
 SCALE = 1.0 / math.sqrt(DH)
 SCALE_LOG2 = SCALE / math.log(2.0)
 NT = (((1,), (1,)), ((), ()))
@@ -29,7 +28,7 @@
     return lax.dot_general(a, b, dims, preferred_element_type=F32)
 
 
-def call(kernel, out_shape, args, scratch=(), flops=0, vmem=24 << 20, specs=None):
+def call(kernel, out_shape, args, scratch=(), flops=0, vmem=52 << 20, specs=None):
     moved = sum(a.size * a.dtype.itemsize for a in args)
     outs = out_shape if isinstance(out_shape, tuple) else (out_shape,)
     moved += sum(math.prod(o.shape) * o.dtype.itemsize for o in outs)
@@ -74,66 +73,52 @@
         copy.wait()
 
 
-def pack_row_kernel(flip_ref, q_hbm, k_hbm, v_hbm, og_hbm, w_hbm, row_ref, grad_ref, *scratch):
-    og_ref, w_ref, k_ref, v_ref, q_ref, sems = scratch
-    tokens = og_ref.shape[0]
-    half = k_ref.shape[1]
-    fetch(
-        (
-            (og_hbm, og_ref),
-            (w_hbm, w_ref),
-            (k_hbm.at[:, :half], k_ref),
-            (v_hbm.at[:, :half], v_ref),
-            (q_hbm.at[:, :half], q_ref),
-        ),
-        sems,
-    )
+def pack_kernel(
+    flip_ref, me_ref, q_hbm, k_hbm, v_hbm, og_hbm, w_hbm, row_ref, *rest
+):
+    outs = rest[:-8]
+    og_ref, w_ref, k_ref, v_ref, q_ref, kv_all, qg_all, sems = rest[-8:]
+    tokens, width = og_ref.shape
+    half = width // 2
+    pairs = ((k_hbm, k_ref), (v_hbm, v_ref), (q_hbm, q_ref), (og_hbm, og_ref), (w_hbm, w_ref))
+    copies = [
+        pltpu.make_async_copy(source, target, sems.at[i])
+        for i, (source, target) in enumerate(pairs)
+    ]
+    for copy in copies:
+        copy.start()
     low = low_half(tokens)
-    grad = dot(og_ref[...], w_ref[...], NT).astype(BF16)
-    grad_ref[...] = grad[:, half:]
-    for tile in range(half // LANES):
+    heads = half // DH
+
+    def put(tile, one, two, rows, both):
         cut = slice(tile * LANES, (tile + 1) * LANES)
-        kv = paired(k_ref[:, cut], v_ref[:, cut], low)
-        qg = paired(q_ref[:, cut], grad[:, cut], low)
-        for side in range(2):
-            slot = (2 * tile + side) ^ flip_ref[0]
-            row_ref[slot, :tokens] = kv[side]
-            row_ref[slot, tokens:] = qg[side]
-
-
-def pack_col_kernel(me_ref, q_hbm, k_hbm, v_hbm, grad_hbm, *rest):
-    count = len(rest) - 7
-    outs = rest[:count]
-    k_ref, v_ref, q_ref, grad_ref, kv_all, qg_all, sems = rest[count:]
-    tokens, half = k_ref.shape
-    part = tokens // count
-    fetch(
-        (
-            (k_hbm.at[:, half:], k_ref),
-            (v_hbm.at[:, half:], v_ref),
-            (q_hbm.at[:, half:], q_ref),
-            (grad_hbm, grad_ref),
-        ),
-        sems,
-    )
-    low = low_half(tokens)
-    for tile in range(half // LANES):
-        cut = slice(tile * LANES, (tile + 1) * LANES)
-        kv = paired(k_ref[:, cut], v_ref[:, cut], low)
-        qg = paired(q_ref[:, cut], grad_ref[:, cut], low)
-        for side in range(2):
-            lanes = slice((2 * tile + side) * LANES, (2 * tile + side + 1) * LANES)
-            kv_all[:, lanes] = kv[side]
-            qg_all[:, lanes] = qg[side]
-    for hop, out_ref in enumerate(outs):
-        rows = pl.ds(pl.multiple_of((me_ref[0] ^ hop) * part, part), part)
+        for side, value in enumerate(paired(one[:, cut], two[:, cut], low)):
+            head = 2 * tile + side
+            if head < heads:
+                row_ref[head ^ flip_ref[0], rows] = value
+            else:
+                both[:, (head - heads) * LANES : (head - heads + 1) * LANES] = value
+
+    for copy in copies[:3]:
+        copy.wait()
+    for tile in range(width // LANES):
+        put(tile, k_ref, v_ref, slice(0, tokens), kv_all)
+    for copy in copies[3:]:
+        copy.wait()
+    og_ref[...] = dot(og_ref[...], w_ref[...], NT).astype(BF16)
+    for tile in range(width // LANES):
+        put(tile, q_ref, og_ref, slice(tokens, 2 * tokens), qg_all)
+    part = tokens // len(outs)
+    for slot, out_ref in enumerate(outs):
+        rows = pl.ds(pl.multiple_of((me_ref[0] ^ slot) * part, part), part)
         out_ref[:part] = kv_all[rows]
         out_ref[part:] = qg_all[rows]
 
 
-def split_diag(qg, low):
+def split_diag(qg, low, factor=1.0):
     zero = jnp.zeros_like(qg)
-    return jnp.concatenate([jnp.where(low, qg, zero), jnp.where(low, zero, qg)], axis=0)
+    grad = qg * BF16(factor) if factor != 1.0 else qg
+    return jnp.concatenate([jnp.where(low, qg, zero), jnp.where(low, zero, grad)], axis=0)
 
 
 def col_kernel(me_ref, *rest):
@@ -148,22 +133,24 @@
     query = lax.broadcasted_iota(jnp.int32, (tokens, tokens), 1)
     flip = me_ref[0] * part
     allowed = ((key ^ flip) <= (query ^ flip)) & (((query ^ key) & (part - 1)) == 0)
-    for head in range(width // LANES):
-        cut = slice(head * LANES, (head + 1) * LANES)
-        kv = held[:, :part, cut].reshape(tokens, LANES)
-        qg = held[:, part:, cut].reshape(tokens, LANES)
-        diag = split_diag(qg, low)
-        both = dot(kv, diag, NT)
+    heads = range(width // LANES)
+    cuts = [slice(head * LANES, (head + 1) * LANES) for head in heads]
+    kvs = [held[:, :part, cut].reshape(tokens, LANES) for cut in cuts]
+    qgs = [held[:, part:, cut].reshape(tokens, LANES) for cut in cuts]
+    boths = [dot(kv, split_diag(qg, low, SCALE), NT) for kv, qg in zip(kvs, qgs)]
+    pairs = []
+    for both in boths:
         score = jnp.where(allowed, both[:, :tokens] * SCALE_LOG2, -jnp.inf)
         weight = jnp.exp2(score - jnp.max(score, axis=0, keepdims=True))
-        prob = weight / jnp.sum(weight, axis=0, keepdims=True)
         grad = both[:, tokens:]
+        scaled = 1.0 / jnp.sum(weight, axis=0, keepdims=True)
+        prob = weight * scaled
         delta = jnp.sum(prob * grad, axis=0, keepdims=True)
-        score_grad = prob * (grad - delta) * SCALE
-        pair = jnp.concatenate([score_grad.astype(BF16), prob.astype(BF16)], axis=1)
-        kv_grad = dot(pair, diag).astype(BF16)
-        kv_t = kv.astype(F32).T.astype(BF16)
-        flat = dot(kv_t, pair)
+        score_grad = prob * (grad - delta)
+        pairs.append(jnp.concatenate([score_grad.astype(BF16), prob.astype(BF16)], axis=1))
+    kv_grads = [dot(pair, split_diag(qg, low)).astype(BF16) for pair, qg in zip(pairs, qgs)]
+    flats = [dot(kv.astype(F32).T.astype(BF16), pair) for kv, pair in zip(kvs, pairs)]
+    for cut, flat, kv_grad in zip(cuts, flats, kv_grads):
         back = jnp.concatenate([flat[:DH, :tokens], flat[DH:, tokens:]], axis=0)
         back = back.T.astype(BF16)
         for slot, out_ref in enumerate(outs):
@@ -186,14 +173,16 @@
         ),
         sems,
     )
-    for block in range(2 * tiles):
-        kv_t[:, block * size : (block + 1) * size] = kv[block].astype(F32).T.astype(BF16)
     acc[...] = jnp.zeros_like(acc)
     key = lax.broadcasted_iota(jnp.int32, (size, size), 0)
     query = lax.broadcasted_iota(jnp.int32, (size, size), 1)
-    for tile in range(tiles):
-        base = tile * size
-        diag = split_diag(qg[tile], low)
+
+    def turn(block):
+        kv_t[:, block * size : (block + 1) * size] = kv[block].astype(F32).T.astype(BF16)
+
+    def scores(tile):
+        slot = tile % 2
+        diag = split_diag(qg[tile], low, SCALE)
         top = None
         for chunk in range(chunks):
             rows = slice(chunk * size, (chunk + 1) * size)
@@ -205,34 +194,51 @@
                 now = jnp.where(key <= query, now, -jnp.inf)
             if tile + chunk < tiles:
                 now = now + bias
-            score[rows] = now
-            grad[rows] = both[:, size:]
+            score[slot, rows] = now
+            grad[slot, rows] = both[:, size:]
             best = jnp.max(now, axis=0, keepdims=True)
             top = best if top is None else jnp.maximum(top, best)
+        return top
+
+    def softmax(tile, top):
+        slot = tile % 2
         total = jnp.zeros((1, size), F32)
         inner = jnp.zeros((1, size), F32)
         for chunk in range(chunks):
             rows = slice(chunk * size, (chunk + 1) * size)
-            weight = jnp.exp2(score[rows] - top)
-            score[rows] = weight
+            weight = jnp.exp2(score[slot, rows] - top)
+            score[slot, rows] = weight
             total = total + jnp.sum(weight, axis=0, keepdims=True)
-            inner = inner + jnp.sum(weight * grad[rows], axis=0, keepdims=True)
+            inner = inner + jnp.sum(weight * grad[slot, rows], axis=0, keepdims=True)
         scaled = 1.0 / total
         delta = inner * scaled
         for chunk in range(chunks):
             rows = slice(chunk * size, (chunk + 1) * size)
-            prob = score[rows] * scaled
-            pair[rows, :size] = (prob * (grad[rows] - delta) * SCALE).astype(BF16)
-            pair[rows, size:] = prob.astype(BF16)
-        window = slice(base, base + chunks * size)
-        acc[window] += dot(pair[...], diag)
-        flat = dot(kv_t[:, window], pair[...])
+            prob = score[slot, rows] * scaled
+            pair[slot, rows, :size] = (prob * (grad[slot, rows] - delta)).astype(BF16)
+            pair[slot, rows, size:] = prob.astype(BF16)
+
+    def products(tile):
+        slot = tile % 2
+        window = slice(tile * size, (tile + chunks) * size)
+        acc[window] += dot(pair[slot], split_diag(qg[tile], low))
+        flat = dot(kv_t[:, window], pair[slot])
         back = jnp.concatenate([flat[:DH, :size], flat[DH:, size:]], axis=0)
         out_ref[tile, :size] = back.T.astype(BF16)
+
+    top = scores(0)
+    for block in range(chunks):
+        turn(block)
     for tile in range(tiles):
-        out_ref[tile, size : 2 * size] = acc[span + tile * size : span + (tile + 1) * size].astype(
-            BF16
-        )
+        later = scores(tile + 1) if tile + 1 < tiles else None
+        softmax(tile, top)
+        products(tile)
+        if tile + 1 < tiles:
+            turn(tile + chunks)
+        top = later
+    for tile in range(tiles):
+        own = acc[span + tile * size : span + (tile + 1) * size]
+        out_ref[tile, size : 2 * size] = own.astype(BF16)
         out_ref[tile, 2 * size :] = acc[tile * size : (tile + 1) * size].astype(BF16)
 
 
@@ -326,37 +332,40 @@
     out_ref[...] = dot(att[...], grad[...]).astype(BF16).reshape(out_ref.shape)
 
 
-def plane_sum_kernel(in_ref, out_ref):
-    planes, piece, width = in_ref.shape
-    pieces, rows, lanes = out_ref.shape
-    kept = rows * lanes // width
-    lines = piece // kept
+def plane_sum_kernel(me_ref, in_ref, *rest):
+    outs, held = rest[:-1], rest[-1]
+    planes = in_ref.shape[0]
+    lines, rows, lanes = held.shape
+    kept = in_ref.shape[1] // lines
     total = in_ref[0].astype(F32)
     for plane in range(1, planes):
         total = total + in_ref[plane].astype(F32)
     for line in range(lines):
         mine = total[line * kept : (line + 1) * kept]
-        cuts = [mine[:, i * lanes : (i + 1) * lanes] for i in range(width // lanes)]
-        packed = jnp.concatenate(cuts, axis=0).astype(BF16)
-        for clip in range(pieces // lines):
-            out_ref[clip * lines + line] = packed
-
-
-def line_sum_kernel(clips, factor, in_ref, out_ref):
-    pieces, rows, lanes = in_ref.shape
-    lines = pieces // clips
+        cuts = [mine[:, i * lanes : (i + 1) * lanes] for i in range(rows // kept)]
+        held[line] = jnp.concatenate(cuts, axis=0)
+    for hop, out_ref in enumerate(outs):
+        out_ref[...] = held[me_ref[0] ^ hop].astype(BF16)
+
+
+def line_sum_kernel(factor, *refs):
+    total = refs[0][...].astype(F32)
+    for ref in refs[1:-1]:
+        total = total + ref[...].astype(F32)
+    refs[-1][...] = total * factor
+
+
+def gather_kernel(me_ref, *rest):
+    parts, out_ref, held = rest[:-2], rest[-2], rest[-1]
+    clips, rows, lanes = held.shape
     kept = out_ref.shape[0] // clips
+    for hop, ref in enumerate(parts):
+        held[me_ref[0] ^ hop] = ref[...]
     for clip in range(clips):
-        total = in_ref[clip * lines].astype(F32)
-        for line in range(1, lines):
-            total = total + in_ref[clip * lines + line].astype(F32)
-        total = total * factor
-        for part in range(rows // kept):
-            cut = slice(part * lanes, (part + 1) * lanes)
-            for row in range(kept):
-                at = part * kept + row
-                to = row * clips + clip
-                out_ref[to : to + 1, cut] = total[at : at + 1]
+        for at in range(rows):
+            to = (at % kept) * clips + clip
+            cut = slice(at // kept * lanes, (at // kept + 1) * lanes)
+            out_ref[to : to + 1, cut] = held[clip, at : at + 1]
 
 
 def swapped(array, axes):
@@ -377,53 +386,48 @@
     q, k, v, og = (a.reshape(tokens, width) for a in (queries, keys, values, out_grad))
     block_index = lax.axis_index("b").astype(jnp.int32).reshape(1)
     clip_index = lax.axis_index("d").astype(jnp.int32).reshape(1)
+    line_index = lax.axis_index("z").astype(jnp.int32).reshape(1)
     flip = (block_index & 1) * lines
 
     project = 2 * tokens * width * width
-    half = width // 2
     sems = pltpu.SemaphoreType.DMA
-    row_in, grad_col = call(
-        pack_row_kernel,
-        (shape(heads, 2 * tokens, LANES), shape(tokens, half)),
-        (flip, q, k, v, og, w_out),
+    col_piece = shape(2 * part, heads * LANES)
+    row_in, *col_in = call(
+        pack_kernel,
+        (shape(heads, 2 * tokens, LANES), *[col_piece] * blocks),
+        (flip, block_index, q, k, v, og, w_out),
         scratch=(
             pltpu.VMEM((tokens, width), BF16),
             pltpu.VMEM(w_out.shape, BF16),
-            *[pltpu.VMEM((tokens, half), BF16)] * 3,
+            *[pltpu.VMEM((tokens, width), BF16)] * 5,
             sems((5,)),
         ),
         flops=project,
         vmem=ROOM,
-        specs=[SMEM] + [HBM] * 5,
+        specs=[SMEM] * 2 + [HBM] * 5,
     )
     row_got = swapped(row_in, row_axes)
-    col_piece = shape(2 * part, heads * LANES)
-    col_in = call(
-        pack_col_kernel,
-        (col_piece,) * blocks,
-        (block_index, q, k, v, grad_col),
-        scratch=(
-            *[pltpu.VMEM((tokens, half), BF16)] * 4,
-            *[pltpu.VMEM((tokens, width), BF16)] * 2,
-            sems((4,)),
-        ),
-        specs=[SMEM] + [HBM] * 4,
-    )
-
-    def to_members(pieces, hops):
-        return [
-            lax.ppermute(pieces[hop], "b", [(i, i ^ hop) for i in range(blocks)]) for hop in hops
-        ]
-
-    first, second = range(1, EARLY + 1), range(EARLY + 1, blocks)
-    col_got = to_members(col_in, first)
-    row_got, og_later, *rest = lax.optimization_barrier(
-        (row_got, og, *col_got, *(col_in[hop] for hop in second))
-    )
-    col_got, col_wait = rest[:EARLY], dict(zip(second, rest[EARLY:]))
+
+    def to_members(pieces):
+        got = dict(enumerate(pieces))
+        for hop in range(1, blocks):
+            got[hop] = lax.ppermute(pieces[hop], "b", [(i, i ^ hop) for i in range(blocks)])
+        return [got[hop] for hop in range(blocks)]
+
+    row_got, og_later, *col_got = lax.optimization_barrier((row_got, og, *to_members(col_in)))
     onward = [(i * yl + j, (i + 1) * yl + j ^ 1) for i in range(blocks - 1) for j in range(yl)]
     prev = lax.ppermute(row_got[:, :tokens], ("b", "yl"), onward)
-    col_got = [col_in[0], *col_got, *to_members(col_wait, second)]
+    col_res = call(
+        col_kernel,
+        (col_piece,) * blocks,
+        (block_index, *col_got),
+        scratch=(pltpu.VMEM((blocks, 2 * part, heads * LANES), BF16), sems((blocks,))),
+        flops=heads * 12 * tokens * tokens * LANES,
+        specs=[SMEM] + [HBM] * blocks,
+    )
+    beside, beyond = (
+        lax.ppermute(og_later, "d", [(i, i ^ hop) for i in range(clips)]) for hop in (1, 2)
+    )
     col_res = call(
         col_kernel,
         (col_piece,) * blocks,
@@ -448,17 +452,24 @@
             pltpu.VMEM((members, tokens, LANES), BF16),
             pltpu.VMEM((LANES, 2 * span), BF16),
             pltpu.VMEM((2 * span, LANES), F32),
-            pltpu.VMEM((window, tokens), F32),
-            pltpu.VMEM((window, tokens), F32),
-            pltpu.VMEM((window, 2 * tokens), BF16),
+            pltpu.VMEM((2, window, tokens), F32),
+            pltpu.VMEM((2, window, tokens), F32),
+            pltpu.VMEM((2, window, 2 * tokens), BF16),
             sems((3,)),
         ),
         flops=members * 12 * window * tokens * LANES,
         specs=[SMEM, HBM, HBM],
     )
-    row_res, col_res, other_grads = lax.optimization_barrier((row_res, col_res, other_grads))
+    row_res, col_res, beside, beyond = lax.optimization_barrier(
+        (row_res, col_res, beside, beyond)
+    )
     row_back = swapped(row_res, row_axes)
-    col_back = [col_res[0], *to_members(col_res, range(1, blocks))]
+    col_back = to_members(col_res)
+    other_grads = [
+        beside,
+        beyond,
+        lax.ppermute(beyond, "d", [(i, i ^ 1) for i in range(clips)]),
+    ]
     share = width // clips
     piece = share // planes
     kept = piece // lines
@@ -512,20 +523,35 @@
             sems((2 * clips,)),
         ),
         flops=project,
-        vmem=ROOM,
         specs=[HBM] * (2 * clips),
     )
     lanes = kept * width // piece
+
+    def paired_off(pieces, axis, count):
+        return [pieces[0]] + [
+            lax.ppermute(pieces[hop], axis, [(i, i ^ hop) for i in range(count)])
+            for hop in range(1, count)
+        ]
+
     summed = call(
         plane_sum_kernel,
-        shape(clips * lines, piece, lanes),
-        (swapped(partial, plane_axes),),
+        (shape(piece, lanes),) * lines,
+        (line_index, swapped(partial, plane_axes)),
+        scratch=(pltpu.VMEM((lines, piece, lanes), F32),),
+        specs=[SMEM, VMEM],
     )
     factor = 1.0 / math.sqrt(clips * tokens * positions)
+    total = call(
+        functools.partial(line_sum_kernel, factor),
+        shape(piece, lanes, dtype=F32),
+        paired_off(summed, "z", lines),
+    )
     weight_grad = call(
-        functools.partial(line_sum_kernel, clips, factor),
+        gather_kernel,
         shape(kept * clips, width, dtype=F32),
-        (swapped(summed, line_axes),),
+        (clip_index, *paired_off([total] * clips, "d", clips)),
+        scratch=(pltpu.VMEM((clips, piece, lanes), F32),),
+        specs=[SMEM] + [VMEM] * clips,
     )
     whole = (1, tokens, width)
     return (

time: 128 us -> 126 us (0.984)
  starting transfers between devices: 68.3 us -> 74.9 us
  waiting for transfers between devices: 33.6 us -> 30 us
  Pallas kernels: 22.6 us -> 19.4 us
  local copies, waits for them, and re-layouts: 2.48 us -> 0.88 us
    ppermute x0 -> x7, starting transfers between devices: none -> 13.2 us  [the longest x6 12.6 us: paired_off(): lax.ppermute(pieces[hop], axis, [(i, i ^ hop) for i in range(count)])]
    all_to_all x4 -> x3, waiting for transfers between devices: 19.8 us -> 9.54 us  [swapped(): return lax.all_to_all(array, axes, split_axis=0, concat_axis=0, tiled=True)]
    all_to_all x4 -> x3, starting transfers between devices: 27.2 us -> 21.3 us  [swapped(): return lax.all_to_all(array, axes, split_axis=0, concat_axis=0, tiled=True)]
    ppermute x0 -> x7, waiting for transfers between devices: none -> 5.18 us  [the longest x6 5.18 us: paired_off(): lax.ppermute(pieces[hop], axis, [(i, i ^ hop) for i in range(count)])]
    pallas_call x10, Pallas kernels: 22.6 us -> 19.4 us  [call(): pl.pallas_call(kernel, out_shape=out_shape, in_specs=specs or [VMEM] * le...]
    ppermute x14, waiting for transfers between devices: 11.1 us -> 14.1 us  [to_members(): lax.ppermute(pieces[hop], 'b', [(i, i ^ hop) for i in range(blocks)])]
    ppermute x3, starting transfers between devices: 6.41 us -> 4.46 us  [on_device(): lax.ppermute(turned[hop], 'd', [(i, i ^ hop) for i in range(clips)])]
    unnamed x20 -> x4, local copies, waits for them, and re-layouts: 2.44 us -> 0.84 us
  transfers between devices with their start and end apart: 26 -> 31, of which waited for: 11 -> 11; matrix products, arithmetic and copies ran while one was open for 0% -> 0% of each run, Pallas kernels for 12% -> 11%
where the time goes in v4:
time: 126 us
  starting transfers between devices  74.9 us (59%)
  waiting for transfers between devices  30 us (24%)
  Pallas kernels  19.4 us (15%)
    ppermute x14, starting transfers between devices, to_members(): lax.ppermute(pieces[hop], 'b', [(i, i ^ hop) for i in range(blocks)])  26 us
    all_to_all x3, starting transfers between devices, swapped(): return lax.all_to_all(array, axes, split_axis=0, concat_axis=0, tiled=True)  21.3 us
    pallas_call x10, Pallas kernels, call(): pl.pallas_call(kernel, out_shape=out_shape, in_specs=specs or [VMEM] * le...  19.4 us
    ppermute x14, waiting for transfers between devices, to_members(): lax.ppermute(pieces[hop], 'b', [(i, i ^ hop) for i in range(blocks)])  14.1 us
    ppermute x6, starting transfers between devices, paired_off(): lax.ppermute(pieces[hop], axis, [(i, i ^ hop) for i in range(count)])  12.6 us
    all_to_all x3, waiting for transfers between devices, swapped(): return lax.all_to_all(array, axes, split_axis=0, concat_axis=0, tiled=True)  9.54 us
    ppermute x6, waiting for transfers between devices, paired_off(): lax.ppermute(pieces[hop], axis, [(i, i ^ hop) for i in range(count)])  5.18 us
    ppermute x3, starting transfers between devices, on_device(): lax.ppermute(turned[hop], 'd', [(i, i ^ hop) for i in range(clips)])  4.46 us
  transfers between devices with their start and end apart: 31, of which 11 were waited for; matrix products, arithmetic and copies ran while one was open for 0% of the time, Pallas kernels for 11%

profile of v4, /device:TPU:1, one launch (start us, length us, event | category | flops | bytes accessed | tf_op | source)
XLA Modules:
  0.0 126.0 jit_solution(17382900474877557862)
XLA Ops:
  0.6 3.7 %shard_map.92 = (bf16[8,256,128]{2,1,0:T(8,128)(2,1)}, bf16[32,1024]{1,0:T(8,128)(2,1)}, bf16[32,1024]{1,0:T(8,128)(2,1)}, bf16[32,1024]{1,0:T(8,128)(2,1)}, bf1...) custom-call(s32[1]{0:T(128)S(6)} %mul.3.flip_ref, ...), custom_call_target="tpu_custom_call" | custom-call | flops 268435456 | bytes 4194312 | tf_op jit(solution)/shard_map/pallas_call | solution.py:35
  4.4 10.0 %all-to-all-start = ((bf16[8,256,128]{2,1,0:T(8,128)(2,1)}), bf16[8,256,128]{2,1,0:T(8,128)(2,1)S(1)}, u32[]{:S(2)}, u32[]{:S(2)}) async-start(bf16[8,256,128]{2,1,0:T(8,128)(2,1)} %get-tuple-element.69), calls=%async_computation | async-start | bytes 1048576 | tf_op jit(solution)/shard_map/all_to_all | solution.py:372
  14.4 2.6 %collective-permute-start = (bf16[32,1024]{1,0:T(8,128)(2,1)}, bf16[32,1024]{1,0:T(8,128)(2,1)S(1)}, u32[]{:S(2)}, u32[]{:S(2)}) collective-permute-start(bf16[32,1024]{1,0:T(8,128)(2,1)} %get-tuple-element.71), channel_id=1, source_target_pairs={{0,8},{8,0},{16,24},{24,16},{32,40},{40,32},{48,56},{56,48},{1,9},... | collective-permute-start | bytes 196616 | tf_op jit(solution)/shard_map/ppermute | solution.py:414
  17.0 1.2 collective-permute-start.1
  18.3 0.3 collective-permute-start.2
  18.6 2.7 %collective-permute-start.3 = (bf16[32,1024]{1,0:T(8,128)(2,1)}, bf16[32,1024]{1,0:T(8,128)(2,1)S(1)}, u32[]{:S(2)}, u32[]{:S(2)}) collective-permute-start(bf16[32,1024]{1,0:T(8,128)(2,1)} %get-tuple-element.74), channel_id=1, source_target_pairs={{0,32},{8,40},{16,48},{24,56},{32,0},{40,8},{48,16},{56,24},{1,33}... | collective-permute-start | bytes 196616 | tf_op jit(solution)/shard_map/ppermute | solution.py:414
  21.3 2.6 %collective-permute-start.4 = (bf16[32,1024]{1,0:T(8,128)(2,1)}, bf16[32,1024]{1,0:T(8,128)(2,1)S(1)}, u32[]{:S(2)}, u32[]{:S(2)}) collective-permute-start(bf16[32,1024]{1,0:T(8,128)(2,1)} %get-tuple-element.75), channel_id=1, source_target_pairs={{0,40},{8,32},{16,56},{24,48},{32,8},{40,0},{48,24},{56,16},{1,41}... | collective-permute-start | bytes 196616 | tf_op jit(solution)/shard_map/ppermute | solution.py:414
  23.9 2.5 %collective-permute-start.5 = (bf16[32,1024]{1,0:T(8,128)(2,1)}, bf16[32,1024]{1,0:T(8,128)(2,1)S(1)}, u32[]{:S(2)}, u32[]{:S(2)}) collective-permute-start(bf16[32,1024]{1,0:T(8,128)(2,1)} %get-tuple-element.76), channel_id=1, source_target_pairs={{0,48},{8,56},{16,32},{24,40},{32,16},{40,24},{48,0},{56,8},{1,49}... | collective-permute-start | bytes 196616 | tf_op jit(solution)/shard_map/ppermute | solution.py:414
  26.4 0.3 collective-permute-start.6
  26.6 2.6 %collective-permute-done.4.rest_5_ = bf16[32,1024]{1,0:T(8,128)(2,1)S(1)} collective-permute-done((bf16[32,1024]{1,0:T(8,128)(2,1)}, bf16[32,1024]{1,0:T(8,128)(2,1)S(1)}, u32[]{:S(2)}, u32[]{:S(2)}) %collective-permute-start.4) | collective-permute-done | bytes 65568 | tf_op jit(solution)/shard_map/ppermute | solution.py:414
  29.3 0.1 collective-permute-done.5.rest_6_
  29.4 3.9 %collective-permute-done.6.rest_7_ = bf16[32,1024]{1,0:T(8,128)(2,1)S(1)} collective-permute-done((bf16[32,1024]{1,0:T(8,128)(2,1)}, bf16[32,1024]{1,0:T(8,128)(2,1)S(1)}, u32[]{:S(2)}, u32[]{:S(2)}) %collective-permute-start.6) | collective-permute-done | bytes 65568 | tf_op jit(solution)/shard_map/ppermute | solution.py:414
  33.3 4.3 %collective-permute-start.7 = (bf16[8,128,128]{2,1,0:T(8,128)(2,1)S(1)}, bf16[8,128,128]{2,1,0:T(8,128)(2,1)S(1)}, u32[]{:S(2)}, u32[]{:S(2)}) collective-permute-start(bf16[8,128,128]{2,1,0:T(8,128)(2,1)S(1)} %slice.6), channel_id=1, source_target_pairs={{0,12},{4,8},{8,20},{12,16},{16,28},{20,24},{24,36},{28,32},{32,44... | collective-permute-start | bytes 786440 | tf_op jit(solution)/shard_map/ppermute | solution.py:419
  37.6 1.0 collective-permute-start.9
  38.6 3.3 %collective-permute-start.8 = (bf16[128,1024]{1,0:T(8,128)(2,1)S(1)}, bf16[128,1024]{1,0:T(8,128)(2,1)S(1)}, u32[]{:S(2)}, u32[]{:S(2)}) collective-permute-start(bf16[128,1024]{1,0:T(8,128)(2,1)S(1)} %bitcast.13), channel_id=1, source_target_pairs={{0,64},{64,0},{128,192},{192,128},{1,65},{65,1},{129,193},{193,129... | collective-permute-start | bytes 786440 | tf_op jit(solution)/shard_map/ppermute | solution.py:429
  42.0 0.8 copy-done.1
  42.8 1.6 %shard_map.93 = (bf16[32,1024]{1,0:T(8,128)(2,1)S(1)}, bf16[32,1024]{1,0:T(8,128)(2,1)S(1)}, bf16[32,1024]{1,0:T(8,128)(2,1)S(1)}, bf16[32,1024]{1,0:T(8,128)(2,...) custom-call(s32[1]{0:T(128)} %bitcast.me_ref.first_ref.block_ref, ...), custom_call_target="tpu_custom_call" | custom-call | flops 201326592 | bytes 1048580 | tf_op jit(solution)/shard_map/pallas_call | solution.py:35
  44.4 6.7 %shard_map.94 = bf16[8,384,128]{2,1,0:T(8,128)(2,1)} custom-call(s32[1]{0:T(128)} %bitcast.me_ref.first_ref.block_ref, bf16[8,256,128]{2,1,0:T(8,128)(2,1)S(1)} %all-to-all-done.in_hbm, bf16[8,128,128]{2,1,0:T(8,128)(2,1)S(1)} %collective-permute-done.7.prev_hbm), custom_call_target="tpu_custom_call" | custom-call | flops 1811939328 | bytes 1572868 | tf_op jit(solution)/shard_map/pallas_call | solution.py:35
  51.1 6.4 %all-to-all-start.1 = ((bf16[8,384,128]{2,1,0:T(8,128)(2,1)}), bf16[8,384,128]{2,1,0:T(8,128)(2,1)S(1)}, u32[]{:S(2)}, u32[]{:S(2)}) async-start(bf16[8,384,128]{2,1,0:T(8,128)(2,1)} %shard_map.94), calls=%async_computation.1 | async-start | bytes 1572864 | tf_op jit(solution)/shard_map/all_to_all | solution.py:372
  57.5 0.6 collective-permute-start.21
  58.1 4.3 %collective-permute-start.10 = (bf16[32,1024]{1,0:T(8,128)(2,1)S(1)}, bf16[32,1024]{1,0:T(8,128)(2,1)S(1)}, u32[]{:S(2)}, u32[]{:S(2)}) collective-permute-start(bf16[32,1024]{1,0:T(8,128)(2,1)S(1)} %get-tuple-element.107), channel_id=1, source_target_pairs={{0,8},{8,0},{16,24},{24,16},{32,40},{40,32},{48,56},{56,48},{1,9},... | collective-permute-start | bytes 196616 | tf_op jit(solution)/shard_map/ppermute | solution.py:414
  62.4 1.2 collective-permute-start.12
  63.6 1.9 %collective-permute-start.13 = (bf16[32,1024]{1,0:T(8,128)(2,1)S(1)}, bf16[32,1024]{1,0:T(8,128)(2,1)S(1)}, u32[]{:S(2)}, u32[]{:S(2)}) collective-permute-start(bf16[32,1024]{1,0:T(8,128)(2,1)S(1)} %get-tuple-element.110), channel_id=1, source_target_pairs={{0,32},{8,40},{16,48},{24,56},{32,0},{40,8},{48,16},{56,24},{1,33}... | collective-permute-start | bytes 196616 | tf_op jit(solution)/shard_map/ppermute | solution.py:414
  65.6 3.7 %collective-permute-start.14 = (bf16[32,1024]{1,0:T(8,128)(2,1)S(1)}, bf16[32,1024]{1,0:T(8,128)(2,1)S(1)}, u32[]{:S(2)}, u32[]{:S(2)}) collective-permute-start(bf16[32,1024]{1,0:T(8,128)(2,1)S(1)} %get-tuple-element.111), channel_id=1, source_target_pairs={{0,40},{8,32},{16,56},{24,48},{32,8},{40,0},{48,24},{56,16},{1,41}... | collective-permute-start | bytes 196616 | tf_op jit(solution)/shard_map/ppermute | solution.py:414
  69.3 2.1 %collective-permute-start.15 = (bf16[32,1024]{1,0:T(8,128)(2,1)S(1)}, bf16[32,1024]{1,0:T(8,128)(2,1)S(1)}, u32[]{:S(2)}, u32[]{:S(2)}) collective-permute-start(bf16[32,1024]{1,0:T(8,128)(2,1)S(1)} %get-tuple-element.112), channel_id=1, source_target_pairs={{0,48},{8,56},{16,32},{24,40},{32,16},{40,24},{48,0},{56,8},{1,49}... | collective-permute-start | bytes 196616 | tf_op jit(solution)/shard_map/ppermute | solution.py:414
  71.4 0.5 collective-permute-start.16
  71.9 1.3 %collective-permute-done.14.rest_5_ = bf16[32,1024]{1,0:T(8,128)(2,1)S(1)} collective-permute-done((bf16[32,1024]{1,0:T(8,128)(2,1)S(1)}, bf16[32,1024]{1,0:T(8,128)(2,1)S(1)}, u32[]{:S(2)}, u32[]{:S(2)}) %collective-permute-start.14) | collective-permute-done | bytes 65568 | tf_op jit(solution)/shard_map/ppermute | solution.py:414
  73.2 1.0 collective-permute-done.15.rest_6_
  74.2 5.1 %collective-permute-done.16.rest_7_ = bf16[32,1024]{1,0:T(8,128)(2,1)S(1)} collective-permute-done((bf16[32,1024]{1,0:T(8,128)(2,1)S(1)}, bf16[32,1024]{1,0:T(8,128)(2,1)S(1)}, u32[]{:S(2)}, u32[]{:S(2)}) %collective-permute-start.16) | collective-permute-done | bytes 65568 | tf_op jit(solution)/shard_map/ppermute | solution.py:414
  79.3 0.9 shard_map.95
  80.2 2.2 %collective-permute-start.17 = (bf16[256,128]{1,0:T(8,128)(2,1)S(1)}, bf16[256,128]{1,0:T(8,128)(2,1)S(1)}, u32[]{:S(2)}, u32[]{:S(2)}) collective-permute-start(bf16[256,128]{1,0:T(8,128)(2,1)S(1)} %get-tuple-element.115), channel_id=1, source_target_pairs={{0,64},{64,0},{128,192},{192,128},{1,65},{65,1},{129,193},{193,129... | collective-permute-start | bytes 196616 | tf_op jit(solution)/shard_map/ppermute | solution.py:485
  82.4 2.2 %collective-permute-start.18 = (bf16[256,128]{1,0:T(8,128)(2,1)S(1)}, bf16[256,128]{1,0:T(8,128)(2,1)S(1)}, u32[]{:S(2)}, u32[]{:S(2)}) collective-permute-start(bf16[256,128]{1,0:T(8,128)(2,1)S(1)} %get-tuple-element.116), channel_id=1, source_target_pairs={{0,128},{64,192},{128,0},{192,64},{1,129},{65,193},{129,1},{193,65... | collective-permute-start | bytes 196616 | tf_op jit(solution)/shard_map/ppermute | solution.py:485
  84.7 2.8 %shard_map.96 = (bf16[128,1024]{1,0:T(8,128)(2,1)}, bf16[128,1024]{1,0:T(8,128)(2,1)}) custom-call(s32[1]{0:T(128)S(6)} %mul.3.flip_ref, s32[1]{0:T(128)} %bitcast.me_ref.first_ref.block_ref, bf16[1024,1024]{1,0:T(8,128)(2,1)} %w_hbm.3, bf16[8,384,128]{2,1,0:T(8,128)(2,1)S(1)} %all-to-all-done.1.row_hbm, bf16[32,1024]{1,0:T(8,128)(2,1)S(1)} %get-tuple-element.106.rest_0_, ...), custom_call_target="tpu_custom_call" | custom-call | flops 268435456 | bytes 3932168 | tf_op jit(solution)/shard_map/pallas_call | solution.py:35
  87.5 1.1 collective-permute-done.19.refs_3_
  88.7 1.4 %shard_map.98 = bf16[16,16,1024]{2,1,0:T(8,128)(2,1)} custom-call(bf16[256,128]{1,0:T(8,128)(2,1)S(1)} %get-tuple-element.123.refs_0_, bf16[256,128]{1,0:T(8,128)(2,1)S(1)} %collective-permute-done.17.refs_1_, bf16[256,128]{1,0:T(8,128)(2,1)S(1)} %collective-permute-done.18.refs_2_, bf16[256,128]{1,0:T(8,128)(2,1)S(1)} %collective-permute-done.19.refs_3_, ...), custom_call_target="tpu_custom_call" | custom-call | flops 268435456 | bytes 1835008 | tf_op jit(solution)/shard_map/pallas_call | solution.py:35
  90.1 4.9 %all-to-all-start.2 = ((bf16[16,16,1024]{2,1,0:T(8,128)(2,1)}), bf16[16,16,1024]{2,1,0:T(8,128)(2,1)S(1)}, u32[]{:S(2)}, u32[]{:S(2)}) async-start(bf16[16,16,1024]{2,1,0:T(8,128)(2,1)} %shard_map.98), calls=%async_computation.2 | async-start | bytes 1048576 | tf_op jit(solution)/shard_map/all_to_all | solution.py:372
  95.0 1.3 %collective-permute-start.20 = (bf16[8,128,128]{2,1,0:T(8,128)(2,1)S(1)}, bf16[8,128,128]{2,1,0:T(8,128)(2,1)S(1)}, u32[]{:S(2)}, u32[]{:S(2)}) collective-permute-start(bf16[8,128,128]{2,1,0:T(8,128)(2,1)S(1)} %slice.8), channel_id=1, source_target_pairs={{8,0},{16,8},{24,16},{32,24},{40,32},{48,40},{56,48},{9,1},{17,9},... | collective-permute-start | bytes 786440 | tf_op jit(solution)/shard_map/ppermute | solution.py:488
  96.3 9.5 %all-to-all-done.2.in_ref = bf16[16,16,1024]{2,1,0:T(8,128)(2,1)S(1)} async-done(((bf16[16,16,1024]{2,1,0:T(8,128)(2,1)}), bf16[16,16,1024]{2,1,0:T(8,128)(2,1)S(1)}, u32[]{:S(2)}, u32[]{:S(2)}) %all-to-all-start.2) | async-done | bytes 524320 | tf_op jit(solution)/shard_map/all_to_all | solution.py:372
  105.9 1.3 %collective-permute-start.22 = (bf16[16,256]{1,0:T(8,128)(2,1)S(1)}, bf16[16,256]{1,0:T(8,128)(2,1)S(1)}, u32[]{:S(2)}, u32[]{:S(2)}) collective-permute-start(bf16[16,256]{1,0:T(8,128)(2,1)S(1)} %get-tuple-element.130), channel_id=1, source_target_pairs={{0,1},{1,0},{2,3},{3,2},{4,5},{5,4},{6,7},{7,6},{8,9},{9,8},{10,11... | collective-permute-start | bytes 24584 | tf_op jit(solution)/shard_map/ppermute | solution.py:532
  107.2 6.3 %collective-permute-start.23 = (bf16[16,256]{1,0:T(8,128)(2,1)S(1)}, bf16[16,256]{1,0:T(8,128)(2,1)S(1)}, u32[]{:S(2)}, u32[]{:S(2)}) collective-permute-start(bf16[16,256]{1,0:T(8,128)(2,1)S(1)} %get-tuple-element.131), channel_id=1, source_target_pairs={{0,2},{1,3},{2,0},{3,1},{4,6},{5,7},{6,4},{7,5},{8,10},{9,11},{10,... | collective-permute-start | bytes 24584 | tf_op jit(solution)/shard_map/ppermute | solution.py:532
  113.6 1.1 collective-permute-done.23.refs_2_
  114.7 3.5 %collective-permute-done.24.refs_3_ = bf16[16,256]{1,0:T(8,128)(2,1)S(1)} collective-permute-done((bf16[16,256]{1,0:T(8,128)(2,1)S(1)}, bf16[16,256]{1,0:T(8,128)(2,1)S(1)}, u32[]{:S(2)}, u32[]{:S(2)}) %collective-permute-start.24) | collective-permute-done | bytes 8224 | tf_op jit(solution)/shard_map/ppermute | solution.py:532
  118.2 4.5 %collective-permute-start.27 = (f32[16,256]{1,0:T(8,128)S(1)}, f32[16,256]{1,0:T(8,128)S(1)}, u32[]{:S(2)}, u32[]{:S(2)}) collective-permute-start(f32[16,256]{1,0:T(8,128)S(1)} %shard_map.100.rest_0_), channel_id=1, source_target_pairs={{0,192},{64,128},{128,64},{192,0},{1,193},{65,129},{129,65},{193,1... | collective-permute-start | bytes 49160 | tf_op jit(solution)/shard_map/ppermute | solution.py:532
  122.7 0.4 collective-permute-start.26
  123.1 0.1 collective-permute-start.25
  123.2 1.5 %shard_map.97 = (bf16[128,1024]{1,0:T(8,128)(2,1)}, bf16[128,1024]{1,0:T(8,128)(2,1)}) custom-call(s32[1]{0:T(128)S(6)} %mul.3.flip_ref, s32[1]{0:T(128)} %bitcast.me_ref.first_ref.block_ref, bf16[8,128,128]{2,1,0:T(8,128)(2,1)S(1)} %collective-permute-done.20.later_hbm, bf16[8,384,128]{2,1,0:T(8,128)(2,1)S(1)} %all-to-all-done.1.row_hbm, ...), custom_call_target="tpu_custom_call" | custom-call | bytes 2097160 | tf_op jit(solution)/shard_map/pallas_call | solution.py:35
  124.7 0.6 collective-permute-done.26.rest_2_
  125.3 0.7 shard_map.101
  (30 shorter events, 0.3 us)
Async XLA Ops:
  0.6 37.0 %copy-start = (bf16[1,128,1024]{2,1,0:T(8,128)(2,1)S(1)}, bf16[1,128,1024]{2,1,0:T(8,128)(2,1)}, u32[]{:S(2)}) copy-start(bf16[1,128,1024]{2,1,0:T(8,128)(2,1)} %param.8) | copy-start | bytes 786436
  4.4 28.9 %all-to-all-start = ((bf16[8,256,128]{2,1,0:T(8,128)(2,1)}), bf16[8,256,128]{2,1,0:T(8,128)(2,1)S(1)}, u32[]{:S(2)}, u32[]{:S(2)}) async-start(bf16[8,256,128]{2,1,0:T(8,128)(2,1)} %get-tuple-element.69), calls=%async_computation | async-start | bytes 1048576 | tf_op jit(solution)/shard_map/all_to_all | solution.py:372
  14.4 9.5 %collective-permute-start = (bf16[32,1024]{1,0:T(8,128)(2,1)}, bf16[32,1024]{1,0:T(8,128)(2,1)S(1)}, u32[]{:S(2)}, u32[]{:S(2)}) collective-permute-start(bf16[32,1024]{1,0:T(8,128)(2,1)} %get-tuple-element.71), channel_id=1, source_target_pairs={{0,8},{8,0},{16,24},{24,16},{32,40},{40,32},{48,56},{56,48},{1,9},... | collective-permute-start | bytes 196616 | tf_op jit(solution)/shard_map/ppermute | solution.py:414
  17.0 9.3 %collective-permute-start.1 = (bf16[32,1024]{1,0:T(8,128)(2,1)}, bf16[32,1024]{1,0:T(8,128)(2,1)S(1)}, u32[]{:S(2)}, u32[]{:S(2)}) collective-permute-start(bf16[32,1024]{1,0:T(8,128)(2,1)} %get-tuple-element.72), channel_id=1, source_target_pairs={{0,16},{8,24},{16,0},{24,8},{32,48},{40,56},{48,32},{56,40},{1,17}... | collective-permute-start | bytes 196616 | tf_op jit(solution)/shard_map/ppermute | solution.py:414
  18.3 8.4 %collective-permute-start.2 = (bf16[32,1024]{1,0:T(8,128)(2,1)}, bf16[32,1024]{1,0:T(8,128)(2,1)S(1)}, u32[]{:S(2)}, u32[]{:S(2)}) collective-permute-start(bf16[32,1024]{1,0:T(8,128)(2,1)} %get-tuple-element.73), channel_id=1, source_target_pairs={{0,24},{8,16},{16,8},{24,0},{32,56},{40,48},{48,40},{56,32},{1,25}... | collective-permute-start | bytes 196616 | tf_op jit(solution)/shard_map/ppermute | solution.py:414
  18.6 8.1 %collective-permute-start.3 = (bf16[32,1024]{1,0:T(8,128)(2,1)}, bf16[32,1024]{1,0:T(8,128)(2,1)S(1)}, u32[]{:S(2)}, u32[]{:S(2)}) collective-permute-start(bf16[32,1024]{1,0:T(8,128)(2,1)} %get-tuple-element.74), channel_id=1, source_target_pairs={{0,32},{8,40},{16,48},{24,56},{32,0},{40,8},{48,16},{56,24},{1,33}... | collective-permute-start | bytes 196616 | tf_op jit(solution)/shard_map/ppermute | solution.py:414
  21.3 8.0 %collective-permute-start.4 = (bf16[32,1024]{1,0:T(8,128)(2,1)}, bf16[32,1024]{1,0:T(8,128)(2,1)S(1)}, u32[]{:S(2)}, u32[]{:S(2)}) collective-permute-start(bf16[32,1024]{1,0:T(8,128)(2,1)} %get-tuple-element.75), channel_id=1, source_target_pairs={{0,40},{8,32},{16,56},{24,48},{32,8},{40,0},{48,24},{56,16},{1,41}... | collective-permute-start | bytes 196616 | tf_op jit(solution)/shard_map/ppermute | solution.py:414
  23.9 5.5 %collective-permute-start.5 = (bf16[32,1024]{1,0:T(8,128)(2,1)}, bf16[32,1024]{1,0:T(8,128)(2,1)S(1)}, u32[]{:S(2)}, u32[]{:S(2)}) collective-permute-start(bf16[32,1024]{1,0:T(8,128)(2,1)} %get-tuple-element.76), channel_id=1, source_target_pairs={{0,48},{8,56},{16,32},{24,40},{32,16},{40,24},{48,0},{56,8},{1,49}... | collective-permute-start | bytes 196616 | tf_op jit(solution)/shard_map/ppermute | solution.py:414
  26.4 6.9 %collective-permute-start.6 = (bf16[32,1024]{1,0:T(8,128)(2,1)}, bf16[32,1024]{1,0:T(8,128)(2,1)S(1)}, u32[]{:S(2)}, u32[]{:S(2)}) collective-permute-start(bf16[32,1024]{1,0:T(8,128)(2,1)} %get-tuple-element.77), channel_id=1, source_target_pairs={{0,56},{8,48},{16,40},{24,32},{32,24},{40,16},{48,8},{56,0},{1,57}... | collective-permute-start | bytes 196616 | tf_op jit(solution)/shard_map/ppermute | solution.py:414
  33.3 11.0 %collective-permute-start.7 = (bf16[8,128,128]{2,1,0:T(8,128)(2,1)S(1)}, bf16[8,128,128]{2,1,0:T(8,128)(2,1)S(1)}, u32[]{:S(2)}, u32[]{:S(2)}) collective-permute-start(bf16[8,128,128]{2,1,0:T(8,128)(2,1)S(1)} %slice.6), channel_id=1, source_target_pairs={{0,12},{4,8},{8,20},{12,16},{16,28},{20,24},{24,36},{28,32},{32,44... | collective-permute-start | bytes 786440 | tf_op jit(solution)/shard_map/ppermute | solution.py:419
  37.6 13.5 %collective-permute-start.9 = (bf16[128,1024]{1,0:T(8,128)(2,1)S(1)}, bf16[128,1024]{1,0:T(8,128)(2,1)S(1)}, u32[]{:S(2)}, u32[]{:S(2)}) collective-permute-start(bf16[128,1024]{1,0:T(8,128)(2,1)S(1)} %bitcast.12), channel_id=1, source_target_pairs={{0,128},{64,192},{128,0},{192,64},{1,129},{65,193},{129,1},{193,65... | collective-permute-start | bytes 786440 | tf_op jit(solution)/shard_map/ppermute | solution.py:429
  38.6 12.5 %collective-permute-start.8 = (bf16[128,1024]{1,0:T(8,128)(2,1)S(1)}, bf16[128,1024]{1,0:T(8,128)(2,1)S(1)}, u32[]{:S(2)}, u32[]{:S(2)}) collective-permute-start(bf16[128,1024]{1,0:T(8,128)(2,1)S(1)} %bitcast.13), channel_id=1, source_target_pairs={{0,64},{64,0},{128,192},{192,128},{1,65},{65,1},{129,193},{193,129... | collective-permute-start | bytes 786440 | tf_op jit(solution)/shard_map/ppermute | solution.py:429
  42.0 0.8 copy-start.1
  51.1 28.2 %all-to-all-start.1 = ((bf16[8,384,128]{2,1,0:T(8,128)(2,1)}), bf16[8,384,128]{2,1,0:T(8,128)(2,1)S(1)}, u32[]{:S(2)}, u32[]{:S(2)}) async-start(bf16[8,384,128]{2,1,0:T(8,128)(2,1)} %shard_map.94), calls=%async_computation.1 | async-start | bytes 1572864 | tf_op jit(solution)/shard_map/all_to_all | solution.py:372
  57.5 31.2 %collective-permute-start.21 = (bf16[128,1024]{1,0:T(8,128)(2,1)S(1)}, bf16[128,1024]{1,0:T(8,128)(2,1)S(1)}, u32[]{:S(2)}, u32[]{:S(2)}) collective-permute-start(bf16[128,1024]{1,0:T(8,128)(2,1)S(1)} %collective-permute-done.9.refs_6_), channel_id=1, source_target_pairs={{0,64},{64,0},{128,192},{192,128},{1,65},{65,1},{129,193},{193,129... | collective-permute-start | bytes 786440 | tf_op jit(solution)/shard_map/ppermute | solution.py:471
  58.1 7.4 %collective-permute-start.10 = (bf16[32,1024]{1,0:T(8,128)(2,1)S(1)}, bf16[32,1024]{1,0:T(8,128)(2,1)S(1)}, u32[]{:S(2)}, u32[]{:S(2)}) collective-permute-start(bf16[32,1024]{1,0:T(8,128)(2,1)S(1)} %get-tuple-element.107), channel_id=1, source_target_pairs={{0,8},{8,0},{16,24},{24,16},{32,40},{40,32},{48,56},{56,48},{1,9},... | collective-permute-start | bytes 196616 | tf_op jit(solution)/shard_map/ppermute | solution.py:414
  62.4 6.8 %collective-permute-start.11 = (bf16[32,1024]{1,0:T(8,128)(2,1)S(1)}, bf16[32,1024]{1,0:T(8,128)(2,1)S(1)}, u32[]{:S(2)}, u32[]{:S(2)}) collective-permute-start(bf16[32,1024]{1,0:T(8,128)(2,1)S(1)} %get-tuple-element.108), channel_id=1, source_target_pairs={{0,16},{8,24},{16,0},{24,8},{32,48},{40,56},{48,32},{56,40},{1,17}... | collective-permute-start | bytes 196616 | tf_op jit(solution)/shard_map/ppermute | solution.py:414
  62.4 9.0 %collective-permute-start.12 = (bf16[32,1024]{1,0:T(8,128)(2,1)S(1)}, bf16[32,1024]{1,0:T(8,128)(2,1)S(1)}, u32[]{:S(2)}, u32[]{:S(2)}) collective-permute-start(bf16[32,1024]{1,0:T(8,128)(2,1)S(1)} %get-tuple-element.109), channel_id=1, source_target_pairs={{0,24},{8,16},{16,8},{24,0},{32,56},{40,48},{48,40},{56,32},{1,25}... | collective-permute-start | bytes 196616 | tf_op jit(solution)/shard_map/ppermute | solution.py:414
  63.6 8.3 %collective-permute-start.13 = (bf16[32,1024]{1,0:T(8,128)(2,1)S(1)}, bf16[32,1024]{1,0:T(8,128)(2,1)S(1)}, u32[]{:S(2)}, u32[]{:S(2)}) collective-permute-start(bf16[32,1024]{1,0:T(8,128)(2,1)S(1)} %get-tuple-element.110), channel_id=1, source_target_pairs={{0,32},{8,40},{16,48},{24,56},{32,0},{40,8},{48,16},{56,24},{1,33}... | collective-permute-start | bytes 196616 | tf_op jit(solution)/shard_map/ppermute | solution.py:414
  65.6 7.6 %collective-permute-start.14 = (bf16[32,1024]{1,0:T(8,128)(2,1)S(1)}, bf16[32,1024]{1,0:T(8,128)(2,1)S(1)}, u32[]{:S(2)}, u32[]{:S(2)}) collective-permute-start(bf16[32,1024]{1,0:T(8,128)(2,1)S(1)} %get-tuple-element.111), channel_id=1, source_target_pairs={{0,40},{8,32},{16,56},{24,48},{32,8},{40,0},{48,24},{56,16},{1,41}... | collective-permute-start | bytes 196616 | tf_op jit(solution)/shard_map/ppermute | solution.py:414
  69.3 5.0 %collective-permute-start.15 = (bf16[32,1024]{1,0:T(8,128)(2,1)S(1)}, bf16[32,1024]{1,0:T(8,128)(2,1)S(1)}, u32[]{:S(2)}, u32[]{:S(2)}) collective-permute-start(bf16[32,1024]{1,0:T(8,128)(2,1)S(1)} %get-tuple-element.112), channel_id=1, source_target_pairs={{0,48},{8,56},{16,32},{24,40},{32,16},{40,24},{48,0},{56,8},{1,49}... | collective-permute-start | bytes 196616 | tf_op jit(solution)/shard_map/ppermute | solution.py:414
  71.4 7.9 %collective-permute-start.16 = (bf16[32,1024]{1,0:T(8,128)(2,1)S(1)}, bf16[32,1024]{1,0:T(8,128)(2,1)S(1)}, u32[]{:S(2)}, u32[]{:S(2)}) collective-permute-start(bf16[32,1024]{1,0:T(8,128)(2,1)S(1)} %get-tuple-element.113), channel_id=1, source_target_pairs={{0,56},{8,48},{16,40},{24,32},{32,24},{40,16},{48,8},{56,0},{1,57}... | collective-permute-start | bytes 196616 | tf_op jit(solution)/shard_map/ppermute | solution.py:414
  80.2 7.3 %collective-permute-start.17 = (bf16[256,128]{1,0:T(8,128)(2,1)S(1)}, bf16[256,128]{1,0:T(8,128)(2,1)S(1)}, u32[]{:S(2)}, u32[]{:S(2)}) collective-permute-start(bf16[256,128]{1,0:T(8,128)(2,1)S(1)} %get-tuple-element.115), channel_id=1, source_target_pairs={{0,64},{64,0},{128,192},{192,128},{1,65},{65,1},{129,193},{193,129... | collective-permute-start | bytes 196616 | tf_op jit(solution)/shard_map/ppermute | solution.py:485
  82.4 5.1 %collective-permute-start.18 = (bf16[256,128]{1,0:T(8,128)(2,1)S(1)}, bf16[256,128]{1,0:T(8,128)(2,1)S(1)}, u32[]{:S(2)}, u32[]{:S(2)}) collective-permute-start(bf16[256,128]{1,0:T(8,128)(2,1)S(1)} %get-tuple-element.116), channel_id=1, source_target_pairs={{0,128},{64,192},{128,0},{192,64},{1,129},{65,193},{129,1},{193,65... | collective-permute-start | bytes 196616 | tf_op jit(solution)/shard_map/ppermute | solution.py:485
  84.6 4.1 %collective-permute-start.19 = (bf16[256,128]{1,0:T(8,128)(2,1)S(1)}, bf16[256,128]{1,0:T(8,128)(2,1)S(1)}, u32[]{:S(2)}, u32[]{:S(2)}) collective-permute-start(bf16[256,128]{1,0:T(8,128)(2,1)S(1)} %get-tuple-element.117), channel_id=1, source_target_pairs={{0,192},{64,128},{128,64},{192,0},{1,193},{65,129},{129,65},{193,1... | collective-permute-start | bytes 196616 | tf_op jit(solution)/shard_map/ppermute | solution.py:485
  90.1 15.8 %all-to-all-start.2 = ((bf16[16,16,1024]{2,1,0:T(8,128)(2,1)}), bf16[16,16,1024]{2,1,0:T(8,128)(2,1)S(1)}, u32[]{:S(2)}, u32[]{:S(2)}) async-start(bf16[16,16,1024]{2,1,0:T(8,128)(2,1)} %shard_map.98), calls=%async_computation.2 | async-start | bytes 1048576 | tf_op jit(solution)/shard_map/all_to_all | solution.py:372
  95.0 28.2 %collective-permute-start.20 = (bf16[8,128,128]{2,1,0:T(8,128)(2,1)S(1)}, bf16[8,128,128]{2,1,0:T(8,128)(2,1)S(1)}, u32[]{:S(2)}, u32[]{:S(2)}) collective-permute-start(bf16[8,128,128]{2,1,0:T(8,128)(2,1)S(1)} %slice.8), channel_id=1, source_target_pairs={{8,0},{16,8},{24,16},{32,24},{40,32},{48,40},{56,48},{9,1},{17,9},... | collective-permute-start | bytes 786440 | tf_op jit(solution)/shard_map/ppermute | solution.py:488
  105.9 7.6 %collective-permute-start.22 = (bf16[16,256]{1,0:T(8,128)(2,1)S(1)}, bf16[16,256]{1,0:T(8,128)(2,1)S(1)}, u32[]{:S(2)}, u32[]{:S(2)}) collective-permute-start(bf16[16,256]{1,0:T(8,128)(2,1)S(1)} %get-tuple-element.130), channel_id=1, source_target_pairs={{0,1},{1,0},{2,3},{3,2},{4,5},{5,4},{6,7},{7,6},{8,9},{9,8},{10,11... | collective-permute-start | bytes 24584 | tf_op jit(solution)/shard_map/ppermute | solution.py:532
  107.2 7.5 %collective-permute-start.23 = (bf16[16,256]{1,0:T(8,128)(2,1)S(1)}, bf16[16,256]{1,0:T(8,128)(2,1)S(1)}, u32[]{:S(2)}, u32[]{:S(2)}) collective-permute-start(bf16[16,256]{1,0:T(8,128)(2,1)S(1)} %get-tuple-element.131), channel_id=1, source_target_pairs={{0,2},{1,3},{2,0},{3,1},{4,6},{5,7},{6,4},{7,5},{8,10},{9,11},{10,... | collective-permute-start | bytes 24584 | tf_op jit(solution)/shard_map/ppermute | solution.py:532
  113.6 4.6 %collective-permute-start.24 = (bf16[16,256]{1,0:T(8,128)(2,1)S(1)}, bf16[16,256]{1,0:T(8,128)(2,1)S(1)}, u32[]{:S(2)}, u32[]{:S(2)}) collective-permute-start(bf16[16,256]{1,0:T(8,128)(2,1)S(1)} %get-tuple-element.132), channel_id=1, source_target_pairs={{0,3},{1,2},{2,1},{3,0},{4,7},{5,6},{6,5},{7,4},{8,11},{9,10},{10,... | collective-permute-start | bytes 24584 | tf_op jit(solution)/shard_map/ppermute | solution.py:532
  118.2 6.5 %collective-permute-start.27 = (f32[16,256]{1,0:T(8,128)S(1)}, f32[16,256]{1,0:T(8,128)S(1)}, u32[]{:S(2)}, u32[]{:S(2)}) collective-permute-start(f32[16,256]{1,0:T(8,128)S(1)} %shard_map.100.rest_0_), channel_id=1, source_target_pairs={{0,192},{64,128},{128,64},{192,0},{1,193},{65,129},{129,65},{193,1... | collective-permute-start | bytes 49160 | tf_op jit(solution)/shard_map/ppermute | solution.py:532
  122.7 2.6 %collective-permute-start.26 = (f32[16,256]{1,0:T(8,128)S(1)}, f32[16,256]{1,0:T(8,128)S(1)}, u32[]{:S(2)}, u32[]{:S(2)}) collective-permute-start(f32[16,256]{1,0:T(8,128)S(1)} %shard_map.100.rest_0_), channel_id=1, source_target_pairs={{0,128},{64,192},{128,0},{192,64},{1,129},{65,193},{129,1},{193,65... | collective-permute-start | bytes 49160 | tf_op jit(solution)/shard_map/ppermute | solution.py:532
  123.1 2.2 %collective-permute-start.25 = (f32[16,256]{1,0:T(8,128)S(1)}, f32[16,256]{1,0:T(8,128)S(1)}, u32[]{:S(2)}, u32[]{:S(2)}) collective-permute-start(f32[16,256]{1,0:T(8,128)S(1)} %shard_map.100.rest_0_), channel_id=1, source_target_pairs={{0,64},{64,0},{128,192},{192,128},{1,65},{65,1},{129,193},{193,129... | collective-permute-start | bytes 49160 | tf_op jit(solution)/shard_map/ppermute | solution.py:532

commit v5 on v4

--- a/solution.py
+++ b/solution.py
@@ -15,6 +15,7 @@
 BF16 = jnp.bfloat16
 F32 = jnp.float32
 ROOM = 60 << 20
+FAR_FIRST = (5, 3, 7, 1, 4, 2, 6, 0)
 SCALE = 1.0 / math.sqrt(DH)
 SCALE_LOG2 = SCALE / math.log(2.0)
 NT = (((1,), (1,)), ((), ()))
@@ -408,13 +409,19 @@
     )
     row_got = swapped(row_in, row_axes)
 
+    def tied(first, second, pieces):
+        first, second, *moved = lax.optimization_barrier(
+            (first, second, *(pieces[hop] for hop in FAR_FIRST))
+        )
+        return first, second, [moved[FAR_FIRST.index(hop)] for hop in range(blocks)]
+
     def to_members(pieces):
         got = dict(enumerate(pieces))
         for hop in range(1, blocks):
             got[hop] = lax.ppermute(pieces[hop], "b", [(i, i ^ hop) for i in range(blocks)])
         return [got[hop] for hop in range(blocks)]
 
-    row_got, og_later, *col_got = lax.optimization_barrier((row_got, og, *to_members(col_in)))
+    row_got, og_later, col_got = tied(row_got, og, to_members(col_in))
     onward = [(i * yl + j, (i + 1) * yl + j ^ 1) for i in range(blocks - 1) for j in range(yl)]
     prev = lax.ppermute(row_got[:, :tokens], ("b", "yl"), onward)
     col_res = call(
@@ -464,12 +471,7 @@
         (row_res, col_res, beside, beyond)
     )
     row_back = swapped(row_res, row_axes)
-    col_back = to_members(col_res)
-    other_grads = [
-        beside,
-        beyond,
-        lax.ppermute(beyond, "d", [(i, i ^ 1) for i in range(clips)]),
-    ]
+    row_back, _, col_back = tied(row_back, og, to_members(col_res))
     share = width // clips
     piece = share // planes
     kept = piece // lines
@@ -481,6 +483,12 @@
         scratch=(*packed, pltpu.VMEM((width, tokens), F32), sems((blocks + 1,))),
         specs=[SMEM] * 3 + [HBM] * (blocks + 1),
     )
+    turned, beyond = lax.optimization_barrier((turned, beyond))
+    other_grads = [
+        beside,
+        beyond,
+        lax.ppermute(beyond, "d", [(i, i ^ 1) for i in range(clips)]),
+    ]
     att_got = [turned[0]] + [
         lax.ppermute(turned[hop], "d", [(i, i ^ hop) for i in range(clips)])
         for hop in range(1, clips)
@@ -516,7 +524,8 @@
     partial = call(
         weight_kernel,
         shape(planes, piece, width),
-        (*att_got, og, *other_grads),
+        tuple(att_got[hop] for hop in (2, 3, 1, 0))
+        + tuple((og, *other_grads)[hop] for hop in (2, 3, 1, 0)),
         scratch=(
             pltpu.VMEM((share, clips * tokens), BF16),
             pltpu.VMEM((clips * tokens, width), BF16),
@@ -541,10 +550,11 @@
         specs=[SMEM, VMEM],
     )
     factor = 1.0 / math.sqrt(clips * tokens * positions)
+    moved = paired_off(summed, "z", lines)
     total = call(
         functools.partial(line_sum_kernel, factor),
         shape(piece, lanes, dtype=F32),
-        paired_off(summed, "z", lines),
+        (moved[2], moved[1], moved[3], moved[0]),
     )
     weight_grad = call(
         gather_kernel,

time: 126 us -> 119 us (0.944)
  starting transfers between devices: 74.9 us -> 69.2 us
  waiting for transfers between devices: 30 us -> 27.9 us
    all_to_all x3, waiting for transfers between devices: 9.54 us -> 14.9 us  [swapped(): return lax.all_to_all(array, axes, split_axis=0, concat_axis=0, tiled=True)]
    ppermute x14, waiting for transfers between devices: 14.1 us -> 9.6 us  [to_members(): lax.ppermute(pieces[hop], 'b', [(i, i ^ hop) for i in range(blocks)])]
    ppermute x6, waiting for transfers between devices: 5.18 us -> 2.09 us  [paired_off(): lax.ppermute(pieces[hop], axis, [(i, i ^ hop) for i in range(count)])]
    ppermute x14, starting transfers between devices: 26 us -> 23.5 us  [to_members(): lax.ppermute(pieces[hop], 'b', [(i, i ^ hop) for i in range(blocks)])]
    ppermute x6, starting transfers between devices: 12.6 us -> 10.5 us  [paired_off(): lax.ppermute(pieces[hop], axis, [(i, i ^ hop) for i in range(count)])]
    ppermute x1, starting transfers between devices: 0.6 us -> 2.09 us  [on_device(): lax.ppermute(beyond, 'd', [(i, i ^ 1) for i in range(clips)])]
where the time goes in v5:
time: 119 us; the launch traced here: 118 us
  starting transfers between devices  69.2 us (58%)
  waiting for transfers between devices  27.9 us (23%)
  Pallas kernels  19.4 us (16%)
    ppermute x14, starting transfers between devices, to_members(): lax.ppermute(pieces[hop], 'b', [(i, i ^ hop) for i in range(blocks)])  23.5 us
    all_to_all x3, starting transfers between devices, swapped(): return lax.all_to_all(array, axes, split_axis=0, concat_axis=0, tiled=True)  20.5 us
    pallas_call x10, Pallas kernels, call(): pl.pallas_call(kernel, out_shape=out_shape, in_specs=specs or [VMEM] * le...  19.4 us
    all_to_all x3, waiting for transfers between devices, swapped(): return lax.all_to_all(array, axes, split_axis=0, concat_axis=0, tiled=True)  14.9 us
    ppermute x6, starting transfers between devices, paired_off(): lax.ppermute(pieces[hop], axis, [(i, i ^ hop) for i in range(count)])  10.5 us
    ppermute x14, waiting for transfers between devices, to_members(): lax.ppermute(pieces[hop], 'b', [(i, i ^ hop) for i in range(blocks)])  9.6 us
    ppermute x2, starting transfers between devices, on_device(): lax.ppermute(og_later, 'd', [(i, i ^ hop) for i in range(clips)])  4.29 us
    ppermute x3, starting transfers between devices, on_device(): lax.ppermute(turned[hop], 'd', [(i, i ^ hop) for i in range(clips)])  3.53 us
  transfers between devices with their start and end apart: 31, of which 11 were waited for; matrix products, arithmetic and copies ran while one was open for 0% of the time, Pallas kernels for 11%

profile of v5, /device:TPU:1, one launch (start us, length us, event | category | flops | bytes accessed | tf_op | source)
XLA Modules:
  0.0 118.2 jit_solution(9526294157546182906)
XLA Ops:
  0.6 3.7 %shard_map.92 = (bf16[8,256,128]{2,1,0:T(8,128)(2,1)}, bf16[32,1024]{1,0:T(8,128)(2,1)}, bf16[32,1024]{1,0:T(8,128)(2,1)}, bf16[32,1024]{1,0:T(8,128)(2,1)}, bf1...) custom-call(s32[1]{0:T(128)S(6)} %mul.3.flip_ref, ...), custom_call_target="tpu_custom_call" | custom-call | flops 268435456 | bytes 4194312 | tf_op jit(solution)/shard_map/pallas_call | solution.py:36
  4.4 10.0 %all-to-all-start = ((bf16[8,256,128]{2,1,0:T(8,128)(2,1)}), bf16[8,256,128]{2,1,0:T(8,128)(2,1)S(1)}, u32[]{:S(2)}, u32[]{:S(2)}) async-start(bf16[8,256,128]{2,1,0:T(8,128)(2,1)} %get-tuple-element.83), calls=%async_computation | async-start | bytes 1048576 | tf_op jit(solution)/shard_map/all_to_all | solution.py:373
  14.4 5.1 %collective-permute-start = (bf16[32,1024]{1,0:T(8,128)(2,1)}, bf16[32,1024]{1,0:T(8,128)(2,1)S(1)}, u32[]{:S(2)}, u32[]{:S(2)}) collective-permute-start(bf16[32,1024]{1,0:T(8,128)(2,1)} %get-tuple-element.84), channel_id=1, source_target_pairs={{0,40},{8,32},{16,56},{24,48},{32,8},{40,0},{48,24},{56,16},{1,41}... | collective-permute-start | bytes 196616 | tf_op jit(solution)/shard_map/ppermute | solution.py:421
  19.5 0.4 collective-permute-start.1
  19.9 2.5 %collective-permute-start.2 = (bf16[32,1024]{1,0:T(8,128)(2,1)}, bf16[32,1024]{1,0:T(8,128)(2,1)S(1)}, u32[]{:S(2)}, u32[]{:S(2)}) collective-permute-start(bf16[32,1024]{1,0:T(8,128)(2,1)} %get-tuple-element.86), channel_id=1, source_target_pairs={{0,56},{8,48},{16,40},{24,32},{32,24},{40,16},{48,8},{56,0},{1,57}... | collective-permute-start | bytes 196616 | tf_op jit(solution)/shard_map/ppermute | solution.py:421
  22.4 0.6 collective-permute-start.3
  23.1 2.5 %collective-permute-start.4 = (bf16[32,1024]{1,0:T(8,128)(2,1)}, bf16[32,1024]{1,0:T(8,128)(2,1)S(1)}, u32[]{:S(2)}, u32[]{:S(2)}) collective-permute-start(bf16[32,1024]{1,0:T(8,128)(2,1)} %get-tuple-element.88), channel_id=1, source_target_pairs={{0,32},{8,40},{16,48},{24,56},{32,0},{40,8},{48,16},{56,24},{1,33}... | collective-permute-start | bytes 196616 | tf_op jit(solution)/shard_map/ppermute | solution.py:421
  25.5 0.3 collective-permute-start.5
  25.8 0.6 collective-permute-start.6
  26.5 1.1 collective-permute-done.2.rest_7_
  27.5 5.3 %collective-permute-done.3.rest_1_ = bf16[32,1024]{1,0:T(8,128)(2,1)S(1)} collective-permute-done((bf16[32,1024]{1,0:T(8,128)(2,1)}, bf16[32,1024]{1,0:T(8,128)(2,1)S(1)}, u32[]{:S(2)}, u32[]{:S(2)}) %collective-permute-start.3) | collective-permute-done | bytes 65568 | tf_op jit(solution)/shard_map/ppermute | solution.py:421
  32.9 3.4 %collective-permute-start.7 = (bf16[8,128,128]{2,1,0:T(8,128)(2,1)S(1)}, bf16[8,128,128]{2,1,0:T(8,128)(2,1)S(1)}, u32[]{:S(2)}, u32[]{:S(2)}) collective-permute-start(bf16[8,128,128]{2,1,0:T(8,128)(2,1)S(1)} %slice.6), channel_id=1, source_target_pairs={{0,12},{4,8},{8,20},{12,16},{16,28},{20,24},{24,36},{28,32},{32,44... | collective-permute-start | bytes 786440 | tf_op jit(solution)/shard_map/ppermute | solution.py:426
  36.4 0.7 collective-permute-start.9
  37.1 3.6 %collective-permute-start.8 = (bf16[128,1024]{1,0:T(8,128)(2,1)S(1)}, bf16[128,1024]{1,0:T(8,128)(2,1)S(1)}, u32[]{:S(2)}, u32[]{:S(2)}) collective-permute-start(bf16[128,1024]{1,0:T(8,128)(2,1)S(1)} %bitcast.13), channel_id=1, source_target_pairs={{0,64},{64,0},{128,192},{192,128},{1,65},{65,1},{129,193},{193,129... | collective-permute-start | bytes 786440 | tf_op jit(solution)/shard_map/ppermute | solution.py:436
  40.7 0.8 copy-done.1
  41.5 1.6 %shard_map.93 = (bf16[32,1024]{1,0:T(8,128)(2,1)S(1)}, bf16[32,1024]{1,0:T(8,128)(2,1)S(1)}, bf16[32,1024]{1,0:T(8,128)(2,1)S(1)}, bf16[32,1024]{1,0:T(8,128)(2,...) custom-call(s32[1]{0:T(128)} %bitcast.me_ref.first_ref.block_ref, ...), custom_call_target="tpu_custom_call" | custom-call | flops 201326592 | bytes 1048580 | tf_op jit(solution)/shard_map/pallas_call | solution.py:36
  43.1 6.7 %shard_map.94 = bf16[8,384,128]{2,1,0:T(8,128)(2,1)} custom-call(s32[1]{0:T(128)} %bitcast.me_ref.first_ref.block_ref, bf16[8,256,128]{2,1,0:T(8,128)(2,1)S(1)} %all-to-all-done.in_hbm, bf16[8,128,128]{2,1,0:T(8,128)(2,1)S(1)} %collective-permute-done.7.prev_hbm), custom_call_target="tpu_custom_call" | custom-call | flops 1811939328 | bytes 1572868 | tf_op jit(solution)/shard_map/pallas_call | solution.py:36
  49.9 6.4 %all-to-all-start.1 = ((bf16[8,384,128]{2,1,0:T(8,128)(2,1)}), bf16[8,384,128]{2,1,0:T(8,128)(2,1)S(1)}, u32[]{:S(2)}, u32[]{:S(2)}) async-start(bf16[8,384,128]{2,1,0:T(8,128)(2,1)} %shard_map.94), calls=%async_computation.1 | async-start | bytes 1572864 | tf_op jit(solution)/shard_map/all_to_all | solution.py:373
  56.2 2.7 %collective-permute-start.10 = (bf16[32,1024]{1,0:T(8,128)(2,1)S(1)}, bf16[32,1024]{1,0:T(8,128)(2,1)S(1)}, u32[]{:S(2)}, u32[]{:S(2)}) collective-permute-start(bf16[32,1024]{1,0:T(8,128)(2,1)S(1)} %get-tuple-element.120), channel_id=1, source_target_pairs={{0,40},{8,32},{16,56},{24,48},{32,8},{40,0},{48,24},{56,16},{1,41}... | collective-permute-start | bytes 196616 | tf_op jit(solution)/shard_map/ppermute | solution.py:421
  58.9 0.6 collective-permute-start.11
  59.6 2.7 %collective-permute-start.12 = (bf16[32,1024]{1,0:T(8,128)(2,1)S(1)}, bf16[32,1024]{1,0:T(8,128)(2,1)S(1)}, u32[]{:S(2)}, u32[]{:S(2)}) collective-permute-start(bf16[32,1024]{1,0:T(8,128)(2,1)S(1)} %get-tuple-element.122), channel_id=1, source_target_pairs={{0,56},{8,48},{16,40},{24,32},{32,24},{40,16},{48,8},{56,0},{1,57}... | collective-permute-start | bytes 196616 | tf_op jit(solution)/shard_map/ppermute | solution.py:421
  62.2 2.3 %collective-permute-start.13 = (bf16[32,1024]{1,0:T(8,128)(2,1)S(1)}, bf16[32,1024]{1,0:T(8,128)(2,1)S(1)}, u32[]{:S(2)}, u32[]{:S(2)}) collective-permute-start(bf16[32,1024]{1,0:T(8,128)(2,1)S(1)} %get-tuple-element.123), channel_id=1, source_target_pairs={{0,8},{8,0},{16,24},{24,16},{32,40},{40,32},{48,56},{56,48},{1,9},... | collective-permute-start | bytes 196616 | tf_op jit(solution)/shard_map/ppermute | solution.py:421
  64.6 0.5 collective-permute-start.14
  65.1 0.4 collective-permute-start.15
  65.6 2.2 %collective-permute-start.16 = (bf16[32,1024]{1,0:T(8,128)(2,1)S(1)}, bf16[32,1024]{1,0:T(8,128)(2,1)S(1)}, u32[]{:S(2)}, u32[]{:S(2)}) collective-permute-start(bf16[32,1024]{1,0:T(8,128)(2,1)S(1)} %get-tuple-element.126), channel_id=1, source_target_pairs={{0,48},{8,56},{16,32},{24,40},{32,16},{40,24},{48,0},{56,8},{1,49}... | collective-permute-start | bytes 196616 | tf_op jit(solution)/shard_map/ppermute | solution.py:421
  67.8 1.9 %collective-permute-done.13.rest_1_ = bf16[32,1024]{1,0:T(8,128)(2,1)S(1)} collective-permute-done((bf16[32,1024]{1,0:T(8,128)(2,1)S(1)}, bf16[32,1024]{1,0:T(8,128)(2,1)S(1)}, u32[]{:S(2)}, u32[]{:S(2)}) %collective-permute-start.13) | collective-permute-done | bytes 65568 | tf_op jit(solution)/shard_map/ppermute | solution.py:421
  69.7 1.2 %collective-permute-done.16.rest_6_ = bf16[32,1024]{1,0:T(8,128)(2,1)S(1)} collective-permute-done((bf16[32,1024]{1,0:T(8,128)(2,1)S(1)}, bf16[32,1024]{1,0:T(8,128)(2,1)S(1)}, u32[]{:S(2)}, u32[]{:S(2)}) %collective-permute-start.16) | collective-permute-done | bytes 65568 | tf_op jit(solution)/shard_map/ppermute | solution.py:421
  70.9 5.5 %all-to-all-done.1.row_hbm = bf16[8,384,128]{2,1,0:T(8,128)(2,1)S(1)} async-done(((bf16[8,384,128]{2,1,0:T(8,128)(2,1)}), bf16[8,384,128]{2,1,0:T(8,128)(2,1)S(1)}, u32[]{:S(2)}, u32[]{:S(2)}) %all-to-all-start.1) | async-done | bytes 786464 | tf_op jit(solution)/shard_map/all_to_all | solution.py:373
  76.4 0.9 shard_map.95
  77.3 2.1 %collective-permute-start.21 = (bf16[128,1024]{1,0:T(8,128)(2,1)S(1)}, bf16[128,1024]{1,0:T(8,128)(2,1)S(1)}, u32[]{:S(2)}, u32[]{:S(2)}) collective-permute-start(bf16[128,1024]{1,0:T(8,128)(2,1)S(1)} %collective-permute-done.9.refs_4_), channel_id=1, source_target_pairs={{0,64},{64,0},{128,192},{192,128},{1,65},{65,1},{129,193},{193,129... | collective-permute-start | bytes 786440 | tf_op jit(solution)/shard_map/ppermute | solution.py:490
  79.4 0.3 collective-permute-start.17
  79.7 3.1 %collective-permute-start.18 = (bf16[256,128]{1,0:T(8,128)(2,1)S(1)}, bf16[256,128]{1,0:T(8,128)(2,1)S(1)}, u32[]{:S(2)}, u32[]{:S(2)}) collective-permute-start(bf16[256,128]{1,0:T(8,128)(2,1)S(1)} %get-tuple-element.144), channel_id=1, source_target_pairs={{0,128},{64,192},{128,0},{192,64},{1,129},{65,193},{129,1},{193,65... | collective-permute-start | bytes 196616 | tf_op jit(solution)/shard_map/ppermute | solution.py:493
  82.9 2.8 %shard_map.96 = (bf16[128,1024]{1,0:T(8,128)(2,1)}, bf16[128,1024]{1,0:T(8,128)(2,1)}) custom-call(s32[1]{0:T(128)S(6)} %mul.3.flip_ref, s32[1]{0:T(128)} %bitcast.me_ref.first_ref.block_ref, bf16[1024,1024]{1,0:T(8,128)(2,1)} %w_hbm.3, bf16[8,384,128]{2,1,0:T(8,128)(2,1)S(1)} %all-to-all-done.1.row_hbm, bf16[32,1024]{1,0:T(8,128)(2,1)S(1)} %get-tuple-element.129.rest_0_, ...), custom_call_target="tpu_custom_call" | custom-call | flops 268435456 | bytes 3932168 | tf_op jit(solution)/shard_map/pallas_call | solution.py:36
  85.8 1.3 %collective-permute-done.19.refs_1_ = bf16[256,128]{1,0:T(8,128)(2,1)S(1)} collective-permute-done((bf16[256,128]{1,0:T(8,128)(2,1)S(1)}, bf16[256,128]{1,0:T(8,128)(2,1)S(1)}, u32[]{:S(2)}, u32[]{:S(2)}) %collective-permute-start.19) | collective-permute-done | bytes 65568 | tf_op jit(solution)/shard_map/ppermute | solution.py:493
  87.0 1.4 %shard_map.98 = bf16[16,16,1024]{2,1,0:T(8,128)(2,1)} custom-call(bf16[256,128]{1,0:T(8,128)(2,1)S(1)} %collective-permute-done.18.refs_0_, bf16[256,128]{1,0:T(8,128)(2,1)S(1)} %collective-permute-done.19.refs_1_, bf16[256,128]{1,0:T(8,128)(2,1)S(1)} %collective-permute-done.17.refs_2_, bf16[256,128]{1,0:T(8,128)(2,1)S(1)} %get-tuple-element.154.refs_3_, ...), custom_call_target="tpu_custom_call" | custom-call | flops 268435456 | bytes 1835008 | tf_op jit(solution)/shard_map/pallas_call | solution.py:36
  88.5 4.1 %all-to-all-start.2 = ((bf16[16,16,1024]{2,1,0:T(8,128)(2,1)}), bf16[16,16,1024]{2,1,0:T(8,128)(2,1)S(1)}, u32[]{:S(2)}, u32[]{:S(2)}) async-start(bf16[16,16,1024]{2,1,0:T(8,128)(2,1)} %shard_map.98), calls=%async_computation.2 | async-start | bytes 1048576 | tf_op jit(solution)/shard_map/all_to_all | solution.py:373
  92.6 1.3 %collective-permute-start.20 = (bf16[8,128,128]{2,1,0:T(8,128)(2,1)S(1)}, bf16[8,128,128]{2,1,0:T(8,128)(2,1)S(1)}, u32[]{:S(2)}, u32[]{:S(2)}) collective-permute-start(bf16[8,128,128]{2,1,0:T(8,128)(2,1)S(1)} %slice.7), channel_id=1, source_target_pairs={{8,0},{16,8},{24,16},{32,24},{40,32},{48,40},{56,48},{9,1},{17,9},... | collective-permute-start | bytes 786440 | tf_op jit(solution)/shard_map/ppermute | solution.py:496
  93.9 9.4 %all-to-all-done.2.in_ref = bf16[16,16,1024]{2,1,0:T(8,128)(2,1)S(1)} async-done(((bf16[16,16,1024]{2,1,0:T(8,128)(2,1)}), bf16[16,16,1024]{2,1,0:T(8,128)(2,1)S(1)}, u32[]{:S(2)}, u32[]{:S(2)}) %all-to-all-start.2) | async-done | bytes 524320 | tf_op jit(solution)/shard_map/all_to_all | solution.py:373
  103.4 2.3 %collective-permute-start.22 = (bf16[16,256]{1,0:T(8,128)(2,1)S(1)}, bf16[16,256]{1,0:T(8,128)(2,1)S(1)}, u32[]{:S(2)}, u32[]{:S(2)}) collective-permute-start(bf16[16,256]{1,0:T(8,128)(2,1)S(1)} %get-tuple-element.157), channel_id=1, source_target_pairs={{0,2},{1,3},{2,0},{3,1},{4,6},{5,7},{6,4},{7,5},{8,10},{9,11},{10,... | collective-permute-start | bytes 24584 | tf_op jit(solution)/shard_map/ppermute | solution.py:541
  105.6 0.3 collective-permute-start.23
  105.9 3.2 %collective-permute-start.24 = (bf16[16,256]{1,0:T(8,128)(2,1)S(1)}, bf16[16,256]{1,0:T(8,128)(2,1)S(1)}, u32[]{:S(2)}, u32[]{:S(2)}) collective-permute-start(bf16[16,256]{1,0:T(8,128)(2,1)S(1)} %get-tuple-element.159), channel_id=1, source_target_pairs={{0,3},{1,2},{2,1},{3,0},{4,7},{5,6},{6,5},{7,4},{8,11},{9,10},{10,... | collective-permute-start | bytes 24584 | tf_op jit(solution)/shard_map/ppermute | solution.py:541
  109.1 0.9 collective-permute-done.22.refs_0_
  110.0 0.5 collective-permute-done.24.refs_2_
  110.6 4.0 %collective-permute-start.27 = (f32[16,256]{1,0:T(8,128)S(1)}, f32[16,256]{1,0:T(8,128)S(1)}, u32[]{:S(2)}, u32[]{:S(2)}) collective-permute-start(f32[16,256]{1,0:T(8,128)S(1)} %shard_map.100.rest_0_), channel_id=1, source_target_pairs={{0,192},{64,128},{128,64},{192,0},{1,193},{65,129},{129,65},{193,1... | collective-permute-start | bytes 49160 | tf_op jit(solution)/shard_map/ppermute | solution.py:541
  114.6 0.7 collective-permute-start.26
  115.3 1.5 %shard_map.97 = (bf16[128,1024]{1,0:T(8,128)(2,1)}, bf16[128,1024]{1,0:T(8,128)(2,1)}) custom-call(s32[1]{0:T(128)S(6)} %mul.3.flip_ref, s32[1]{0:T(128)} %bitcast.me_ref.first_ref.block_ref, bf16[8,128,128]{2,1,0:T(8,128)(2,1)S(1)} %collective-permute-done.20.later_hbm, bf16[8,384,128]{2,1,0:T(8,128)(2,1)S(1)} %all-to-all-done.1.row_hbm, ...), custom_call_target="tpu_custom_call" | custom-call | bytes 2097160 | tf_op jit(solution)/shard_map/pallas_call | solution.py:36
  116.8 0.7 collective-permute-done.26.rest_2_
  117.5 0.7 shard_map.101
  (30 shorter events, 0.4 us)
Async XLA Ops:
  0.6 35.8 %copy-start = (bf16[1,128,1024]{2,1,0:T(8,128)(2,1)S(1)}, bf16[1,128,1024]{2,1,0:T(8,128)(2,1)}, u32[]{:S(2)}) copy-start(bf16[1,128,1024]{2,1,0:T(8,128)(2,1)} %param.8) | copy-start | bytes 786436
  4.4 28.5 %all-to-all-start = ((bf16[8,256,128]{2,1,0:T(8,128)(2,1)}), bf16[8,256,128]{2,1,0:T(8,128)(2,1)S(1)}, u32[]{:S(2)}, u32[]{:S(2)}) async-start(bf16[8,256,128]{2,1,0:T(8,128)(2,1)} %get-tuple-element.83), calls=%async_computation | async-start | bytes 1048576 | tf_op jit(solution)/shard_map/all_to_all | solution.py:373
  14.4 11.1 %collective-permute-start = (bf16[32,1024]{1,0:T(8,128)(2,1)}, bf16[32,1024]{1,0:T(8,128)(2,1)S(1)}, u32[]{:S(2)}, u32[]{:S(2)}) collective-permute-start(bf16[32,1024]{1,0:T(8,128)(2,1)} %get-tuple-element.84), channel_id=1, source_target_pairs={{0,40},{8,32},{16,56},{24,48},{32,8},{40,0},{48,24},{56,16},{1,41}... | collective-permute-start | bytes 196616 | tf_op jit(solution)/shard_map/ppermute | solution.py:421
  19.5 6.3 %collective-permute-start.1 = (bf16[32,1024]{1,0:T(8,128)(2,1)}, bf16[32,1024]{1,0:T(8,128)(2,1)S(1)}, u32[]{:S(2)}, u32[]{:S(2)}) collective-permute-start(bf16[32,1024]{1,0:T(8,128)(2,1)} %get-tuple-element.85), channel_id=1, source_target_pairs={{0,24},{8,16},{16,8},{24,0},{32,56},{40,48},{48,40},{56,32},{1,25}... | collective-permute-start | bytes 196616 | tf_op jit(solution)/shard_map/ppermute | solution.py:421
  19.9 7.7 %collective-permute-start.2 = (bf16[32,1024]{1,0:T(8,128)(2,1)}, bf16[32,1024]{1,0:T(8,128)(2,1)S(1)}, u32[]{:S(2)}, u32[]{:S(2)}) collective-permute-start(bf16[32,1024]{1,0:T(8,128)(2,1)} %get-tuple-element.86), channel_id=1, source_target_pairs={{0,56},{8,48},{16,40},{24,32},{32,24},{40,16},{48,8},{56,0},{1,57}... | collective-permute-start | bytes 196616 | tf_op jit(solution)/shard_map/ppermute | solution.py:421
  22.4 10.5 %collective-permute-start.3 = (bf16[32,1024]{1,0:T(8,128)(2,1)}, bf16[32,1024]{1,0:T(8,128)(2,1)S(1)}, u32[]{:S(2)}, u32[]{:S(2)}) collective-permute-start(bf16[32,1024]{1,0:T(8,128)(2,1)} %get-tuple-element.87), channel_id=1, source_target_pairs={{0,8},{8,0},{16,24},{24,16},{32,40},{40,32},{48,56},{56,48},{1,9},... | collective-permute-start | bytes 196616 | tf_op jit(solution)/shard_map/ppermute | solution.py:421
  23.1 9.8 %collective-permute-start.4 = (bf16[32,1024]{1,0:T(8,128)(2,1)}, bf16[32,1024]{1,0:T(8,128)(2,1)S(1)}, u32[]{:S(2)}, u32[]{:S(2)}) collective-permute-start(bf16[32,1024]{1,0:T(8,128)(2,1)} %get-tuple-element.88), channel_id=1, source_target_pairs={{0,32},{8,40},{16,48},{24,56},{32,0},{40,8},{48,16},{56,24},{1,33}... | collective-permute-start | bytes 196616 | tf_op jit(solution)/shard_map/ppermute | solution.py:421
  25.5 7.4 %collective-permute-start.5 = (bf16[32,1024]{1,0:T(8,128)(2,1)}, bf16[32,1024]{1,0:T(8,128)(2,1)S(1)}, u32[]{:S(2)}, u32[]{:S(2)}) collective-permute-start(bf16[32,1024]{1,0:T(8,128)(2,1)} %get-tuple-element.89), channel_id=1, source_target_pairs={{0,16},{8,24},{16,0},{24,8},{32,48},{40,56},{48,32},{56,40},{1,17}... | collective-permute-start | bytes 196616 | tf_op jit(solution)/shard_map/ppermute | solution.py:421
  25.8 7.1 %collective-permute-start.6 = (bf16[32,1024]{1,0:T(8,128)(2,1)}, bf16[32,1024]{1,0:T(8,128)(2,1)S(1)}, u32[]{:S(2)}, u32[]{:S(2)}) collective-permute-start(bf16[32,1024]{1,0:T(8,128)(2,1)} %get-tuple-element.90), channel_id=1, source_target_pairs={{0,48},{8,56},{16,32},{24,40},{32,16},{40,24},{48,0},{56,8},{1,49}... | collective-permute-start | bytes 196616 | tf_op jit(solution)/shard_map/ppermute | solution.py:421
  32.9 10.2 %collective-permute-start.7 = (bf16[8,128,128]{2,1,0:T(8,128)(2,1)S(1)}, bf16[8,128,128]{2,1,0:T(8,128)(2,1)S(1)}, u32[]{:S(2)}, u32[]{:S(2)}) collective-permute-start(bf16[8,128,128]{2,1,0:T(8,128)(2,1)S(1)} %slice.6), channel_id=1, source_target_pairs={{0,12},{4,8},{8,20},{12,16},{16,28},{20,24},{24,36},{28,32},{32,44... | collective-permute-start | bytes 786440 | tf_op jit(solution)/shard_map/ppermute | solution.py:426
  36.4 13.4 %collective-permute-start.9 = (bf16[128,1024]{1,0:T(8,128)(2,1)S(1)}, bf16[128,1024]{1,0:T(8,128)(2,1)S(1)}, u32[]{:S(2)}, u32[]{:S(2)}) collective-permute-start(bf16[128,1024]{1,0:T(8,128)(2,1)S(1)} %bitcast.12), channel_id=1, source_target_pairs={{0,128},{64,192},{128,0},{192,64},{1,129},{65,193},{129,1},{193,65... | collective-permute-start | bytes 786440 | tf_op jit(solution)/shard_map/ppermute | solution.py:436
  37.1 12.8 %collective-permute-start.8 = (bf16[128,1024]{1,0:T(8,128)(2,1)S(1)}, bf16[128,1024]{1,0:T(8,128)(2,1)S(1)}, u32[]{:S(2)}, u32[]{:S(2)}) collective-permute-start(bf16[128,1024]{1,0:T(8,128)(2,1)S(1)} %bitcast.13), channel_id=1, source_target_pairs={{0,64},{64,0},{128,192},{192,128},{1,65},{65,1},{129,193},{193,129... | collective-permute-start | bytes 786440 | tf_op jit(solution)/shard_map/ppermute | solution.py:436
  40.7 0.8 copy-start.1
  49.9 26.5 %all-to-all-start.1 = ((bf16[8,384,128]{2,1,0:T(8,128)(2,1)}), bf16[8,384,128]{2,1,0:T(8,128)(2,1)S(1)}, u32[]{:S(2)}, u32[]{:S(2)}) async-start(bf16[8,384,128]{2,1,0:T(8,128)(2,1)} %shard_map.94), calls=%async_computation.1 | async-start | bytes 1572864 | tf_op jit(solution)/shard_map/all_to_all | solution.py:373
  56.2 8.9 %collective-permute-start.10 = (bf16[32,1024]{1,0:T(8,128)(2,1)S(1)}, bf16[32,1024]{1,0:T(8,128)(2,1)S(1)}, u32[]{:S(2)}, u32[]{:S(2)}) collective-permute-start(bf16[32,1024]{1,0:T(8,128)(2,1)S(1)} %get-tuple-element.120), channel_id=1, source_target_pairs={{0,40},{8,32},{16,56},{24,48},{32,8},{40,0},{48,24},{56,16},{1,41}... | collective-permute-start | bytes 196616 | tf_op jit(solution)/shard_map/ppermute | solution.py:421
  58.9 6.7 %collective-permute-start.11 = (bf16[32,1024]{1,0:T(8,128)(2,1)S(1)}, bf16[32,1024]{1,0:T(8,128)(2,1)S(1)}, u32[]{:S(2)}, u32[]{:S(2)}) collective-permute-start(bf16[32,1024]{1,0:T(8,128)(2,1)S(1)} %get-tuple-element.121), channel_id=1, source_target_pairs={{0,24},{8,16},{16,8},{24,0},{32,56},{40,48},{48,40},{56,32},{1,25}... | collective-permute-start | bytes 196616 | tf_op jit(solution)/shard_map/ppermute | solution.py:421
  59.6 8.3 %collective-permute-start.12 = (bf16[32,1024]{1,0:T(8,128)(2,1)S(1)}, bf16[32,1024]{1,0:T(8,128)(2,1)S(1)}, u32[]{:S(2)}, u32[]{:S(2)}) collective-permute-start(bf16[32,1024]{1,0:T(8,128)(2,1)S(1)} %get-tuple-element.122), channel_id=1, source_target_pairs={{0,56},{8,48},{16,40},{24,32},{32,24},{40,16},{48,8},{56,0},{1,57}... | collective-permute-start | bytes 196616 | tf_op jit(solution)/shard_map/ppermute | solution.py:421
  62.2 7.5 %collective-permute-start.13 = (bf16[32,1024]{1,0:T(8,128)(2,1)S(1)}, bf16[32,1024]{1,0:T(8,128)(2,1)S(1)}, u32[]{:S(2)}, u32[]{:S(2)}) collective-permute-start(bf16[32,1024]{1,0:T(8,128)(2,1)S(1)} %get-tuple-element.123), channel_id=1, source_target_pairs={{0,8},{8,0},{16,24},{24,16},{32,40},{40,32},{48,56},{56,48},{1,9},... | collective-permute-start | bytes 196616 | tf_op jit(solution)/shard_map/ppermute | solution.py:421
  64.6 5.1 %collective-permute-start.14 = (bf16[32,1024]{1,0:T(8,128)(2,1)S(1)}, bf16[32,1024]{1,0:T(8,128)(2,1)S(1)}, u32[]{:S(2)}, u32[]{:S(2)}) collective-permute-start(bf16[32,1024]{1,0:T(8,128)(2,1)S(1)} %get-tuple-element.124), channel_id=1, source_target_pairs={{0,32},{8,40},{16,48},{24,56},{32,0},{40,8},{48,16},{56,24},{1,33}... | collective-permute-start | bytes 196616 | tf_op jit(solution)/shard_map/ppermute | solution.py:421
  65.1 4.6 %collective-permute-start.15 = (bf16[32,1024]{1,0:T(8,128)(2,1)S(1)}, bf16[32,1024]{1,0:T(8,128)(2,1)S(1)}, u32[]{:S(2)}, u32[]{:S(2)}) collective-permute-start(bf16[32,1024]{1,0:T(8,128)(2,1)S(1)} %get-tuple-element.125), channel_id=1, source_target_pairs={{0,16},{8,24},{16,0},{24,8},{32,48},{40,56},{48,32},{56,40},{1,17}... | collective-permute-start | bytes 196616 | tf_op jit(solution)/shard_map/ppermute | solution.py:421
  65.6 5.3 %collective-permute-start.16 = (bf16[32,1024]{1,0:T(8,128)(2,1)S(1)}, bf16[32,1024]{1,0:T(8,128)(2,1)S(1)}, u32[]{:S(2)}, u32[]{:S(2)}) collective-permute-start(bf16[32,1024]{1,0:T(8,128)(2,1)S(1)} %get-tuple-element.126), channel_id=1, source_target_pairs={{0,48},{8,56},{16,32},{24,40},{32,16},{40,24},{48,0},{56,8},{1,49}... | collective-permute-start | bytes 196616 | tf_op jit(solution)/shard_map/ppermute | solution.py:421
  77.3 9.8 %collective-permute-start.21 = (bf16[128,1024]{1,0:T(8,128)(2,1)S(1)}, bf16[128,1024]{1,0:T(8,128)(2,1)S(1)}, u32[]{:S(2)}, u32[]{:S(2)}) collective-permute-start(bf16[128,1024]{1,0:T(8,128)(2,1)S(1)} %collective-permute-done.9.refs_4_), channel_id=1, source_target_pairs={{0,64},{64,0},{128,192},{192,128},{1,65},{65,1},{129,193},{193,129... | collective-permute-start | bytes 786440 | tf_op jit(solution)/shard_map/ppermute | solution.py:490
  79.4 6.4 %collective-permute-start.17 = (bf16[256,128]{1,0:T(8,128)(2,1)S(1)}, bf16[256,128]{1,0:T(8,128)(2,1)S(1)}, u32[]{:S(2)}, u32[]{:S(2)}) collective-permute-start(bf16[256,128]{1,0:T(8,128)(2,1)S(1)} %get-tuple-element.143), channel_id=1, source_target_pairs={{0,64},{64,0},{128,192},{192,128},{1,65},{65,1},{129,193},{193,129... | collective-permute-start | bytes 196616 | tf_op jit(solution)/shard_map/ppermute | solution.py:493
  79.7 6.1 %collective-permute-start.18 = (bf16[256,128]{1,0:T(8,128)(2,1)S(1)}, bf16[256,128]{1,0:T(8,128)(2,1)S(1)}, u32[]{:S(2)}, u32[]{:S(2)}) collective-permute-start(bf16[256,128]{1,0:T(8,128)(2,1)S(1)} %get-tuple-element.144), channel_id=1, source_target_pairs={{0,128},{64,192},{128,0},{192,64},{1,129},{65,193},{129,1},{193,65... | collective-permute-start | bytes 196616 | tf_op jit(solution)/shard_map/ppermute | solution.py:493
  82.8 4.2 %collective-permute-start.19 = (bf16[256,128]{1,0:T(8,128)(2,1)S(1)}, bf16[256,128]{1,0:T(8,128)(2,1)S(1)}, u32[]{:S(2)}, u32[]{:S(2)}) collective-permute-start(bf16[256,128]{1,0:T(8,128)(2,1)S(1)} %get-tuple-element.145), channel_id=1, source_target_pairs={{0,192},{64,128},{128,64},{192,0},{1,193},{65,129},{129,65},{193,1... | collective-permute-start | bytes 196616 | tf_op jit(solution)/shard_map/ppermute | solution.py:493
  88.5 14.9 %all-to-all-start.2 = ((bf16[16,16,1024]{2,1,0:T(8,128)(2,1)}), bf16[16,16,1024]{2,1,0:T(8,128)(2,1)S(1)}, u32[]{:S(2)}, u32[]{:S(2)}) async-start(bf16[16,16,1024]{2,1,0:T(8,128)(2,1)} %shard_map.98), calls=%async_computation.2 | async-start | bytes 1048576 | tf_op jit(solution)/shard_map/all_to_all | solution.py:373
  92.6 22.7 %collective-permute-start.20 = (bf16[8,128,128]{2,1,0:T(8,128)(2,1)S(1)}, bf16[8,128,128]{2,1,0:T(8,128)(2,1)S(1)}, u32[]{:S(2)}, u32[]{:S(2)}) collective-permute-start(bf16[8,128,128]{2,1,0:T(8,128)(2,1)S(1)} %slice.7), channel_id=1, source_target_pairs={{8,0},{16,8},{24,16},{32,24},{40,32},{48,40},{56,48},{9,1},{17,9},... | collective-permute-start | bytes 786440 | tf_op jit(solution)/shard_map/ppermute | solution.py:496
  103.4 6.6 %collective-permute-start.22 = (bf16[16,256]{1,0:T(8,128)(2,1)S(1)}, bf16[16,256]{1,0:T(8,128)(2,1)S(1)}, u32[]{:S(2)}, u32[]{:S(2)}) collective-permute-start(bf16[16,256]{1,0:T(8,128)(2,1)S(1)} %get-tuple-element.157), channel_id=1, source_target_pairs={{0,2},{1,3},{2,0},{3,1},{4,6},{5,7},{6,4},{7,5},{8,10},{9,11},{10,... | collective-permute-start | bytes 24584 | tf_op jit(solution)/shard_map/ppermute | solution.py:541
  105.6 4.4 %collective-permute-start.23 = (bf16[16,256]{1,0:T(8,128)(2,1)S(1)}, bf16[16,256]{1,0:T(8,128)(2,1)S(1)}, u32[]{:S(2)}, u32[]{:S(2)}) collective-permute-start(bf16[16,256]{1,0:T(8,128)(2,1)S(1)} %get-tuple-element.158), channel_id=1, source_target_pairs={{0,1},{1,0},{2,3},{3,2},{4,5},{5,4},{6,7},{7,6},{8,9},{9,8},{10,11... | collective-permute-start | bytes 24584 | tf_op jit(solution)/shard_map/ppermute | solution.py:541
  105.9 4.6 %collective-permute-start.24 = (bf16[16,256]{1,0:T(8,128)(2,1)S(1)}, bf16[16,256]{1,0:T(8,128)(2,1)S(1)}, u32[]{:S(2)}, u32[]{:S(2)}) collective-permute-start(bf16[16,256]{1,0:T(8,128)(2,1)S(1)} %get-tuple-element.159), channel_id=1, source_target_pairs={{0,3},{1,2},{2,1},{3,0},{4,7},{5,6},{6,5},{7,4},{8,11},{9,10},{10,... | collective-permute-start | bytes 24584 | tf_op jit(solution)/shard_map/ppermute | solution.py:541
  110.6 6.3 %collective-permute-start.27 = (f32[16,256]{1,0:T(8,128)S(1)}, f32[16,256]{1,0:T(8,128)S(1)}, u32[]{:S(2)}, u32[]{:S(2)}) collective-permute-start(f32[16,256]{1,0:T(8,128)S(1)} %shard_map.100.rest_0_), channel_id=1, source_target_pairs={{0,192},{64,128},{128,64},{192,0},{1,193},{65,129},{129,65},{193,1... | collective-permute-start | bytes 49160 | tf_op jit(solution)/shard_map/ppermute | solution.py:541
  114.6 2.9 %collective-permute-start.26 = (f32[16,256]{1,0:T(8,128)S(1)}, f32[16,256]{1,0:T(8,128)S(1)}, u32[]{:S(2)}, u32[]{:S(2)}) collective-permute-start(f32[16,256]{1,0:T(8,128)S(1)} %shard_map.100.rest_0_), channel_id=1, source_target_pairs={{0,128},{64,192},{128,0},{192,64},{1,129},{65,193},{129,1},{193,65... | collective-permute-start | bytes 49160 | tf_op jit(solution)/shard_map/ppermute | solution.py:541
  115.3 2.2 %collective-permute-start.25 = (f32[16,256]{1,0:T(8,128)S(1)}, f32[16,256]{1,0:T(8,128)S(1)}, u32[]{:S(2)}, u32[]{:S(2)}) collective-permute-start(f32[16,256]{1,0:T(8,128)S(1)} %shard_map.100.rest_0_), channel_id=1, source_target_pairs={{0,64},{64,0},{128,192},{192,128},{1,65},{65,1},{129,193},{193,129... | collective-permute-start | bytes 49160 | tf_op jit(solution)/shard_map/ppermute | solution.py:541

commit v6 on v5

--- a/solution.py
+++ b/solution.py
@@ -15,7 +15,7 @@
 BF16 = jnp.bfloat16
 F32 = jnp.float32
 ROOM = 60 << 20
-FAR_FIRST = (5, 3, 7, 1, 4, 2, 6, 0)
+FAR_FIRST = (5, 4, 3, 7, 1, 2, 6, 0)
 SCALE = 1.0 / math.sqrt(DH)
 SCALE_LOG2 = SCALE / math.log(2.0)
 NT = (((1,), (1,)), ((), ()))
@@ -465,6 +465,7 @@
             sems((3,)),
         ),
         flops=members * 12 * window * tokens * LANES,
+        vmem=24 << 20,
         specs=[SMEM, HBM, HBM],
     )
     row_res, col_res, beside, beyond = lax.optimization_barrier(

time: 119 us -> 118 us (level)
  starting transfers between devices: 69.2 us -> 67.8 us
    ppermute x14, waiting for transfers between devices: 9.6 us -> 11.4 us  [to_members(): lax.ppermute(pieces[hop], 'b', [(i, i ^ hop) for i in range(blocks)])]
    all_to_all x3, waiting for transfers between devices: 14.9 us -> 13.7 us  [swapped(): return lax.all_to_all(array, axes, split_axis=0, concat_axis=0, tiled=True)]
  transfers between devices with their start and end apart: 31 -> 31, of which waited for: 11 -> 12; matrix products, arithmetic and copies ran while one was open for 0% -> 0% of each run, Pallas kernels for 11% -> 11%
where the time goes in v6:
time: 118 us
  starting transfers between devices  67.8 us (57%)
  waiting for transfers between devices  28.9 us (24%)
  Pallas kernels  19.4 us (16%)
    ppermute x14, starting transfers between devices, to_members(): lax.ppermute(pieces[hop], 'b', [(i, i ^ hop) for i in range(blocks)])  23.6 us
    all_to_all x3, starting transfers between devices, swapped(): return lax.all_to_all(array, axes, split_axis=0, concat_axis=0, tiled=True)  20 us
    pallas_call x10, Pallas kernels, call(): pl.pallas_call(kernel, out_shape=out_shape, in_specs=specs or [VMEM] * le...  19.4 us
    all_to_all x3, waiting for transfers between devices, swapped(): return lax.all_to_all(array, axes, split_axis=0, concat_axis=0, tiled=True)  13.7 us
    ppermute x14, waiting for transfers between devices, to_members(): lax.ppermute(pieces[hop], 'b', [(i, i ^ hop) for i in range(blocks)])  11.4 us
    ppermute x6, starting transfers between devices, paired_off(): lax.ppermute(pieces[hop], axis, [(i, i ^ hop) for i in range(count)])  10.1 us
    ppermute x2, starting transfers between devices, on_device(): lax.ppermute(og_later, 'd', [(i, i ^ hop) for i in range(clips)])  3.64 us
    ppermute x3, starting transfers between devices, on_device(): lax.ppermute(turned[hop], 'd', [(i, i ^ hop) for i in range(clips)])  3.53 us
  transfers between devices with their start and end apart: 31, of which 12 were waited for; matrix products, arithmetic and copies ran while one was open for 0% of the time, Pallas kernels for 11%

profile of v6, /device:TPU:1, one launch (start us, length us, event | category | flops | bytes accessed | tf_op | source)
XLA Modules:
  0.0 117.9 jit_solution(14736379331225692556)
XLA Ops:
  0.6 3.7 %shard_map.92 = (bf16[8,256,128]{2,1,0:T(8,128)(2,1)}, bf16[32,1024]{1,0:T(8,128)(2,1)}, bf16[32,1024]{1,0:T(8,128)(2,1)}, bf16[32,1024]{1,0:T(8,128)(2,1)}, bf1...) custom-call(s32[1]{0:T(128)S(6)} %mul.3.flip_ref, ...), custom_call_target="tpu_custom_call" | custom-call | flops 268435456 | bytes 4194312 | tf_op jit(solution)/shard_map/pallas_call | solution.py:36
  4.4 10.0 %all-to-all-start = ((bf16[8,256,128]{2,1,0:T(8,128)(2,1)}), bf16[8,256,128]{2,1,0:T(8,128)(2,1)S(1)}, u32[]{:S(2)}, u32[]{:S(2)}) async-start(bf16[8,256,128]{2,1,0:T(8,128)(2,1)} %get-tuple-element.83), calls=%async_computation | async-start | bytes 1048576 | tf_op jit(solution)/shard_map/all_to_all | solution.py:373
  14.4 5.1 %collective-permute-start = (bf16[32,1024]{1,0:T(8,128)(2,1)}, bf16[32,1024]{1,0:T(8,128)(2,1)S(1)}, u32[]{:S(2)}, u32[]{:S(2)}) collective-permute-start(bf16[32,1024]{1,0:T(8,128)(2,1)} %get-tuple-element.84), channel_id=1, source_target_pairs={{0,40},{8,32},{16,56},{24,48},{32,8},{40,0},{48,24},{56,16},{1,41}... | collective-permute-start | bytes 196616 | tf_op jit(solution)/shard_map/ppermute | solution.py:421
  19.5 0.2 collective-permute-start.1
  19.7 1.3 %collective-permute-start.2 = (bf16[32,1024]{1,0:T(8,128)(2,1)}, bf16[32,1024]{1,0:T(8,128)(2,1)S(1)}, u32[]{:S(2)}, u32[]{:S(2)}) collective-permute-start(bf16[32,1024]{1,0:T(8,128)(2,1)} %get-tuple-element.86), channel_id=1, source_target_pairs={{0,24},{8,16},{16,8},{24,0},{32,56},{40,48},{48,40},{56,32},{1,25}... | collective-permute-start | bytes 196616 | tf_op jit(solution)/shard_map/ppermute | solution.py:421
  21.0 4.2 %collective-permute-start.3 = (bf16[32,1024]{1,0:T(8,128)(2,1)}, bf16[32,1024]{1,0:T(8,128)(2,1)S(1)}, u32[]{:S(2)}, u32[]{:S(2)}) collective-permute-start(bf16[32,1024]{1,0:T(8,128)(2,1)} %get-tuple-element.87), channel_id=1, source_target_pairs={{0,56},{8,48},{16,40},{24,32},{32,24},{40,16},{48,8},{56,0},{1,57}... | collective-permute-start | bytes 196616 | tf_op jit(solution)/shard_map/ppermute | solution.py:421
  25.2 0.3 collective-permute-start.4
  25.5 0.3 collective-permute-start.5
  25.8 0.6 collective-permute-start.6
  26.5 2.1 %collective-permute-done.3.rest_7_ = bf16[32,1024]{1,0:T(8,128)(2,1)S(1)} collective-permute-done((bf16[32,1024]{1,0:T(8,128)(2,1)}, bf16[32,1024]{1,0:T(8,128)(2,1)S(1)}, u32[]{:S(2)}, u32[]{:S(2)}) %collective-permute-start.3) | collective-permute-done | bytes 65568 | tf_op jit(solution)/shard_map/ppermute | solution.py:421
  28.6 4.9 %collective-permute-done.4.rest_1_ = bf16[32,1024]{1,0:T(8,128)(2,1)S(1)} collective-permute-done((bf16[32,1024]{1,0:T(8,128)(2,1)}, bf16[32,1024]{1,0:T(8,128)(2,1)S(1)}, u32[]{:S(2)}, u32[]{:S(2)}) %collective-permute-start.4) | collective-permute-done | bytes 65568 | tf_op jit(solution)/shard_map/ppermute | solution.py:421
  33.5 3.5 %collective-permute-start.7 = (bf16[8,128,128]{2,1,0:T(8,128)(2,1)S(1)}, bf16[8,128,128]{2,1,0:T(8,128)(2,1)S(1)}, u32[]{:S(2)}, u32[]{:S(2)}) collective-permute-start(bf16[8,128,128]{2,1,0:T(8,128)(2,1)S(1)} %slice.6), channel_id=1, source_target_pairs={{0,12},{4,8},{8,20},{12,16},{16,28},{20,24},{24,36},{28,32},{32,44... | collective-permute-start | bytes 786440 | tf_op jit(solution)/shard_map/ppermute | solution.py:426
  37.1 3.6 %collective-permute-start.8 = (bf16[128,1024]{1,0:T(8,128)(2,1)S(1)}, bf16[128,1024]{1,0:T(8,128)(2,1)S(1)}, u32[]{:S(2)}, u32[]{:S(2)}) collective-permute-start(bf16[128,1024]{1,0:T(8,128)(2,1)S(1)} %bitcast.13), channel_id=1, source_target_pairs={{0,64},{64,0},{128,192},{192,128},{1,65},{65,1},{129,193},{193,129... | collective-permute-start | bytes 786440 | tf_op jit(solution)/shard_map/ppermute | solution.py:436
  40.7 0.8 copy-done.1
  41.5 1.6 %shard_map.93 = (bf16[32,1024]{1,0:T(8,128)(2,1)S(1)}, bf16[32,1024]{1,0:T(8,128)(2,1)S(1)}, bf16[32,1024]{1,0:T(8,128)(2,1)S(1)}, bf16[32,1024]{1,0:T(8,128)(2,...) custom-call(s32[1]{0:T(128)} %bitcast.me_ref.first_ref.block_ref, ...), custom_call_target="tpu_custom_call" | custom-call | flops 201326592 | bytes 1048580 | tf_op jit(solution)/shard_map/pallas_call | solution.py:36
  43.1 6.7 %shard_map.94 = bf16[8,384,128]{2,1,0:T(8,128)(2,1)} custom-call(s32[1]{0:T(128)} %bitcast.me_ref.first_ref.block_ref, bf16[8,256,128]{2,1,0:T(8,128)(2,1)S(1)} %all-to-all-done.in_hbm, bf16[8,128,128]{2,1,0:T(8,128)(2,1)S(1)} %collective-permute-done.7.prev_hbm), custom_call_target="tpu_custom_call" | custom-call | flops 1811939328 | bytes 1572868 | tf_op jit(solution)/shard_map/pallas_call | solution.py:36
  49.9 6.4 %all-to-all-start.1 = ((bf16[8,384,128]{2,1,0:T(8,128)(2,1)}), bf16[8,384,128]{2,1,0:T(8,128)(2,1)S(1)}, u32[]{:S(2)}, u32[]{:S(2)}) async-start(bf16[8,384,128]{2,1,0:T(8,128)(2,1)} %shard_map.94), calls=%async_computation.1 | async-start | bytes 1572864 | tf_op jit(solution)/shard_map/all_to_all | solution.py:373
  56.2 2.2 %collective-permute-start.10 = (bf16[32,1024]{1,0:T(8,128)(2,1)S(1)}, bf16[32,1024]{1,0:T(8,128)(2,1)S(1)}, u32[]{:S(2)}, u32[]{:S(2)}) collective-permute-start(bf16[32,1024]{1,0:T(8,128)(2,1)S(1)} %get-tuple-element.120), channel_id=1, source_target_pairs={{0,40},{8,32},{16,56},{24,48},{32,8},{40,0},{48,24},{56,16},{1,41}... | collective-permute-start | bytes 196616 | tf_op jit(solution)/shard_map/ppermute | solution.py:421
  58.4 1.1 collective-permute-start.11
  59.5 2.0 %collective-permute-start.12 = (bf16[32,1024]{1,0:T(8,128)(2,1)S(1)}, bf16[32,1024]{1,0:T(8,128)(2,1)S(1)}, u32[]{:S(2)}, u32[]{:S(2)}) collective-permute-start(bf16[32,1024]{1,0:T(8,128)(2,1)S(1)} %get-tuple-element.122), channel_id=1, source_target_pairs={{0,24},{8,16},{16,8},{24,0},{32,56},{40,48},{48,40},{56,32},{1,25}... | collective-permute-start | bytes 196616 | tf_op jit(solution)/shard_map/ppermute | solution.py:421
  61.5 2.6 %collective-permute-start.13 = (bf16[32,1024]{1,0:T(8,128)(2,1)S(1)}, bf16[32,1024]{1,0:T(8,128)(2,1)S(1)}, u32[]{:S(2)}, u32[]{:S(2)}) collective-permute-start(bf16[32,1024]{1,0:T(8,128)(2,1)S(1)} %get-tuple-element.123), channel_id=1, source_target_pairs={{0,56},{8,48},{16,40},{24,32},{32,24},{40,16},{48,8},{56,0},{1,57}... | collective-permute-start | bytes 196616 | tf_op jit(solution)/shard_map/ppermute | solution.py:421
  64.1 3.0 %collective-permute-start.14 = (bf16[32,1024]{1,0:T(8,128)(2,1)S(1)}, bf16[32,1024]{1,0:T(8,128)(2,1)S(1)}, u32[]{:S(2)}, u32[]{:S(2)}) collective-permute-start(bf16[32,1024]{1,0:T(8,128)(2,1)S(1)} %get-tuple-element.124), channel_id=1, source_target_pairs={{0,8},{8,0},{16,24},{24,16},{32,40},{40,32},{48,56},{56,48},{1,9},... | collective-permute-start | bytes 196616 | tf_op jit(solution)/shard_map/ppermute | solution.py:421
  67.1 0.7 collective-permute-start.16
  67.8 1.5 %collective-permute-done.13.rest_7_ = bf16[32,1024]{1,0:T(8,128)(2,1)S(1)} collective-permute-done((bf16[32,1024]{1,0:T(8,128)(2,1)S(1)}, bf16[32,1024]{1,0:T(8,128)(2,1)S(1)}, u32[]{:S(2)}, u32[]{:S(2)}) %collective-permute-start.13) | collective-permute-done | bytes 65568 | tf_op jit(solution)/shard_map/ppermute | solution.py:421
  69.3 0.5 collective-permute-done.14.rest_1_
  69.8 0.7 collective-permute-done.15.rest_2_
  70.5 1.7 %collective-permute-done.16.rest_6_ = bf16[32,1024]{1,0:T(8,128)(2,1)S(1)} collective-permute-done((bf16[32,1024]{1,0:T(8,128)(2,1)S(1)}, bf16[32,1024]{1,0:T(8,128)(2,1)S(1)}, u32[]{:S(2)}, u32[]{:S(2)}) %collective-permute-start.16) | collective-permute-done | bytes 65568 | tf_op jit(solution)/shard_map/ppermute | solution.py:421
  72.2 4.1 %all-to-all-done.1.row_hbm = bf16[8,384,128]{2,1,0:T(8,128)(2,1)S(1)} async-done(((bf16[8,384,128]{2,1,0:T(8,128)(2,1)}), bf16[8,384,128]{2,1,0:T(8,128)(2,1)S(1)}, u32[]{:S(2)}, u32[]{:S(2)}) %all-to-all-start.1) | async-done | bytes 786464 | tf_op jit(solution)/shard_map/all_to_all | solution.py:373
  76.4 0.9 shard_map.95
  77.2 2.1 %collective-permute-start.21 = (bf16[128,1024]{1,0:T(8,128)(2,1)S(1)}, bf16[128,1024]{1,0:T(8,128)(2,1)S(1)}, u32[]{:S(2)}, u32[]{:S(2)}) collective-permute-start(bf16[128,1024]{1,0:T(8,128)(2,1)S(1)} %collective-permute-done.9.refs_4_), channel_id=1, source_target_pairs={{0,64},{64,0},{128,192},{192,128},{1,65},{65,1},{129,193},{193,129... | collective-permute-start | bytes 786440 | tf_op jit(solution)/shard_map/ppermute | solution.py:491
  79.4 0.3 collective-permute-start.17
  79.7 3.1 %collective-permute-start.18 = (bf16[256,128]{1,0:T(8,128)(2,1)S(1)}, bf16[256,128]{1,0:T(8,128)(2,1)S(1)}, u32[]{:S(2)}, u32[]{:S(2)}) collective-permute-start(bf16[256,128]{1,0:T(8,128)(2,1)S(1)} %get-tuple-element.144), channel_id=1, source_target_pairs={{0,128},{64,192},{128,0},{192,64},{1,129},{65,193},{129,1},{193,65... | collective-permute-start | bytes 196616 | tf_op jit(solution)/shard_map/ppermute | solution.py:494
  82.8 0.1 collective-permute-start.19
  82.9 2.8 %shard_map.96 = (bf16[128,1024]{1,0:T(8,128)(2,1)}, bf16[128,1024]{1,0:T(8,128)(2,1)}) custom-call(s32[1]{0:T(128)S(6)} %mul.3.flip_ref, s32[1]{0:T(128)} %bitcast.me_ref.first_ref.block_ref, bf16[1024,1024]{1,0:T(8,128)(2,1)} %w_hbm.3, bf16[8,384,128]{2,1,0:T(8,128)(2,1)S(1)} %all-to-all-done.1.row_hbm, bf16[32,1024]{1,0:T(8,128)(2,1)S(1)} %get-tuple-element.129.rest_0_, ...), custom_call_target="tpu_custom_call" | custom-call | flops 268435456 | bytes 3932168 | tf_op jit(solution)/shard_map/pallas_call | solution.py:36
  85.8 1.3 %collective-permute-done.19.refs_1_ = bf16[256,128]{1,0:T(8,128)(2,1)S(1)} collective-permute-done((bf16[256,128]{1,0:T(8,128)(2,1)S(1)}, bf16[256,128]{1,0:T(8,128)(2,1)S(1)}, u32[]{:S(2)}, u32[]{:S(2)}) %collective-permute-start.19) | collective-permute-done | bytes 65568 | tf_op jit(solution)/shard_map/ppermute | solution.py:494
  87.0 1.4 %shard_map.98 = bf16[16,16,1024]{2,1,0:T(8,128)(2,1)} custom-call(bf16[256,128]{1,0:T(8,128)(2,1)S(1)} %collective-permute-done.18.refs_0_, bf16[256,128]{1,0:T(8,128)(2,1)S(1)} %collective-permute-done.19.refs_1_, bf16[256,128]{1,0:T(8,128)(2,1)S(1)} %collective-permute-done.17.refs_2_, bf16[256,128]{1,0:T(8,128)(2,1)S(1)} %get-tuple-element.154.refs_3_, ...), custom_call_target="tpu_custom_call" | custom-call | flops 268435456 | bytes 1835008 | tf_op jit(solution)/shard_map/pallas_call | solution.py:36
  88.5 3.6 %all-to-all-start.2 = ((bf16[16,16,1024]{2,1,0:T(8,128)(2,1)}), bf16[16,16,1024]{2,1,0:T(8,128)(2,1)S(1)}, u32[]{:S(2)}, u32[]{:S(2)}) async-start(bf16[16,16,1024]{2,1,0:T(8,128)(2,1)} %shard_map.98), calls=%async_computation.2 | async-start | bytes 1048576 | tf_op jit(solution)/shard_map/all_to_all | solution.py:373
  92.1 1.3 %collective-permute-start.20 = (bf16[8,128,128]{2,1,0:T(8,128)(2,1)S(1)}, bf16[8,128,128]{2,1,0:T(8,128)(2,1)S(1)}, u32[]{:S(2)}, u32[]{:S(2)}) collective-permute-start(bf16[8,128,128]{2,1,0:T(8,128)(2,1)S(1)} %slice.7), channel_id=1, source_target_pairs={{8,0},{16,8},{24,16},{32,24},{40,32},{48,40},{56,48},{9,1},{17,9},... | collective-permute-start | bytes 786440 | tf_op jit(solution)/shard_map/ppermute | solution.py:497
  93.4 9.5 %all-to-all-done.2.in_ref = bf16[16,16,1024]{2,1,0:T(8,128)(2,1)S(1)} async-done(((bf16[16,16,1024]{2,1,0:T(8,128)(2,1)}), bf16[16,16,1024]{2,1,0:T(8,128)(2,1)S(1)}, u32[]{:S(2)}, u32[]{:S(2)}) %all-to-all-start.2) | async-done | bytes 524320 | tf_op jit(solution)/shard_map/all_to_all | solution.py:373
  103.0 2.7 %collective-permute-start.22 = (bf16[16,256]{1,0:T(8,128)(2,1)S(1)}, bf16[16,256]{1,0:T(8,128)(2,1)S(1)}, u32[]{:S(2)}, u32[]{:S(2)}) collective-permute-start(bf16[16,256]{1,0:T(8,128)(2,1)S(1)} %get-tuple-element.157), channel_id=1, source_target_pairs={{0,2},{1,3},{2,0},{3,1},{4,6},{5,7},{6,4},{7,5},{8,10},{9,11},{10,... | collective-permute-start | bytes 24584 | tf_op jit(solution)/shard_map/ppermute | solution.py:542
  105.6 0.7 collective-permute-start.23
  106.3 2.4 %collective-permute-start.24 = (bf16[16,256]{1,0:T(8,128)(2,1)S(1)}, bf16[16,256]{1,0:T(8,128)(2,1)S(1)}, u32[]{:S(2)}, u32[]{:S(2)}) collective-permute-start(bf16[16,256]{1,0:T(8,128)(2,1)S(1)} %get-tuple-element.159), channel_id=1, source_target_pairs={{0,3},{1,2},{2,1},{3,0},{4,7},{5,6},{6,5},{7,4},{8,11},{9,10},{10,... | collective-permute-start | bytes 24584 | tf_op jit(solution)/shard_map/ppermute | solution.py:542
  108.7 0.8 collective-permute-done.22.refs_0_
  109.5 1.8 %collective-permute-done.24.refs_2_ = bf16[16,256]{1,0:T(8,128)(2,1)S(1)} collective-permute-done((bf16[16,256]{1,0:T(8,128)(2,1)S(1)}, bf16[16,256]{1,0:T(8,128)(2,1)S(1)}, u32[]{:S(2)}, u32[]{:S(2)}) %collective-permute-start.24) | collective-permute-done | bytes 8224 | tf_op jit(solution)/shard_map/ppermute | solution.py:542
  111.3 3.4 %collective-permute-start.27 = (f32[16,256]{1,0:T(8,128)S(1)}, f32[16,256]{1,0:T(8,128)S(1)}, u32[]{:S(2)}, u32[]{:S(2)}) collective-permute-start(f32[16,256]{1,0:T(8,128)S(1)} %shard_map.100.rest_0_), channel_id=1, source_target_pairs={{0,192},{64,128},{128,64},{192,0},{1,193},{65,129},{129,65},{193,1... | collective-permute-start | bytes 49160 | tf_op jit(solution)/shard_map/ppermute | solution.py:542
  114.6 1.0 collective-permute-start.26
  115.6 1.5 %shard_map.97 = (bf16[128,1024]{1,0:T(8,128)(2,1)}, bf16[128,1024]{1,0:T(8,128)(2,1)}) custom-call(s32[1]{0:T(128)S(6)} %mul.3.flip_ref, s32[1]{0:T(128)} %bitcast.me_ref.first_ref.block_ref, bf16[8,128,128]{2,1,0:T(8,128)(2,1)S(1)} %collective-permute-done.20.later_hbm, bf16[8,384,128]{2,1,0:T(8,128)(2,1)S(1)} %all-to-all-done.1.row_hbm, ...), custom_call_target="tpu_custom_call" | custom-call | bytes 2097160 | tf_op jit(solution)/shard_map/pallas_call | solution.py:36
  117.2 0.7 shard_map.101
  (30 shorter events, 0.3 us)
Async XLA Ops:
  0.6 36.4 %copy-start = (bf16[1,128,1024]{2,1,0:T(8,128)(2,1)S(1)}, bf16[1,128,1024]{2,1,0:T(8,128)(2,1)}, u32[]{:S(2)}) copy-start(bf16[1,128,1024]{2,1,0:T(8,128)(2,1)} %param.8) | copy-start | bytes 786436
  4.4 29.1 %all-to-all-start = ((bf16[8,256,128]{2,1,0:T(8,128)(2,1)}), bf16[8,256,128]{2,1,0:T(8,128)(2,1)S(1)}, u32[]{:S(2)}, u32[]{:S(2)}) async-start(bf16[8,256,128]{2,1,0:T(8,128)(2,1)} %get-tuple-element.83), calls=%async_computation | async-start | bytes 1048576 | tf_op jit(solution)/shard_map/all_to_all | solution.py:373
  14.4 11.1 %collective-permute-start = (bf16[32,1024]{1,0:T(8,128)(2,1)}, bf16[32,1024]{1,0:T(8,128)(2,1)S(1)}, u32[]{:S(2)}, u32[]{:S(2)}) collective-permute-start(bf16[32,1024]{1,0:T(8,128)(2,1)} %get-tuple-element.84), channel_id=1, source_target_pairs={{0,40},{8,32},{16,56},{24,48},{32,8},{40,0},{48,24},{56,16},{1,41}... | collective-permute-start | bytes 196616 | tf_op jit(solution)/shard_map/ppermute | solution.py:421
  19.5 6.3 %collective-permute-start.1 = (bf16[32,1024]{1,0:T(8,128)(2,1)}, bf16[32,1024]{1,0:T(8,128)(2,1)S(1)}, u32[]{:S(2)}, u32[]{:S(2)}) collective-permute-start(bf16[32,1024]{1,0:T(8,128)(2,1)} %get-tuple-element.85), channel_id=1, source_target_pairs={{0,32},{8,40},{16,48},{24,56},{32,0},{40,8},{48,16},{56,24},{1,33}... | collective-permute-start | bytes 196616 | tf_op jit(solution)/shard_map/ppermute | solution.py:421
  19.7 6.7 %collective-permute-start.2 = (bf16[32,1024]{1,0:T(8,128)(2,1)}, bf16[32,1024]{1,0:T(8,128)(2,1)S(1)}, u32[]{:S(2)}, u32[]{:S(2)}) collective-permute-start(bf16[32,1024]{1,0:T(8,128)(2,1)} %get-tuple-element.86), channel_id=1, source_target_pairs={{0,24},{8,16},{16,8},{24,0},{32,56},{40,48},{48,40},{56,32},{1,25}... | collective-permute-start | bytes 196616 | tf_op jit(solution)/shard_map/ppermute | solution.py:421
  21.0 7.6 %collective-permute-start.3 = (bf16[32,1024]{1,0:T(8,128)(2,1)}, bf16[32,1024]{1,0:T(8,128)(2,1)S(1)}, u32[]{:S(2)}, u32[]{:S(2)}) collective-permute-start(bf16[32,1024]{1,0:T(8,128)(2,1)} %get-tuple-element.87), channel_id=1, source_target_pairs={{0,56},{8,48},{16,40},{24,32},{32,24},{40,16},{48,8},{56,0},{1,57}... | collective-permute-start | bytes 196616 | tf_op jit(solution)/shard_map/ppermute | solution.py:421
  25.2 8.3 %collective-permute-start.4 = (bf16[32,1024]{1,0:T(8,128)(2,1)}, bf16[32,1024]{1,0:T(8,128)(2,1)S(1)}, u32[]{:S(2)}, u32[]{:S(2)}) collective-permute-start(bf16[32,1024]{1,0:T(8,128)(2,1)} %get-tuple-element.88), channel_id=1, source_target_pairs={{0,8},{8,0},{16,24},{24,16},{32,40},{40,32},{48,56},{56,48},{1,9},... | collective-permute-start | bytes 196616 | tf_op jit(solution)/shard_map/ppermute | solution.py:421
  25.5 8.0 %collective-permute-start.5 = (bf16[32,1024]{1,0:T(8,128)(2,1)}, bf16[32,1024]{1,0:T(8,128)(2,1)S(1)}, u32[]{:S(2)}, u32[]{:S(2)}) collective-permute-start(bf16[32,1024]{1,0:T(8,128)(2,1)} %get-tuple-element.89), channel_id=1, source_target_pairs={{0,16},{8,24},{16,0},{24,8},{32,48},{40,56},{48,32},{56,40},{1,17}... | collective-permute-start | bytes 196616 | tf_op jit(solution)/shard_map/ppermute | solution.py:421
  25.8 7.7 %collective-permute-start.6 = (bf16[32,1024]{1,0:T(8,128)(2,1)}, bf16[32,1024]{1,0:T(8,128)(2,1)S(1)}, u32[]{:S(2)}, u32[]{:S(2)}) collective-permute-start(bf16[32,1024]{1,0:T(8,128)(2,1)} %get-tuple-element.90), channel_id=1, source_target_pairs={{0,48},{8,56},{16,32},{24,40},{32,16},{40,24},{48,0},{56,8},{1,49}... | collective-permute-start | bytes 196616 | tf_op jit(solution)/shard_map/ppermute | solution.py:421
  33.5 9.6 %collective-permute-start.7 = (bf16[8,128,128]{2,1,0:T(8,128)(2,1)S(1)}, bf16[8,128,128]{2,1,0:T(8,128)(2,1)S(1)}, u32[]{:S(2)}, u32[]{:S(2)}) collective-permute-start(bf16[8,128,128]{2,1,0:T(8,128)(2,1)S(1)} %slice.6), channel_id=1, source_target_pairs={{0,12},{4,8},{8,20},{12,16},{16,28},{20,24},{24,36},{28,32},{32,44... | collective-permute-start | bytes 786440 | tf_op jit(solution)/shard_map/ppermute | solution.py:426
  37.0 12.8 %collective-permute-start.9 = (bf16[128,1024]{1,0:T(8,128)(2,1)S(1)}, bf16[128,1024]{1,0:T(8,128)(2,1)S(1)}, u32[]{:S(2)}, u32[]{:S(2)}) collective-permute-start(bf16[128,1024]{1,0:T(8,128)(2,1)S(1)} %bitcast.12), channel_id=1, source_target_pairs={{0,128},{64,192},{128,0},{192,64},{1,129},{65,193},{129,1},{193,65... | collective-permute-start | bytes 786440 | tf_op jit(solution)/shard_map/ppermute | solution.py:436
  37.1 12.7 %collective-permute-start.8 = (bf16[128,1024]{1,0:T(8,128)(2,1)S(1)}, bf16[128,1024]{1,0:T(8,128)(2,1)S(1)}, u32[]{:S(2)}, u32[]{:S(2)}) collective-permute-start(bf16[128,1024]{1,0:T(8,128)(2,1)S(1)} %bitcast.13), channel_id=1, source_target_pairs={{0,64},{64,0},{128,192},{192,128},{1,65},{65,1},{129,193},{193,129... | collective-permute-start | bytes 786440 | tf_op jit(solution)/shard_map/ppermute | solution.py:436
  40.7 0.8 copy-start.1
  49.9 26.5 %all-to-all-start.1 = ((bf16[8,384,128]{2,1,0:T(8,128)(2,1)}), bf16[8,384,128]{2,1,0:T(8,128)(2,1)S(1)}, u32[]{:S(2)}, u32[]{:S(2)}) async-start(bf16[8,384,128]{2,1,0:T(8,128)(2,1)} %shard_map.94), calls=%async_computation.1 | async-start | bytes 1572864 | tf_op jit(solution)/shard_map/all_to_all | solution.py:373
  56.2 10.9 %collective-permute-start.10 = (bf16[32,1024]{1,0:T(8,128)(2,1)S(1)}, bf16[32,1024]{1,0:T(8,128)(2,1)S(1)}, u32[]{:S(2)}, u32[]{:S(2)}) collective-permute-start(bf16[32,1024]{1,0:T(8,128)(2,1)S(1)} %get-tuple-element.120), channel_id=1, source_target_pairs={{0,40},{8,32},{16,56},{24,48},{32,8},{40,0},{48,24},{56,16},{1,41}... | collective-permute-start | bytes 196616 | tf_op jit(solution)/shard_map/ppermute | solution.py:421
  58.4 8.7 %collective-permute-start.11 = (bf16[32,1024]{1,0:T(8,128)(2,1)S(1)}, bf16[32,1024]{1,0:T(8,128)(2,1)S(1)}, u32[]{:S(2)}, u32[]{:S(2)}) collective-permute-start(bf16[32,1024]{1,0:T(8,128)(2,1)S(1)} %get-tuple-element.121), channel_id=1, source_target_pairs={{0,32},{8,40},{16,48},{24,56},{32,0},{40,8},{48,16},{56,24},{1,33}... | collective-permute-start | bytes 196616 | tf_op jit(solution)/shard_map/ppermute | solution.py:421
  59.5 8.3 %collective-permute-start.12 = (bf16[32,1024]{1,0:T(8,128)(2,1)S(1)}, bf16[32,1024]{1,0:T(8,128)(2,1)S(1)}, u32[]{:S(2)}, u32[]{:S(2)}) collective-permute-start(bf16[32,1024]{1,0:T(8,128)(2,1)S(1)} %get-tuple-element.122), channel_id=1, source_target_pairs={{0,24},{8,16},{16,8},{24,0},{32,56},{40,48},{48,40},{56,32},{1,25}... | collective-permute-start | bytes 196616 | tf_op jit(solution)/shard_map/ppermute | solution.py:421
  61.5 7.8 %collective-permute-start.13 = (bf16[32,1024]{1,0:T(8,128)(2,1)S(1)}, bf16[32,1024]{1,0:T(8,128)(2,1)S(1)}, u32[]{:S(2)}, u32[]{:S(2)}) collective-permute-start(bf16[32,1024]{1,0:T(8,128)(2,1)S(1)} %get-tuple-element.123), channel_id=1, source_target_pairs={{0,56},{8,48},{16,40},{24,32},{32,24},{40,16},{48,8},{56,0},{1,57}... | collective-permute-start | bytes 196616 | tf_op jit(solution)/shard_map/ppermute | solution.py:421
  64.1 5.7 %collective-permute-start.14 = (bf16[32,1024]{1,0:T(8,128)(2,1)S(1)}, bf16[32,1024]{1,0:T(8,128)(2,1)S(1)}, u32[]{:S(2)}, u32[]{:S(2)}) collective-permute-start(bf16[32,1024]{1,0:T(8,128)(2,1)S(1)} %get-tuple-element.124), channel_id=1, source_target_pairs={{0,8},{8,0},{16,24},{24,16},{32,40},{40,32},{48,56},{56,48},{1,9},... | collective-permute-start | bytes 196616 | tf_op jit(solution)/shard_map/ppermute | solution.py:421
  67.1 3.4 %collective-permute-start.15 = (bf16[32,1024]{1,0:T(8,128)(2,1)S(1)}, bf16[32,1024]{1,0:T(8,128)(2,1)S(1)}, u32[]{:S(2)}, u32[]{:S(2)}) collective-permute-start(bf16[32,1024]{1,0:T(8,128)(2,1)S(1)} %get-tuple-element.125), channel_id=1, source_target_pairs={{0,16},{8,24},{16,0},{24,8},{32,48},{40,56},{48,32},{56,40},{1,17}... | collective-permute-start | bytes 196616 | tf_op jit(solution)/shard_map/ppermute | solution.py:421
  67.1 5.1 %collective-permute-start.16 = (bf16[32,1024]{1,0:T(8,128)(2,1)S(1)}, bf16[32,1024]{1,0:T(8,128)(2,1)S(1)}, u32[]{:S(2)}, u32[]{:S(2)}) collective-permute-start(bf16[32,1024]{1,0:T(8,128)(2,1)S(1)} %get-tuple-element.126), channel_id=1, source_target_pairs={{0,48},{8,56},{16,32},{24,40},{32,16},{40,24},{48,0},{56,8},{1,49}... | collective-permute-start | bytes 196616 | tf_op jit(solution)/shard_map/ppermute | solution.py:421
  77.2 9.8 %collective-permute-start.21 = (bf16[128,1024]{1,0:T(8,128)(2,1)S(1)}, bf16[128,1024]{1,0:T(8,128)(2,1)S(1)}, u32[]{:S(2)}, u32[]{:S(2)}) collective-permute-start(bf16[128,1024]{1,0:T(8,128)(2,1)S(1)} %collective-permute-done.9.refs_4_), channel_id=1, source_target_pairs={{0,64},{64,0},{128,192},{192,128},{1,65},{65,1},{129,193},{193,129... | collective-permute-start | bytes 786440 | tf_op jit(solution)/shard_map/ppermute | solution.py:491
  79.4 6.4 %collective-permute-start.17 = (bf16[256,128]{1,0:T(8,128)(2,1)S(1)}, bf16[256,128]{1,0:T(8,128)(2,1)S(1)}, u32[]{:S(2)}, u32[]{:S(2)}) collective-permute-start(bf16[256,128]{1,0:T(8,128)(2,1)S(1)} %get-tuple-element.143), channel_id=1, source_target_pairs={{0,64},{64,0},{128,192},{192,128},{1,65},{65,1},{129,193},{193,129... | collective-permute-start | bytes 196616 | tf_op jit(solution)/shard_map/ppermute | solution.py:494
  79.7 6.1 %collective-permute-start.18 = (bf16[256,128]{1,0:T(8,128)(2,1)S(1)}, bf16[256,128]{1,0:T(8,128)(2,1)S(1)}, u32[]{:S(2)}, u32[]{:S(2)}) collective-permute-start(bf16[256,128]{1,0:T(8,128)(2,1)S(1)} %get-tuple-element.144), channel_id=1, source_target_pairs={{0,128},{64,192},{128,0},{192,64},{1,129},{65,193},{129,1},{193,65... | collective-permute-start | bytes 196616 | tf_op jit(solution)/shard_map/ppermute | solution.py:494
  82.8 4.2 %collective-permute-start.19 = (bf16[256,128]{1,0:T(8,128)(2,1)S(1)}, bf16[256,128]{1,0:T(8,128)(2,1)S(1)}, u32[]{:S(2)}, u32[]{:S(2)}) collective-permute-start(bf16[256,128]{1,0:T(8,128)(2,1)S(1)} %get-tuple-element.145), channel_id=1, source_target_pairs={{0,192},{64,128},{128,64},{192,0},{1,193},{65,129},{129,65},{193,1... | collective-permute-start | bytes 196616 | tf_op jit(solution)/shard_map/ppermute | solution.py:494
  88.5 14.4 %all-to-all-start.2 = ((bf16[16,16,1024]{2,1,0:T(8,128)(2,1)}), bf16[16,16,1024]{2,1,0:T(8,128)(2,1)S(1)}, u32[]{:S(2)}, u32[]{:S(2)}) async-start(bf16[16,16,1024]{2,1,0:T(8,128)(2,1)} %shard_map.98), calls=%async_computation.2 | async-start | bytes 1048576 | tf_op jit(solution)/shard_map/all_to_all | solution.py:373
  92.1 23.6 %collective-permute-start.20 = (bf16[8,128,128]{2,1,0:T(8,128)(2,1)S(1)}, bf16[8,128,128]{2,1,0:T(8,128)(2,1)S(1)}, u32[]{:S(2)}, u32[]{:S(2)}) collective-permute-start(bf16[8,128,128]{2,1,0:T(8,128)(2,1)S(1)} %slice.7), channel_id=1, source_target_pairs={{8,0},{16,8},{24,16},{32,24},{40,32},{48,40},{56,48},{9,1},{17,9},... | collective-permute-start | bytes 786440 | tf_op jit(solution)/shard_map/ppermute | solution.py:497
  103.0 6.5 %collective-permute-start.22 = (bf16[16,256]{1,0:T(8,128)(2,1)S(1)}, bf16[16,256]{1,0:T(8,128)(2,1)S(1)}, u32[]{:S(2)}, u32[]{:S(2)}) collective-permute-start(bf16[16,256]{1,0:T(8,128)(2,1)S(1)} %get-tuple-element.157), channel_id=1, source_target_pairs={{0,2},{1,3},{2,0},{3,1},{4,6},{5,7},{6,4},{7,5},{8,10},{9,11},{10,... | collective-permute-start | bytes 24584 | tf_op jit(solution)/shard_map/ppermute | solution.py:542
  105.6 3.8 %collective-permute-start.23 = (bf16[16,256]{1,0:T(8,128)(2,1)S(1)}, bf16[16,256]{1,0:T(8,128)(2,1)S(1)}, u32[]{:S(2)}, u32[]{:S(2)}) collective-permute-start(bf16[16,256]{1,0:T(8,128)(2,1)S(1)} %get-tuple-element.158), channel_id=1, source_target_pairs={{0,1},{1,0},{2,3},{3,2},{4,5},{5,4},{6,7},{7,6},{8,9},{9,8},{10,11... | collective-permute-start | bytes 24584 | tf_op jit(solution)/shard_map/ppermute | solution.py:542
  106.3 4.9 %collective-permute-start.24 = (bf16[16,256]{1,0:T(8,128)(2,1)S(1)}, bf16[16,256]{1,0:T(8,128)(2,1)S(1)}, u32[]{:S(2)}, u32[]{:S(2)}) collective-permute-start(bf16[16,256]{1,0:T(8,128)(2,1)S(1)} %get-tuple-element.159), channel_id=1, source_target_pairs={{0,3},{1,2},{2,1},{3,0},{4,7},{5,6},{6,5},{7,4},{8,11},{9,10},{10,... | collective-permute-start | bytes 24584 | tf_op jit(solution)/shard_map/ppermute | solution.py:542
  111.3 5.9 %collective-permute-start.27 = (f32[16,256]{1,0:T(8,128)S(1)}, f32[16,256]{1,0:T(8,128)S(1)}, u32[]{:S(2)}, u32[]{:S(2)}) collective-permute-start(f32[16,256]{1,0:T(8,128)S(1)} %shard_map.100.rest_0_), channel_id=1, source_target_pairs={{0,192},{64,128},{128,64},{192,0},{1,193},{65,129},{129,65},{193,1... | collective-permute-start | bytes 49160 | tf_op jit(solution)/shard_map/ppermute | solution.py:542
  114.6 2.6 %collective-permute-start.26 = (f32[16,256]{1,0:T(8,128)S(1)}, f32[16,256]{1,0:T(8,128)S(1)}, u32[]{:S(2)}, u32[]{:S(2)}) collective-permute-start(f32[16,256]{1,0:T(8,128)S(1)} %shard_map.100.rest_0_), channel_id=1, source_target_pairs={{0,128},{64,192},{128,0},{192,64},{1,129},{65,193},{129,1},{193,65... | collective-permute-start | bytes 49160 | tf_op jit(solution)/shard_map/ppermute | solution.py:542
  115.6 1.6 %collective-permute-start.25 = (f32[16,256]{1,0:T(8,128)S(1)}, f32[16,256]{1,0:T(8,128)S(1)}, u32[]{:S(2)}, u32[]{:S(2)}) collective-permute-start(f32[16,256]{1,0:T(8,128)S(1)} %shard_map.100.rest_0_), channel_id=1, source_target_pairs={{0,64},{64,0},{128,192},{192,128},{1,65},{65,1},{129,193},{193,129... | collective-permute-start | bytes 49160 | tf_op jit(solution)/shard_map/ppermute | solution.py:542
